TPU v7x, 256 devices: a whole 4x4x8 slice. The times are simulated.
256 devices in a mesh: layer: 4 (over y_lo, core), dp: 64 (over x, z, y_hi).
Axes of the slice: x: 4, y: 4 (y_hi: 2, y_lo: 2; y = y_hi * 2 + y_lo), z: 8, core: 2. Of those that a mesh axis runs over, the one named last changes fastest.
Arguments:
- gradients: bfloat16 [32768, 8, 4096], P('dp', 'layer'), may hold values from -6 to 6
- whitener: bfloat16 [8, 16, 256, 256], P('layer')
- owners: int32 [2], replicated, may hold values from 0 to 63
- query_ids: int32 [2, 64], replicated, may hold values from 0 to 511
Outputs:
- scores: float32 [128, 32768], P('layer', 'dp')
All inputs are finite; a program needn't handle non-finite values.
Results may differ from a plain program's by a relative error of at most 0.0029.
Values may be sent and summed in bfloat16 or wider, within the bound.
No kernel may reach another device: no remote copies, remote signals or barrier semaphores. Data moves between devices by JAX's collectives and lax.ppermute only.
A program may use at most 128 MiB of HBM per device.

v0:
```python
import functools
import itertools

import jax
import jax.numpy as jnp
from jax import lax
from jax.experimental import pallas as pl
from jax.experimental.pallas import tpu as pltpu
from jax.sharding import Mesh
from jax.sharding import PartitionSpec as P

NX, NZ, NY = 4, 8, 2
DP = ("x", "z", "yhi")
LAYER = ("ylo", "core")
AXES = LAYER + DP
SIZES = dict(x=NX, z=NZ, yhi=NY)


def shift(value, dx=0, dz=0, dy=0):
    moves = {name: by for name, by in (("x", dx), ("z", dz), ("yhi", dy)) if by}
    names = tuple(moves)

    def index(place):
        flat = 0
        for name, at in zip(names, place):
            flat = flat * SIZES[name] + at % SIZES[name]
        return flat

    pairs = [
        (index(place), index([at + moves[name] for name, at in zip(names, place)]))
        for place in itertools.product(*(range(SIZES[name]) for name in names))
    ]
    return lax.ppermute(value, names if len(names) > 1 else names[0], pairs)


def pick_kernel(counts, ids, gradients, *rest):
    outs, sem = rest[:-1], rest[-1]
    total = 0
    for out, count in zip(outs, counts):
        base = total

        def start(row, carry, out=out, base=base):
            pltpu.make_async_copy(
                gradients.at[ids[base + row]], out.at[row], sem
            ).start()
            return carry

        lax.fori_loop(0, count, start, 0, unroll=8)
        total += count
    for out, count in zip(outs, counts):
        pltpu.make_async_copy(gradients.at[pl.ds(0, count)], out, sem).wait()


def pick_rows(gradients, ids, counts):
    row = gradients.shape[1:]
    moved = 2 * sum(counts) * row[0] * row[1] * gradients.dtype.itemsize
    return pl.pallas_call(
        functools.partial(pick_kernel, counts),
        out_shape=[jax.ShapeDtypeStruct((n,) + row, gradients.dtype) for n in counts],
        in_specs=[
            pl.BlockSpec(memory_space=pltpu.SMEM),
            pl.BlockSpec(memory_space=pl.ANY),
        ],
        out_specs=[pl.BlockSpec(memory_space=pltpu.VMEM) for _ in counts],
        scratch_shapes=[pltpu.SemaphoreType.DMA],
        cost_estimate=pl.CostEstimate(flops=0, bytes_accessed=moved, transcendentals=0),
    )(ids, gradients)


def per_round(flag):
    return flag.reshape(-1, 1, 1, 1)


def piece(parts, at):
    return lax.dynamic_index_in_dim(parts, at, 1, keepdims=False)


def broadcast(gradients, owners, query_ids, beside):
    rounds, queries = query_ids.shape
    tail = gradients.shape[1:]
    quarter, part = queries // 4, queries // 16
    x, z, y = (lax.axis_index(name) for name in DP)
    colour = (x + 2 * z) % 4
    own_x, own_z, own_y = owners // (NZ * NY), owners // NY % NZ, owners % NY
    far_x, far_z, same_y = (x - own_x) % NX, (z - own_z) % NZ, y == own_y

    by_colour = query_ids.reshape(rounds, 4, quarter)
    order = [by_colour[:, (colour + turn) % 4].reshape(-1) for turn in (0, 1, 3)]
    across = by_colour[:, (colour + 2) % 4]
    order += [across[:, : quarter // 2].reshape(-1), across[:, quarter // 2 :].reshape(-1)]
    counts = tuple(ids.shape[0] for ids in order)
    own, to_right, to_left, to_up, to_down = pick_rows(
        gradients, jnp.concatenate(order), counts
    )
    from_left = shift(to_right, dx=1)
    from_right = shift(to_left, dx=-1)
    from_below = shift(to_up, dz=1)
    from_above = shift(to_down, dz=-1)
    from_left, from_right, from_below, from_above = beside(
        (from_left, from_right, from_below, from_above), to_right
    )
    own, from_left, from_right = (
        rows.reshape(rounds, 4, part, *tail) for rows in (own, from_left, from_right)
    )
    from_below, from_above = (rows.reshape(rounds, 2, part, *tail) for rows in (from_below, from_above))

    def held(at):
        low = at < 2
        out = piece(own, at)
        out = jnp.where(per_round((far_x == 0) & (far_z == 1) & low), piece(from_below, at % 2), out)
        out = jnp.where(per_round((far_x == 0) & (far_z == 7) & ~low), piece(from_above, at % 2), out)
        out = jnp.where(per_round((far_x == 1) & (far_z == 0)), piece(from_left, at), out)
        return jnp.where(per_round((far_x == 3) & (far_z == 0)), piece(from_right, at), out)

    mine = z % 4
    steps = (1, 2, -1)
    pieces = [held((z + by) % 4) for by in steps]
    got = [shift(rows, dx=(-2 * by) % 4, dz=by) for by, rows in zip(steps, pieces)]
    got = dict(zip((0,) + steps, (held(mine),) + tuple(beside(tuple(got), pieces[0]))))
    own_colour = (own_x + 2 * own_z) % 4
    source_z = own_z + jnp.where((colour - own_colour) % 4 == 2, jnp.where(mine < 2, 1, -1), 0)
    away = (z - source_z) % NZ
    part_rows = got[0]
    for by in (1, 2, -1):
        part_rows = jnp.where(per_round(away == by % NZ), got[by], part_rows)

    near = (away <= 2) | (away == 7)
    (moved,) = beside((shift(part_rows, dz=4),), part_rows)
    part_rows = jnp.where(per_round(near), part_rows, moved)
    part_rows = jnp.where(per_round(same_y), part_rows, shift(part_rows, dy=1))

    whole = [(mine, part_rows)]
    for by in steps:
        whole.append(((z - by) % 4, shift(part_rows, dx=(-2 * by) % 4, dz=by)))
    mine_rows = jnp.zeros((rounds, 4, part) + tail, gradients.dtype)
    for at, rows in whole:
        mine_rows = lax.dynamic_update_index_in_dim(mine_rows, rows, at, 1)
    mine_rows = mine_rows.reshape(rounds, quarter, *tail)

    half = quarter // 2
    before, after = shift(mine_rows, dx=1), shift(mine_rows, dx=-1)
    low, high = shift(mine_rows[:, :half], dz=1), shift(mine_rows[:, half:], dz=-1)
    after, low, high, before = beside((after, low, high, before), mine_rows)
    return mine_rows, after, low, high, before


NT = (((1,), (1,)), ((), ()))
VMEM_LIMIT = 48 * 2**20


def whiten_kernel(x_ref, w_ref, *refs):
    white_ref, norm_ref = refs[-2:]
    layers, nb, block = w_ref.shape[:3]
    total = jnp.zeros(norm_ref.shape, jnp.float32)
    for layer in range(layers):
        x = x_ref[:, layer, :]
        for b in range(nb):
            y = lax.dot_general(
                w_ref[layer, b], x[:, b * block : (b + 1) * block], NT, preferred_element_type=jnp.float32
            )
            white_ref[layer, b] = y.astype(white_ref.dtype)
            total = total + jnp.sum((y * y).reshape(-1, *total.shape), axis=0)

    @pl.when(pl.program_id(0) == 0)
    def _():
        norm_ref[...] = jnp.zeros_like(norm_ref)

    norm_ref[...] += total


def whiten_blocks(gradients, whitener, white, first, count, nb=2):
    examples, layers, proj = gradients.shape
    nblock, block = whitener.shape[1:3]
    base = first // nb
    cost = pl.CostEstimate(
        flops=2 * layers * count * block * block * examples,
        bytes_accessed=layers * count * block * (4 * examples + 2 * block) * 3,
        transcendentals=0,
    )
    operands, aliases, extra = [gradients, whitener], {}, []
    if white is not None:
        operands.append(white)
        aliases, extra = {2: 0}, [pl.BlockSpec(memory_space=pl.ANY)]
    return pl.pallas_call(
        whiten_kernel,
        grid=(count // nb,),
        out_shape=[
            jax.ShapeDtypeStruct((layers, nblock, block, examples), jnp.bfloat16),
            jax.ShapeDtypeStruct((8, examples), jnp.float32),
        ],
        in_specs=[
            pl.BlockSpec((examples, layers, nb * block), lambda i: (0, 0, base + i)),
            pl.BlockSpec((layers, nb, block, block), lambda i: (0, base + i, 0, 0)),
        ]
        + extra,
        out_specs=[
            pl.BlockSpec((layers, nb, block, examples), lambda i: (0, base + i, 0, 0)),
            pl.BlockSpec((8, examples), lambda i: (0, 0)),
        ],
        input_output_aliases=aliases,
        compiler_params=pltpu.CompilerParams(vmem_limit_bytes=VMEM_LIMIT),
        cost_estimate=cost,
    )(*operands)


def score_kernel(place, *refs):
    *groups, w_ref, white_ref, keep_ref, send_ref, total_ref = refs
    layers, nb, block = w_ref.shape[:3]
    step = pl.program_id(0)

    @pl.when(step == 0)
    def _():
        total_ref[...] = jnp.zeros_like(total_ref)

    rows = jnp.concatenate([g[...].reshape(-1, *g.shape[2:]) for g in groups], axis=0)
    total = jnp.zeros(total_ref.shape, jnp.float32)
    for layer in range(layers):
        x = rows[:, layer, :]
        for b in range(nb):
            query = lax.dot_general(
                x[:, b * block : (b + 1) * block], w_ref[layer, b], NT, preferred_element_type=jnp.float32
            )
            total = total + jnp.dot(
                query.astype(white_ref.dtype), white_ref[layer, b], preferred_element_type=jnp.float32
            )
    total_ref[...] += total

    @pl.when(step == pl.num_programs(0) - 1)
    def _():
        colour, core = place[0], place[1]
        rounds, _, quarter, _ = keep_ref.shape
        half = quarter // 2
        for turn in range(4):
            at = lax.rem(colour + turn, 4)
            for which in range(rounds):
                if turn == 2:
                    low = 2 * 2 * quarter + which * half
                    high = low + rounds * half
                    spans = ((0, low, half), (half, high, half))
                else:
                    spans = ((0, turn * rounds * quarter + which * quarter, quarter),)
                for to, start, length in spans:
                    value = total_ref[start : start + length]
                    for ref, kept in ((keep_ref, True), (send_ref, False)):

                        @pl.when((at // 2 == core) == kept)
                        def _(ref=ref, value=value, to=to, length=length, which=which, at=at):
                            ref[which, at % 2, to : to + length] = value


def score(groups, whitener, white, place, nb=4):
    layers, nblock, block, examples = white.shape
    rounds, quarter = groups[0].shape[:2]
    count = 4 * rounds * quarter
    out = jax.ShapeDtypeStruct((rounds, 2, quarter, examples), jnp.float32)
    out_spec = pl.BlockSpec(out.shape, lambda i: (0, 0, 0, 0))
    cost = pl.CostEstimate(
        flops=2 * layers * nblock * block * count * (block + examples),
        bytes_accessed=2 * layers * nblock * block * (examples + block + count),
        transcendentals=0,
    )
    return pl.pallas_call(
        score_kernel,
        grid=(nblock // nb,),
        out_shape=[out, out],
        in_specs=[pl.BlockSpec(memory_space=pltpu.SMEM)]
        + [pl.BlockSpec(g.shape[:3] + (nb * block,), lambda i: (0, 0, 0, i)) for g in groups]
        + [
            pl.BlockSpec((layers, nb, block, block), lambda i: (0, i, 0, 0)),
            pl.BlockSpec((layers, nb, block, examples), lambda i: (0, i, 0, 0)),
        ],
        out_specs=[out_spec, out_spec],
        scratch_shapes=[pltpu.VMEM((count, examples), jnp.float32)],
        compiler_params=pltpu.CompilerParams(vmem_limit_bytes=VMEM_LIMIT),
        cost_estimate=cost,
    )(place, *groups, whitener, white)


def swap(value, axis):
    return lax.ppermute(value, axis, [(0, 1), (1, 0)])


SHARES = 4


def local(gradients, whitener, owners, query_ids):
    count = gradients.shape[0]
    share = whitener.shape[1] // SHARES
    colour = (lax.axis_index("x") + 2 * lax.axis_index("z")) % 4
    core, ylo = lax.axis_index("core"), lax.axis_index("ylo")
    done = dict(white=None, norms=[])

    def beside(values, sent):
        rows, _ = lax.optimization_barrier((gradients, sent))
        first = len(done["norms"]) * share
        done["white"], norms = whiten_blocks(rows, whitener, done["white"], first, share)
        values, norms = lax.optimization_barrier((values, norms))
        done["norms"].append(norms)
        return values

    groups = broadcast(gradients, owners, query_ids, beside)
    norms = jnp.sum(sum(done["norms"]), axis=0)
    norms = norms + swap(norms, "core")
    norms = norms + swap(norms, "ylo")

    keep, send = score(groups, whitener, done["white"], jnp.stack([colour, core]).astype(jnp.int32))
    half = keep + swap(send, "core")
    mine = lax.dynamic_index_in_dim(half, ylo, 0, keepdims=False)
    mine = mine + swap(lax.dynamic_index_in_dim(half, 1 - ylo, 0, keepdims=False), "ylo")
    return mine.reshape(-1, count) / jnp.sqrt(norms + 1e-06)[None, :]


def solution(mesh):
    torus = Mesh(mesh.devices.reshape(2, 2, NX, NZ, NY), AXES)
    in_specs = (P(DP, LAYER, None), P(LAYER, None, None, None), P(), P())
    return jax.shard_map(
        local, mesh=torus, in_specs=in_specs, out_specs=P(LAYER, DP), check_vma=False
    )
```

profile of v0, /device:TPU:1, one launch (start us, length us, event | category | flops | bytes accessed | tf_op | source)
XLA Modules:
  0.0 107.1 jit_solution(2208381079105929163)
XLA Ops:
  1.9 3.6 %shard_map.46 = (bf16[32,2,4096]{2,1,0:T(2,128)(2,1)}, bf16[32,2,4096]{2,1,0:T(2,128)(2,1)}, bf16[32,2,4096]{2,1,0:T(2,128)(2,1)}, bf16[16,2,4096]{2,1,0:T(2,128)(2,1)}, bf16[16,2,4096]{2,1,0:T(2,128)(2,1)}) custom-call(s32[128]{0:T(128)} %concatenate.3.ids, bf16[512,2,4096]{2,1,0:T(2,128)(2,1)} %x_ref.3), custom_call_target="tpu_custom_call" | custom-call | bytes 4194304 | tf_op jit(solution)/shard_map/pallas_call | solution.py:57
  5.5 2.1 %collective-permute-start = (bf16[32,2,4096]{2,1,0:T(2,128)(2,1)}, bf16[32,2,4096]{2,1,0:T(2,128)(2,1)S(1)}, u32[]{:S(2)}, u32[]{:S(2)}) collective-permute-start(bf16[32,2,4096]{2,1,0:T(2,128)(2,1)} %get-tuple-element.40), channel_id=1, source_target_pairs={{0,16},{16,32},{32,48},{48,0},{1,17},{17,33},{33,49},{49,1},{2,18}... | collective-permute-start | bytes 1572872 | tf_op jit(solution)/shard_map/ppermute | solution.py:33
  9.0 1.8 %collective-permute-start.2 = (bf16[16,2,4096]{2,1,0:T(2,128)(2,1)}, bf16[16,2,4096]{2,1,0:T(2,128)(2,1)S(1)}, u32[]{:S(2)}, u32[]{:S(2)}) collective-permute-start(bf16[16,2,4096]{2,1,0:T(2,128)(2,1)} %get-tuple-element.42), channel_id=1, source_target_pairs={{0,2},{2,4},{4,6},{6,8},{8,10},{10,12},{12,14},{14,0},{1,3},{3,5},... | collective-permute-start | bytes 786440 | tf_op jit(solution)/shard_map/ppermute | solution.py:33
  10.7 3.9 %collective-permute-start.3 = (bf16[16,2,4096]{2,1,0:T(2,128)(2,1)}, bf16[16,2,4096]{2,1,0:T(2,128)(2,1)S(1)}, u32[]{:S(2)}, u32[]{:S(2)}) collective-permute-start(bf16[16,2,4096]{2,1,0:T(2,128)(2,1)} %get-tuple-element.43), channel_id=1, source_target_pairs={{0,14},{2,0},{4,2},{6,4},{8,6},{10,8},{12,10},{14,12},{1,15},{3,1}... | collective-permute-start | bytes 786440 | tf_op jit(solution)/shard_map/ppermute | solution.py:33
  14.9 2.2 %copy-done = bf16[2,16,256,256]{3,2,1,0:T(8,128)(2,1)S(1)} copy-done((bf16[2,16,256,256]{3,2,1,0:T(8,128)(2,1)S(1)}, bf16[2,16,256,256]{3,2,1,0:T(8,128)(2,1)}, u32[]{:S(2)}) %copy-start) | copy-done | bytes 4194328
  17.1 7.6 %shard_map.47 = (bf16[2,16,256,512]{3,2,1,0:T(8,128)(2,1)}, f32[8,512]{1,0:T(8,128)S(1)}) custom-call(bf16[512,2,4096]{2,1,0:T(2,128)(2,1)} %x_ref.3, bf16[2,16,256,256]{3,2,1,0:T(8,128)(2,1)S(1)} %copy-done), custom_call_target="tpu_custom_call" | custom-call | flops 536870912 | bytes 15728640 | tf_op jit(solution)/shard_map/pallas_call | solution.py:184
  25.7 3.1 %collective-permute-start.5 = (bf16[2,4,2,4096]{3,2,1,0:T(2,128)(2,1)S(1)}, bf16[2,4,2,4096]{3,2,1,0:T(2,128)(2,1)S(1)}, u32[]{:S(2)}, u32[]{:S(2)}) collective-permute-start(bf16[2,4,2,4096]{3,2,1,0:T(2,128)(2,1)S(1)} %get-tuple-element.91), channel_id=1, source_target_pairs={{0,4},{2,6},{4,8},{6,10},{8,12},{10,14},{12,0},{14,2},{1,5},{3,7},... | collective-permute-start | bytes 393224 | tf_op jit(solution)/shard_map/ppermute | solution.py:33
  28.9 1.9 %collective-permute-start.6 = (bf16[2,4,2,4096]{3,2,1,0:T(2,128)(2,1)S(1)}, bf16[2,4,2,4096]{3,2,1,0:T(2,128)(2,1)S(1)}, u32[]{:S(2)}, u32[]{:S(2)}) collective-permute-start(bf16[2,4,2,4096]{3,2,1,0:T(2,128)(2,1)S(1)} %get-tuple-element.90), channel_id=1, source_target_pairs={{0,46},{2,32},{4,34},{6,36},{8,38},{10,40},{12,42},{14,44},{16,62}... | collective-permute-start | bytes 393224 | tf_op jit(solution)/shard_map/ppermute | solution.py:33
  30.8 2.2 %copy-done.1 = bf16[2,16,256,256]{3,2,1,0:T(8,128)(2,1)S(1)} copy-done((bf16[2,16,256,256]{3,2,1,0:T(8,128)(2,1)S(1)}, bf16[2,16,256,256]{3,2,1,0:T(8,128)(2,1)}, u32[]{:S(2)}) %copy-start.1) | copy-done | bytes 4194328
  33.0 7.5 %shard_map.48 = (bf16[2,16,256,512]{3,2,1,0:T(8,128)(2,1)}, f32[8,512]{1,0:T(8,128)S(1)}) custom-call(bf16[512,2,4096]{2,1,0:T(2,128)(2,1)} %x_ref.3, bf16[2,16,256,256]{3,2,1,0:T(8,128)(2,1)S(1)} %copy-done.1, bf16[2,16,256,512]{3,2,1,0:T(8,128)(2,1)} %get-tuple-element.52.refs_0_), custom_call_target="tpu_custom_call", output_to_operand_aliasing={{0}: (2, {})} | custom-call | flops 536870912 | bytes 15728640 | tf_op jit(solution)/shard_map/pallas_call | solution.py:184
  41.1 4.1 %collective-permute-start.7 = (bf16[2,4,2,4096]{3,2,1,0:T(2,128)(2,1)S(1)}, bf16[2,4,2,4096]{3,2,1,0:T(2,128)(2,1)S(1)}, u32[]{:S(2)}, u32[]{:S(2)}) collective-permute-start(bf16[2,4,2,4096]{3,2,1,0:T(2,128)(2,1)S(1)} %broadcast_select_fusion.10), channel_id=1, source_target_pairs={{0,8},{2,10},{4,12},{6,14},{8,0},{10,2},{12,4},{14,6},{1,9},{3,11}... | collective-permute-start | bytes 393224 | tf_op jit(solution)/shard_map/ppermute | solution.py:33
  45.2 7.5 %shard_map.49 = (bf16[2,16,256,512]{3,2,1,0:T(8,128)(2,1)}, f32[8,512]{1,0:T(8,128)S(1)}) custom-call(bf16[512,2,4096]{2,1,0:T(2,128)(2,1)} %x_ref.3, bf16[2,16,256,256]{3,2,1,0:T(8,128)(2,1)S(1)} %copy-done.1, bf16[2,16,256,512]{3,2,1,0:T(8,128)(2,1)} %get-tuple-element.58.refs_0_), custom_call_target="tpu_custom_call", output_to_operand_aliasing={{0}: (2, {})} | custom-call | flops 536870912 | bytes 15728640 | tf_op jit(solution)/shard_map/pallas_call | solution.py:184
  53.0 3.0 %collective-permute-start.8 = (bf16[2,4,2,4096]{3,2,1,0:T(2,128)(2,1)S(1)}, bf16[2,4,2,4096]{3,2,1,0:T(2,128)(2,1)S(1)}, u32[]{:S(2)}, u32[]{:S(2)}) collective-permute-start(bf16[2,4,2,4096]{3,2,1,0:T(2,128)(2,1)S(1)} %broadcast_select_fusion.11), channel_id=1, source_target_pairs={{0,1},{1,0},{2,3},{3,2},{4,5},{5,4},{6,7},{7,6},{8,9},{9,8},{10,11... | collective-permute-start | bytes 393224 | tf_op jit(solution)/shard_map/ppermute | solution.py:33
  56.0 2.4 %collective-permute-done.8 = bf16[2,4,2,4096]{3,2,1,0:T(2,128)(2,1)S(1)} collective-permute-done((bf16[2,4,2,4096]{3,2,1,0:T(2,128)(2,1)S(1)}, bf16[2,4,2,4096]{3,2,1,0:T(2,128)(2,1)S(1)}, u32[]{:S(2)}, u32[]{:S(2)}) %collective-permute-start.8) | collective-permute-done | bytes 131104 | tf_op jit(solution)/shard_map/ppermute | solution.py:33
  59.2 1.4 %collective-permute-start.9 = (bf16[2,4,2,4096]{3,2,1,0:T(2,128)(2,1)S(1)}, bf16[2,4,2,4096]{3,2,1,0:T(2,128)(2,1)S(1)}, u32[]{:S(2)}, u32[]{:S(2)}) collective-permute-start(bf16[2,4,2,4096]{3,2,1,0:T(2,128)(2,1)S(1)} %get-tuple-element.79), channel_id=1, source_target_pairs={{0,34},{2,36},{4,38},{6,40},{8,42},{10,44},{12,46},{14,32},{16,50}... | collective-permute-start | bytes 393224 | tf_op jit(solution)/shard_map/ppermute | solution.py:33
  60.7 4.1 %collective-permute-start.11 = (bf16[2,4,2,4096]{3,2,1,0:T(2,128)(2,1)S(1)}, bf16[2,4,2,4096]{3,2,1,0:T(2,128)(2,1)S(1)}, u32[]{:S(2)}, u32[]{:S(2)}) collective-permute-start(bf16[2,4,2,4096]{3,2,1,0:T(2,128)(2,1)S(1)} %get-tuple-element.79), channel_id=1, source_target_pairs={{0,46},{2,32},{4,34},{6,36},{8,38},{10,40},{12,42},{14,44},{16,62}... | collective-permute-start | bytes 393224 | tf_op jit(solution)/shard_map/ppermute | solution.py:33
  64.8 3.3 %collective-permute-done.9 = bf16[2,4,2,4096]{3,2,1,0:T(2,128)(2,1)S(1)} collective-permute-done((bf16[2,4,2,4096]{3,2,1,0:T(2,128)(2,1)S(1)}, bf16[2,4,2,4096]{3,2,1,0:T(2,128)(2,1)S(1)}, u32[]{:S(2)}, u32[]{:S(2)}) %collective-permute-start.9) | collective-permute-done | bytes 131104 | tf_op jit(solution)/shard_map/ppermute | solution.py:33
  68.5 2.4 %collective-permute-start.12 = (bf16[2,16,2,4096]{3,2,1,0:T(2,128)(2,1)S(1)}, bf16[2,16,2,4096]{3,2,1,0:T(2,128)(2,1)S(1)}, u32[]{:S(2)}, u32[]{:S(2)}) collective-permute-start(bf16[2,16,2,4096]{3,2,1,0:T(2,128)(2,1)S(1)} %bitcast.119), channel_id=1, source_target_pairs={{0,48},{16,0},{32,16},{48,32},{1,49},{17,1},{33,17},{49,33},{2,50}... | collective-permute-start | bytes 1572872 | tf_op jit(solution)/shard_map/ppermute | solution.py:33
  72.7 1.6 %collective-permute-start.14 = (bf16[2,8,2,4096]{3,2,1,0:T(2,128)(2,1)S(1)}, bf16[2,8,2,4096]{3,2,1,0:T(2,128)(2,1)S(1)}, u32[]{:S(2)}, u32[]{:S(2)}) collective-permute-start(bf16[2,8,2,4096]{3,2,1,0:T(2,128)(2,1)S(1)} %get-tuple-element.93), channel_id=1, source_target_pairs={{0,14},{2,0},{4,2},{6,4},{8,6},{10,8},{12,10},{14,12},{1,15},{3,1}... | collective-permute-start | bytes 786440 | tf_op jit(solution)/shard_map/ppermute | solution.py:33
  74.4 2.2 %copy-done.2 = bf16[2,16,256,256]{3,2,1,0:T(8,128)(2,1)S(1)} copy-done((bf16[2,16,256,256]{3,2,1,0:T(8,128)(2,1)S(1)}, bf16[2,16,256,256]{3,2,1,0:T(8,128)(2,1)}, u32[]{:S(2)}) %copy-start.2) | copy-done | bytes 4194328
  76.6 7.6 %shard_map.50 = (bf16[2,16,256,512]{3,2,1,0:T(8,128)(2,1)}, f32[8,512]{1,0:T(8,128)S(1)}) custom-call(bf16[512,2,4096]{2,1,0:T(2,128)(2,1)} %x_ref.3, bf16[2,16,256,256]{3,2,1,0:T(8,128)(2,1)S(1)} %copy-done.2, bf16[2,16,256,512]{3,2,1,0:T(8,128)(2,1)} %get-tuple-element.62.refs_0_), custom_call_target="tpu_custom_call", output_to_operand_aliasing={{0}: (2, {})} | custom-call | flops 536870912 | bytes 15728640 | tf_op jit(solution)/shard_map/pallas_call | solution.py:184
  84.2 10.1 %shard_map.51 = (f32[2,2,16,512]{3,2,1,0:T(8,128)S(1)}, f32[2,2,16,512]{3,2,1,0:T(8,128)S(1)}) custom-call(s32[2]{0:T(128)S(1)} %pad_add_fusion.place, bf16[2,16,2,4096]{3,2,1,0:T(2,128)(2,1)S(1)} %bitcast.122, bf16[2,16,2,4096]{3,2,1,0:T(2,128)(2,1)S(1)} %collective-permute-done.12.refs_1_, bf16[2,8,2,4096]{3,2,1,0:T(2,128)(2,1)S(1)} %collective-permute-done.13.refs_2_, ...), custom_call_target="tpu_custom_call" | custom-call | flops 1610612736 | bytes 14680064 | tf_op jit(solution)/shard_map/pallas_call | solution.py:262
  94.3 6.4 %collective-permute-start.16 = (f32[2,2,16,512]{3,2,1,0:T(8,128)S(1)}, f32[2,2,16,512]{3,2,1,0:T(8,128)S(1)}, u32[]{:S(2)}, u32[]{:S(2)}) collective-permute-start(f32[2,2,16,512]{3,2,1,0:T(8,128)S(1)} %get-tuple-element.70), channel_id=1, source_target_pairs={{0,64},{64,0},{1,65},{65,1},{2,66},{66,2},{3,67},{67,3},{4,68},{68... | collective-permute-start | bytes 393224 | tf_op jit(solution)/shard_map/ppermute | solution.py:280
  104.4 2.1 %collective-permute-done.17 = f32[2,16,512]{2,1,0:T(8,128)S(1)} collective-permute-done((f32[2,16,512]{2,1,0:T(8,128)S(1)}, f32[2,16,512]{2,1,0:T(8,128)S(1)}, u32[]{:S(2)}, u32[]{:S(2)}) %collective-permute-start.17) | collective-permute-done | bytes 65568 | tf_op jit(solution)/shard_map/ppermute | solution.py:280
  (63 shorter events, 12.5 us)
Async XLA Ops:
  0.0 14.7 %copy-start.4 = (s32[2]{0:T(128)S(1)}, s32[2]{0:T(128)}, u32[]{:S(2)}) copy-start(s32[2]{0:T(128)} %param.6) | copy-start | bytes 28
  5.5 19.2 %collective-permute-start = (bf16[32,2,4096]{2,1,0:T(2,128)(2,1)}, bf16[32,2,4096]{2,1,0:T(2,128)(2,1)S(1)}, u32[]{:S(2)}, u32[]{:S(2)}) collective-permute-start(bf16[32,2,4096]{2,1,0:T(2,128)(2,1)} %get-tuple-element.40), channel_id=1, source_target_pairs={{0,16},{16,32},{32,48},{48,0},{1,17},{17,33},{33,49},{49,1},{2,18}... | collective-permute-start | bytes 1572872 | tf_op jit(solution)/shard_map/ppermute | solution.py:33
  7.6 17.1 %collective-permute-start.1 = (bf16[32,2,4096]{2,1,0:T(2,128)(2,1)}, bf16[32,2,4096]{2,1,0:T(2,128)(2,1)S(1)}, u32[]{:S(2)}, u32[]{:S(2)}) collective-permute-start(bf16[32,2,4096]{2,1,0:T(2,128)(2,1)} %get-tuple-element.41), channel_id=1, source_target_pairs={{0,48},{16,0},{32,16},{48,32},{1,49},{17,1},{33,17},{49,33},{2,50}... | collective-permute-start | bytes 1572872 | tf_op jit(solution)/shard_map/ppermute | solution.py:33
  9.0 15.7 %collective-permute-start.2 = (bf16[16,2,4096]{2,1,0:T(2,128)(2,1)}, bf16[16,2,4096]{2,1,0:T(2,128)(2,1)S(1)}, u32[]{:S(2)}, u32[]{:S(2)}) collective-permute-start(bf16[16,2,4096]{2,1,0:T(2,128)(2,1)} %get-tuple-element.42), channel_id=1, source_target_pairs={{0,2},{2,4},{4,6},{6,8},{8,10},{10,12},{12,14},{14,0},{1,3},{3,5},... | collective-permute-start | bytes 786440 | tf_op jit(solution)/shard_map/ppermute | solution.py:33
  10.7 14.0 %collective-permute-start.3 = (bf16[16,2,4096]{2,1,0:T(2,128)(2,1)}, bf16[16,2,4096]{2,1,0:T(2,128)(2,1)S(1)}, u32[]{:S(2)}, u32[]{:S(2)}) collective-permute-start(bf16[16,2,4096]{2,1,0:T(2,128)(2,1)} %get-tuple-element.43), channel_id=1, source_target_pairs={{0,14},{2,0},{4,2},{6,4},{8,6},{10,8},{12,10},{14,12},{1,15},{3,1}... | collective-permute-start | bytes 786440 | tf_op jit(solution)/shard_map/ppermute | solution.py:33
  14.9 2.2 %copy-start = (bf16[2,16,256,256]{3,2,1,0:T(8,128)(2,1)S(1)}, bf16[2,16,256,256]{3,2,1,0:T(8,128)(2,1)}, u32[]{:S(2)}) copy-start(bf16[2,16,256,256]{3,2,1,0:T(8,128)(2,1)} %refs_5_.1) | copy-start | bytes 12582916
  17.1 7.6 %copy-start.3 = (bf16[32,2,4096]{2,1,0:T(2,128)(2,1)S(1)}, bf16[32,2,4096]{2,1,0:T(2,128)(2,1)}, u32[]{:S(2)}) copy-start(bf16[32,2,4096]{2,1,0:T(2,128)(2,1)} %get-tuple-element.50) | copy-start | bytes 1572868
  25.6 14.9 %collective-permute-start.4 = (bf16[2,4,2,4096]{3,2,1,0:T(2,128)(2,1)S(1)}, bf16[2,4,2,4096]{3,2,1,0:T(2,128)(2,1)S(1)}, u32[]{:S(2)}, u32[]{:S(2)}) collective-permute-start(bf16[2,4,2,4096]{3,2,1,0:T(2,128)(2,1)S(1)} %get-tuple-element.92), channel_id=1, source_target_pairs={{0,34},{2,36},{4,38},{6,40},{8,42},{10,44},{12,46},{14,32},{16,50}... | collective-permute-start | bytes 393224 | tf_op jit(solution)/shard_map/ppermute | solution.py:33
  25.7 14.8 %collective-permute-start.5 = (bf16[2,4,2,4096]{3,2,1,0:T(2,128)(2,1)S(1)}, bf16[2,4,2,4096]{3,2,1,0:T(2,128)(2,1)S(1)}, u32[]{:S(2)}, u32[]{:S(2)}) collective-permute-start(bf16[2,4,2,4096]{3,2,1,0:T(2,128)(2,1)S(1)} %get-tuple-element.91), channel_id=1, source_target_pairs={{0,4},{2,6},{4,8},{6,10},{8,12},{10,14},{12,0},{14,2},{1,5},{3,7},... | collective-permute-start | bytes 393224 | tf_op jit(solution)/shard_map/ppermute | solution.py:33
  28.9 11.7 %collective-permute-start.6 = (bf16[2,4,2,4096]{3,2,1,0:T(2,128)(2,1)S(1)}, bf16[2,4,2,4096]{3,2,1,0:T(2,128)(2,1)S(1)}, u32[]{:S(2)}, u32[]{:S(2)}) collective-permute-start(bf16[2,4,2,4096]{3,2,1,0:T(2,128)(2,1)S(1)} %get-tuple-element.90), channel_id=1, source_target_pairs={{0,46},{2,32},{4,34},{6,36},{8,38},{10,40},{12,42},{14,44},{16,62}... | collective-permute-start | bytes 393224 | tf_op jit(solution)/shard_map/ppermute | solution.py:33
  30.8 2.2 %copy-start.1 = (bf16[2,16,256,256]{3,2,1,0:T(8,128)(2,1)S(1)}, bf16[2,16,256,256]{3,2,1,0:T(8,128)(2,1)}, u32[]{:S(2)}) copy-start(bf16[2,16,256,256]{3,2,1,0:T(8,128)(2,1)} %refs_5_.1) | copy-start | bytes 12582916
  41.1 11.6 %collective-permute-start.7 = (bf16[2,4,2,4096]{3,2,1,0:T(2,128)(2,1)S(1)}, bf16[2,4,2,4096]{3,2,1,0:T(2,128)(2,1)S(1)}, u32[]{:S(2)}, u32[]{:S(2)}) collective-permute-start(bf16[2,4,2,4096]{3,2,1,0:T(2,128)(2,1)S(1)} %broadcast_select_fusion.10), channel_id=1, source_target_pairs={{0,8},{2,10},{4,12},{6,14},{8,0},{10,2},{12,4},{14,6},{1,9},{3,11}... | collective-permute-start | bytes 393224 | tf_op jit(solution)/shard_map/ppermute | solution.py:33
  53.0 5.4 %collective-permute-start.8 = (bf16[2,4,2,4096]{3,2,1,0:T(2,128)(2,1)S(1)}, bf16[2,4,2,4096]{3,2,1,0:T(2,128)(2,1)S(1)}, u32[]{:S(2)}, u32[]{:S(2)}) collective-permute-start(bf16[2,4,2,4096]{3,2,1,0:T(2,128)(2,1)S(1)} %broadcast_select_fusion.11), channel_id=1, source_target_pairs={{0,1},{1,0},{2,3},{3,2},{4,5},{5,4},{6,7},{7,6},{8,9},{9,8},{10,11... | collective-permute-start | bytes 393224 | tf_op jit(solution)/shard_map/ppermute | solution.py:33
  59.2 8.9 %collective-permute-start.9 = (bf16[2,4,2,4096]{3,2,1,0:T(2,128)(2,1)S(1)}, bf16[2,4,2,4096]{3,2,1,0:T(2,128)(2,1)S(1)}, u32[]{:S(2)}, u32[]{:S(2)}) collective-permute-start(bf16[2,4,2,4096]{3,2,1,0:T(2,128)(2,1)S(1)} %get-tuple-element.79), channel_id=1, source_target_pairs={{0,34},{2,36},{4,38},{6,40},{8,42},{10,44},{12,46},{14,32},{16,50}... | collective-permute-start | bytes 393224 | tf_op jit(solution)/shard_map/ppermute | solution.py:33
  60.7 7.6 %collective-permute-start.10 = (bf16[2,4,2,4096]{3,2,1,0:T(2,128)(2,1)S(1)}, bf16[2,4,2,4096]{3,2,1,0:T(2,128)(2,1)S(1)}, u32[]{:S(2)}, u32[]{:S(2)}) collective-permute-start(bf16[2,4,2,4096]{3,2,1,0:T(2,128)(2,1)S(1)} %get-tuple-element.79), channel_id=1, source_target_pairs={{0,4},{2,6},{4,8},{6,10},{8,12},{10,14},{12,0},{14,2},{1,5},{3,7},... | collective-permute-start | bytes 393224 | tf_op jit(solution)/shard_map/ppermute | solution.py:33
  60.7 7.7 %collective-permute-start.11 = (bf16[2,4,2,4096]{3,2,1,0:T(2,128)(2,1)S(1)}, bf16[2,4,2,4096]{3,2,1,0:T(2,128)(2,1)S(1)}, u32[]{:S(2)}, u32[]{:S(2)}) collective-permute-start(bf16[2,4,2,4096]{3,2,1,0:T(2,128)(2,1)S(1)} %get-tuple-element.79), channel_id=1, source_target_pairs={{0,46},{2,32},{4,34},{6,36},{8,38},{10,40},{12,42},{14,44},{16,62}... | collective-permute-start | bytes 393224 | tf_op jit(solution)/shard_map/ppermute | solution.py:33
  68.5 15.7 %collective-permute-start.12 = (bf16[2,16,2,4096]{3,2,1,0:T(2,128)(2,1)S(1)}, bf16[2,16,2,4096]{3,2,1,0:T(2,128)(2,1)S(1)}, u32[]{:S(2)}, u32[]{:S(2)}) collective-permute-start(bf16[2,16,2,4096]{3,2,1,0:T(2,128)(2,1)S(1)} %bitcast.119), channel_id=1, source_target_pairs={{0,48},{16,0},{32,16},{48,32},{1,49},{17,1},{33,17},{49,33},{2,50}... | collective-permute-start | bytes 1572872 | tf_op jit(solution)/shard_map/ppermute | solution.py:33
  70.9 13.3 %collective-permute-start.15 = (bf16[2,16,2,4096]{3,2,1,0:T(2,128)(2,1)S(1)}, bf16[2,16,2,4096]{3,2,1,0:T(2,128)(2,1)S(1)}, u32[]{:S(2)}, u32[]{:S(2)}) collective-permute-start(bf16[2,16,2,4096]{3,2,1,0:T(2,128)(2,1)S(1)} %bitcast.120), channel_id=1, source_target_pairs={{0,16},{16,32},{32,48},{48,0},{1,17},{17,33},{33,49},{49,1},{2,18}... | collective-permute-start | bytes 1572872 | tf_op jit(solution)/shard_map/ppermute | solution.py:33
  71.3 12.9 %collective-permute-start.13 = (bf16[2,8,2,4096]{3,2,1,0:T(2,128)(2,1)S(1)}, bf16[2,8,2,4096]{3,2,1,0:T(2,128)(2,1)S(1)}, u32[]{:S(2)}, u32[]{:S(2)}) collective-permute-start(bf16[2,8,2,4096]{3,2,1,0:T(2,128)(2,1)S(1)} %get-tuple-element.94), channel_id=1, source_target_pairs={{0,2},{2,4},{4,6},{6,8},{8,10},{10,12},{12,14},{14,0},{1,3},{3,5},... | collective-permute-start | bytes 786440 | tf_op jit(solution)/shard_map/ppermute | solution.py:33
  72.7 11.5 %collective-permute-start.14 = (bf16[2,8,2,4096]{3,2,1,0:T(2,128)(2,1)S(1)}, bf16[2,8,2,4096]{3,2,1,0:T(2,128)(2,1)S(1)}, u32[]{:S(2)}, u32[]{:S(2)}) collective-permute-start(bf16[2,8,2,4096]{3,2,1,0:T(2,128)(2,1)S(1)} %get-tuple-element.93), channel_id=1, source_target_pairs={{0,14},{2,0},{4,2},{6,4},{8,6},{10,8},{12,10},{14,12},{1,15},{3,1}... | collective-permute-start | bytes 786440 | tf_op jit(solution)/shard_map/ppermute | solution.py:33
  94.3 8.9 %collective-permute-start.16 = (f32[2,2,16,512]{3,2,1,0:T(8,128)S(1)}, f32[2,2,16,512]{3,2,1,0:T(8,128)S(1)}, u32[]{:S(2)}, u32[]{:S(2)}) collective-permute-start(f32[2,2,16,512]{3,2,1,0:T(8,128)S(1)} %get-tuple-element.70), channel_id=1, source_target_pairs={{0,64},{64,0},{1,65},{65,1},{2,66},{66,2},{3,67},{67,3},{4,68},{68... | collective-permute-start | bytes 393224 | tf_op jit(solution)/shard_map/ppermute | solution.py:280
  100.7 1.2 %collective-permute-start.18 = (f32[512]{0:T(512)S(1)}, f32[512]{0:T(512)S(1)}, u32[]{:S(2)}, u32[]{:S(2)}) collective-permute-start(f32[512]{0:T(512)S(1)} %add_reduce_fusion), channel_id=1, source_target_pairs={{0,64},{64,0},{1,65},{65,1},{2,66},{66,2},{3,67},{67,3},{4,68},{68... | collective-permute-start | bytes 6152 | tf_op jit(solution)/shard_map/ppermute | solution.py:280
  101.9 2.4 %collective-permute-start.19 = (f32[512]{0:T(512)S(1)}, f32[512]{0:T(512)S(1)}, u32[]{:S(2)}, u32[]{:S(2)}) collective-permute-start(f32[512]{0:T(512)S(1)} %add.255), channel_id=1, source_target_pairs={{0,128},{128,0},{1,129},{129,1},{2,130},{130,2},{3,131},{131,3},{4... | collective-permute-start | bytes 6152 | tf_op jit(solution)/shard_map/ppermute | solution.py:280
  103.3 3.2 %collective-permute-start.17 = (f32[2,16,512]{2,1,0:T(8,128)S(1)}, f32[2,16,512]{2,1,0:T(8,128)S(1)}, u32[]{:S(2)}, u32[]{:S(2)}) collective-permute-start(f32[2,16,512]{2,1,0:T(8,128)S(1)} %dynamic-slice_bitcast_fusion), channel_id=1, source_target_pairs={{0,128},{128,0},{1,129},{129,1},{2,130},{130,2},{3,131},{131,3},{4... | collective-permute-start | bytes 196616 | tf_op jit(solution)/shard_map/ppermute | solution.py:280
  (1 other events, 2.2 us)
where the time goes:
time: 108 us; the launch traced here: 107 us
  Pallas kernels  44 us (41%)
  starting transfers between devices  40.4 us (37%)
  waiting for transfers between devices  9.85 us (9%)
  local copies, waits for them, and re-layouts  9.66 us (9%)
  other arithmetic  2.94 us (3%)
    ppermute x16, starting transfers between devices, shift(): return lax.ppermute(value, names if len(names) > 1 else names[0], pairs)  32.4 us
    pallas_call x4, Pallas kernels, whiten_blocks(): pl.pallas_call(whiten_kernel, grid=(count // nb,), out_shape=[jax.ShapeDt...  30.3 us
    pallas_call x1, Pallas kernels, score(): pl.pallas_call(score_kernel, grid=(nblock // nb,), out_shape=[out, out],...  10.1 us
    ppermute x4, starting transfers between devices, swap(): return lax.ppermute(value, axis, [(0, 1), (1, 0)])  8.02 us
    unnamed x10, local copies, waits for them, and re-layouts  6.57 us
    ppermute x16, waiting for transfers between devices, shift(): return lax.ppermute(value, names if len(names) > 1 else names[0], pairs)  5.77 us
    ppermute x4, waiting for transfers between devices, swap(): return lax.ppermute(value, axis, [(0, 1), (1, 0)])  4.08 us
    pallas_call x1, Pallas kernels, pick_rows(): pl.pallas_call(functools.partial(pick_kernel, counts), out_shape=[jax.Sha...  3.6 us
  transfers between devices with their start and end apart: 20, of which 5 were waited for; matrix products, arithmetic and copies ran while one was open for 1% of the time, Pallas kernels for 28%

commit v1 on v0

v1 whole, which is shorter than its diff:
```python
import functools
import itertools

import jax
import jax.numpy as jnp
from jax import lax
from jax.experimental import pallas as pl
from jax.experimental.pallas import tpu as pltpu
from jax.sharding import Mesh
from jax.sharding import PartitionSpec as P

NX, NZ, NY = 4, 8, 2
DP = ("x", "z", "yhi")
LAYER = ("ylo", "core")
AXES = LAYER + DP
SIZES = dict(x=NX, z=NZ, yhi=NY)
NT = (((1,), (1,)), ((), ()))
STEPS = (1, 2, -1)
SMALL_LIMIT, SCORE_LIMIT, LARGE_LIMIT = 8 * 2**20, 40 * 2**20, 57 * 2**20
IN_VMEM = pl.BlockSpec(memory_space=pltpu.VMEM)
IN_SMEM = pl.BlockSpec(memory_space=pltpu.SMEM)


def shift(value, dx=0, dz=0, dy=0):
    moves = {name: by for name, by in (("x", dx), ("z", dz), ("yhi", dy)) if by}
    names = tuple(moves)

    def index(place):
        flat = 0
        for name, at in zip(names, place):
            flat = flat * SIZES[name] + at % SIZES[name]
        return flat

    pairs = [
        (index(place), index([at + moves[name] for name, at in zip(names, place)]))
        for place in itertools.product(*(range(SIZES[name]) for name in names))
    ]
    return lax.ppermute(value, names if len(names) > 1 else names[0], pairs)


def swap(value, axis):
    return lax.ppermute(value, axis, [(0, 1), (1, 0)])


def pick_kernel(turns, place, ids, gradients, *rest):
    outs, sem = rest[:-1], rest[-1]
    rounds, queries = ids.shape
    quarter = queries // 4
    for turn, out in zip(turns, outs):
        first = lax.rem(place[0] + turn, 4) * quarter
        for which in range(rounds):
            for row in range(quarter):
                pltpu.make_async_copy(
                    gradients.at[ids[which, first + row]], out.at[which * quarter + row], sem
                ).start()
    for out in outs:
        pltpu.make_async_copy(gradients.at[pl.ds(0, out.shape[0])], out, sem).wait()


def pick_rows(gradients, query_ids, place, turns):
    count = query_ids.size // 4
    out = jax.ShapeDtypeStruct((count,) + gradients.shape[1:], gradients.dtype)
    moved = 2 * len(turns) * out.size * 2
    return pl.pallas_call(
        functools.partial(pick_kernel, turns),
        out_shape=[out for _ in turns],
        in_specs=[IN_SMEM, IN_SMEM, pl.BlockSpec(memory_space=pl.ANY)],
        out_specs=[IN_VMEM for _ in turns],
        scratch_shapes=[pltpu.SemaphoreType.DMA],
        compiler_params=pltpu.CompilerParams(vmem_limit_bytes=LARGE_LIMIT),
        cost_estimate=pl.CostEstimate(flops=0, bytes_accessed=moved, transcendentals=0),
    )(place, query_ids, gradients)


def split_kernel(same, rows_ref, other_ref, piece_ref, whole_ref):
    rounds, part, layers, _ = rows_ref.shape
    for which in range(rounds):
        keep = same[which] > 0
        for layer in range(layers):
            value = jnp.where(keep, rows_ref[which, :, layer, :], other_ref[which, :, layer, :])
            piece_ref[layer, which * part : (which + 1) * part] = value
            whole_ref[0, layer, which * part : (which + 1) * part] = value


def split_layers(same, rows, other):
    rounds, part, layers, proj = rows.shape
    piece = (layers, rounds * part, proj)
    return pl.pallas_call(
        split_kernel,
        out_shape=[
            jax.ShapeDtypeStruct(piece, rows.dtype),
            jax.ShapeDtypeStruct((4,) + piece, rows.dtype),
        ],
        in_specs=[IN_SMEM, IN_VMEM, IN_VMEM],
        out_specs=[IN_VMEM, IN_VMEM],
        compiler_params=pltpu.CompilerParams(vmem_limit_bytes=SMALL_LIMIT),
        cost_estimate=pl.CostEstimate(flops=0, bytes_accessed=8 * rows.size, transcendentals=0),
    )(same, rows, other)


def per_round(flag):
    return flag.reshape(-1, 1, 1, 1)


def piece(parts, at):
    return lax.dynamic_index_in_dim(parts, at, 1, keepdims=False)


def broadcast(gradients, owners, query_ids, place, beside):
    rounds, queries = query_ids.shape
    tail = gradients.shape[1:]
    part = queries // 16
    x, z, y = (lax.axis_index(name) for name in DP)
    colour = (x + 2 * z) % 4
    own_x, own_z, own_y = owners // (NZ * NY), owners // NY % NZ, owners % NY
    far_x, far_z, same_y = (x - own_x) % NX, (z - own_z) % NZ, y == own_y

    to_right, to_left, to_up = pick_rows(gradients, query_ids, place, (1, 3, 2))
    given = shift(to_right, dx=1), shift(to_left, dx=-1), shift(to_up, dz=1)
    rows, _ = lax.optimization_barrier((gradients, to_up))
    (own,) = pick_rows(rows, query_ids, place, (0,))
    given = beside(given, own, 2)
    own, from_left, from_right, from_below = (
        rows.reshape(rounds, 4, part, *tail) for rows in (own,) + tuple(given)
    )

    def held(at):
        out = jnp.where(per_round((far_x == 0) & (far_z == 1)), piece(from_below, at), piece(own, at))
        out = jnp.where(per_round((far_x == 1) & (far_z == 0)), piece(from_left, at), out)
        return jnp.where(per_round((far_x == 3) & (far_z == 0)), piece(from_right, at), out)

    mine = z % 4
    pieces = [held((z + by) % 4) for by in STEPS]
    got = [shift(rows, dx=(-2 * by) % 4, dz=by) for by, rows in zip(STEPS, pieces)]
    got = beside(tuple(got), pieces[0], 2)
    own_colour = (own_x + 2 * own_z) % 4
    source_z = own_z + jnp.where((colour - own_colour) % 4 == 2, 1, 0)
    away = (z - source_z) % NZ
    part_rows = held(mine)
    for by, rows in zip(STEPS, got):
        part_rows = jnp.where(per_round(away == by % NZ), rows, part_rows)

    near = (away <= 2) | (away == 7)
    (moved,) = beside((shift(part_rows, dz=4),), part_rows, 2)
    part_rows = jnp.where(per_round(near), part_rows, moved)
    (moved,) = beside((shift(part_rows, dy=1),), part_rows, 1)
    mine_rows, whole = split_layers(same_y.astype(jnp.int32), part_rows, moved)

    got = [shift(mine_rows, dx=(-2 * by) % 4, dz=by) for by in STEPS]
    got = beside(tuple(got), mine_rows, 1)
    for at, rows in enumerate(got):
        whole = lax.dynamic_update_index_in_dim(whole, rows, at + 1, 0)

    return whole, shift(whole, dx=-1), shift(whole, dz=1), shift(whole, dx=1)


def whiten_kernel(x_ref, w_ref, *refs):
    white_ref, norm_ref = refs[-2:]
    layers, nb, block = w_ref.shape[:3]
    total = jnp.zeros(norm_ref.shape, jnp.float32)
    for b in range(nb):
        for layer in range(layers):
            y = lax.dot_general(
                w_ref[layer, b],
                x_ref[:, layer, b * block : (b + 1) * block],
                NT,
                preferred_element_type=jnp.float32,
            )
            white_ref[layer, b] = y.astype(white_ref.dtype)
            total = total + jnp.sum((y * y).reshape(-1, *total.shape), axis=0)

    @pl.when(pl.program_id(0) == 0)
    def _():
        norm_ref[...] = jnp.zeros_like(norm_ref)

    norm_ref[...] += total


def whiten_blocks(gradients, whitener, white, first, count, nb=2):
    examples, layers, proj = gradients.shape
    nblock, block = whitener.shape[1:3]
    base = first // nb
    cost = pl.CostEstimate(
        flops=2 * layers * count * block * block * examples,
        bytes_accessed=layers * count * block * (4 * examples + 2 * block) * 3,
        transcendentals=0,
    )
    operands, aliases, extra = [gradients, whitener], {}, []
    if white is not None:
        operands.append(white)
        aliases, extra = {2: 0}, [pl.BlockSpec(memory_space=pl.ANY)]
    return pl.pallas_call(
        whiten_kernel,
        grid=(count // nb,),
        out_shape=[
            jax.ShapeDtypeStruct((layers, nblock, block, examples), jnp.bfloat16),
            jax.ShapeDtypeStruct((8, examples), jnp.float32),
        ],
        in_specs=[
            pl.BlockSpec((examples, layers, nb * block), lambda i: (0, 0, base + i)),
            pl.BlockSpec((layers, nb, block, block), lambda i: (0, base + i, 0, 0)),
        ]
        + extra,
        out_specs=[
            pl.BlockSpec((layers, nb, block, examples), lambda i: (0, base + i, 0, 0)),
            pl.BlockSpec((8, examples), lambda i: (0, 0)),
        ],
        input_output_aliases=aliases,
        compiler_params=pltpu.CompilerParams(vmem_limit_bytes=LARGE_LIMIT),
        cost_estimate=cost,
    )(*operands)


def score_kernel(place, *refs):
    groups, (w_ref, white_ref, keep_ref, send_ref, total_ref) = refs[:4], refs[4:]
    layers, nb, block = w_ref.shape[:3]
    step = pl.program_id(0)

    @pl.when(step == 0)
    def _():
        total_ref[...] = jnp.zeros_like(total_ref)

    total = jnp.zeros(total_ref.shape, jnp.float32)
    for layer in range(layers):
        rows = jnp.concatenate([g[:, layer].reshape(-1, g.shape[-1]) for g in groups], axis=0)
        query = [
            lax.dot_general(
                rows[:, b * block : (b + 1) * block], w_ref[layer, b], NT, preferred_element_type=jnp.float32
            ).astype(white_ref.dtype)
            for b in range(nb)
        ]
        total = total + jnp.dot(
            jnp.concatenate(query, axis=1),
            white_ref[layer].reshape(nb * block, -1),
            preferred_element_type=jnp.float32,
        )
    total_ref[...] += total

    @pl.when(step == pl.num_programs(0) - 1)
    def _():
        colour, core, z = place[0], place[1], place[2]
        rounds, part = keep_ref.shape[0], keep_ref.shape[3]
        for turn in range(4):
            at = lax.rem(colour + turn, 4)
            from_z = z + 8 - (1 if turn == 2 else 0)
            for ref, kept in ((keep_ref, True), (send_ref, False)):

                @pl.when((at // 2 == core) == kept)
                def _(ref=ref, turn=turn, at=at, from_z=from_z):
                    for slot, back in enumerate((0,) + STEPS):
                        for which in range(rounds):
                            start = ((turn * 4 + slot) * rounds + which) * part
                            to = lax.rem(from_z - back, 4)
                            ref[which, lax.rem(at, 2), to] = total_ref[start : start + part]


def score(groups, whitener, white, place, rounds, nb=8):
    layers, nblock, block, examples = white.shape
    part = groups[0].shape[2] // rounds
    count = 16 * rounds * part
    out = jax.ShapeDtypeStruct((rounds, 2, 4, part, examples), jnp.float32)
    out_spec = pl.BlockSpec(out.shape, lambda i: (0, 0, 0, 0, 0))
    cost = pl.CostEstimate(
        flops=2 * layers * nblock * block * count * (block + examples),
        bytes_accessed=2 * layers * nblock * block * (examples + block + count),
        transcendentals=0,
    )
    return pl.pallas_call(
        score_kernel,
        grid=(nblock // nb,),
        out_shape=[out, out],
        in_specs=[IN_SMEM]
        + [pl.BlockSpec(g.shape[:3] + (nb * block,), lambda i: (0, 0, 0, i)) for g in groups]
        + [
            pl.BlockSpec((layers, nb, block, block), lambda i: (0, i, 0, 0)),
            pl.BlockSpec((layers, nb, block, examples), lambda i: (0, i, 0, 0)),
        ],
        out_specs=[out_spec, out_spec],
        scratch_shapes=[pltpu.VMEM((count, examples), jnp.float32)],
        compiler_params=pltpu.CompilerParams(vmem_limit_bytes=SCORE_LIMIT),
        cost_estimate=cost,
    )(place, *groups, whitener, white)


UNITS = 8


def local(gradients, whitener, owners, query_ids):
    count = gradients.shape[0]
    rounds = owners.shape[0]
    unit = whitener.shape[1] // UNITS
    x, z = lax.axis_index("x"), lax.axis_index("z")
    core, ylo = lax.axis_index("core"), lax.axis_index("ylo")
    place = jnp.stack([(x + 2 * z) % 4, core, z]).astype(jnp.int32)
    norms, done = [], dict(units=0, white=None)

    def beside(values, sent, units):
        rows, _ = lax.optimization_barrier((gradients, sent))
        done["white"], norm = whiten_blocks(
            rows, whitener, done["white"], done["units"] * unit, units * unit
        )
        values, norm = lax.optimization_barrier((values, norm))
        norms.append(norm)
        done["units"] += units
        return values

    groups = broadcast(gradients, owners, query_ids, place, beside)
    norm, _ = lax.optimization_barrier((jnp.sum(sum(norms), axis=0), groups[0]))
    norm = norm + swap(norm, "core")
    norm = norm + swap(norm, "ylo")
    groups, norm = lax.optimization_barrier((groups, norm))

    keep, send = score(groups, whitener, done["white"], place, rounds)
    half = keep + swap(send, "core")
    mine = lax.dynamic_index_in_dim(half, ylo, 0, keepdims=False)
    mine = mine + swap(lax.dynamic_index_in_dim(half, 1 - ylo, 0, keepdims=False), "ylo")
    return mine.reshape(-1, count) / jnp.sqrt(norm + 1e-06)[None, :]


def solution(mesh):
    torus = Mesh(mesh.devices.reshape(2, 2, NX, NZ, NY), AXES)
    in_specs = (P(DP, LAYER, None), P(LAYER, None, None, None), P(), P())
    return jax.shard_map(
        local, mesh=torus, in_specs=in_specs, out_specs=P(LAYER, DP), check_vma=False
    )
```

time: 108 us -> 97.7 us (0.905)
  local copies, waits for them, and re-layouts: 9.66 us -> 0.11 us
  starting transfers between devices: 40.4 us -> 37 us
  waiting for transfers between devices: 9.85 us -> 11.9 us
    ppermute x16 -> x14, starting transfers between devices: 32.4 us -> 25 us  [shift(): return lax.ppermute(value, names if len(names) > 1 else names[0], pairs)]
    unnamed x10 -> x16, local copies, waits for them, and re-layouts: 6.57 us -> 0.03 us
    pallas_call x1, Pallas kernels: 10.1 us -> 5.39 us  [score(): pl.pallas_call(score_kernel, grid=(nblock // nb,), out_shape=[out, out],...]
    ppermute x4, starting transfers between devices: 8.02 us -> 12 us  [swap(): return lax.ppermute(value, axis, [(0, 1), (1, 0)])]
    pallas_call x1 -> x3, Pallas kernels: 3.6 us -> 6.62 us  [the longest x2 5.75 us: pick_rows(): pl.pallas_call(functools.partial(pick_kernel, turns), out_shape=[out for...]
    ppermute x4, waiting for transfers between devices: 4.08 us -> 6.85 us  [swap(): return lax.ppermute(value, axis, [(0, 1), (1, 0)])]
    pallas_call x4 -> x5, Pallas kernels: 30.3 us -> 32.4 us  [whiten_blocks(): pl.pallas_call(whiten_kernel, grid=(count // nb,), out_shape=[jax.ShapeDt...]
    ppermute x16 -> x14, waiting for transfers between devices: 5.77 us -> 5.02 us  [shift(): return lax.ppermute(value, names if len(names) > 1 else names[0], pairs)]
  transfers between devices with their start and end apart: 20 -> 18, of which waited for: 5 -> 5; matrix products, arithmetic and copies ran while one was open for 1% -> 1% of each run, Pallas kernels for 28% -> 36%
where the time goes in v1:
time: 97.7 us; the launch traced here: 97.3 us
  Pallas kernels  44.4 us (45%)
  starting transfers between devices  37 us (38%)
  waiting for transfers between devices  11.9 us (12%)
  other arithmetic  3.68 us (4%)
    pallas_call x5, Pallas kernels, whiten_blocks(): pl.pallas_call(whiten_kernel, grid=(count // nb,), out_shape=[jax.ShapeDt...  32.4 us
    ppermute x14, starting transfers between devices, shift(): return lax.ppermute(value, names if len(names) > 1 else names[0], pairs)  25 us
    ppermute x4, starting transfers between devices, swap(): return lax.ppermute(value, axis, [(0, 1), (1, 0)])  12 us
    ppermute x4, waiting for transfers between devices, swap(): return lax.ppermute(value, axis, [(0, 1), (1, 0)])  6.85 us
    pallas_call x2, Pallas kernels, pick_rows(): pl.pallas_call(functools.partial(pick_kernel, turns), out_shape=[out for...  5.75 us
    pallas_call x1, Pallas kernels, score(): pl.pallas_call(score_kernel, grid=(nblock // nb,), out_shape=[out, out],...  5.39 us
    ppermute x14, waiting for transfers between devices, shift(): return lax.ppermute(value, names if len(names) > 1 else names[0], pairs)  5.02 us
  transfers between devices with their start and end apart: 18, of which 5 were waited for; matrix products, arithmetic and copies ran while one was open for 1% of the time, Pallas kernels for 36%

profile of v1, /device:TPU:1, one launch (start us, length us, event | category | flops | bytes accessed | tf_op | source)
XLA Modules:
  0.0 97.3 jit_solution(1003971221676040380)
XLA Ops:
  0.6 3.2 %shard_map.46 = (bf16[32,2,4096]{2,1,0:T(2,128)(2,1)}, bf16[32,2,4096]{2,1,0:T(2,128)(2,1)}, bf16[32,2,4096]{2,1,0:T(2,128)(2,1)}) custom-call(s32[3]{0:T(128)} %pad_add_fusion.place, s32[2,64]{1,0:T(2,128)} %ids.3, bf16[512,2,4096]{2,1,0:T(2,128)(2,1)} %x_ref.4), custom_call_target="tpu_custom_call" | custom-call | bytes 3145728 | tf_op jit(solution)/shard_map/pallas_call | solution.py:64
  3.9 2.1 %collective-permute-start = (bf16[32,2,4096]{2,1,0:T(2,128)(2,1)}, bf16[32,2,4096]{2,1,0:T(2,128)(2,1)S(1)}, u32[]{:S(2)}, u32[]{:S(2)}) collective-permute-start(bf16[32,2,4096]{2,1,0:T(2,128)(2,1)} %get-tuple-element.50), channel_id=1, source_target_pairs={{0,16},{16,32},{32,48},{48,0},{1,17},{17,33},{33,49},{49,1},{2,18}... | collective-permute-start | bytes 1572872 | tf_op jit(solution)/shard_map/ppermute | solution.py:38
  6.0 1.4 %collective-permute-start.1 = (bf16[32,2,4096]{2,1,0:T(2,128)(2,1)}, bf16[32,2,4096]{2,1,0:T(2,128)(2,1)S(1)}, u32[]{:S(2)}, u32[]{:S(2)}) collective-permute-start(bf16[32,2,4096]{2,1,0:T(2,128)(2,1)} %get-tuple-element.51), channel_id=1, source_target_pairs={{0,48},{16,0},{32,16},{48,32},{1,49},{17,1},{33,17},{49,33},{2,50}... | collective-permute-start | bytes 1572872 | tf_op jit(solution)/shard_map/ppermute | solution.py:38
  7.3 1.7 %collective-permute-start.2 = (bf16[32,2,4096]{2,1,0:T(2,128)(2,1)}, bf16[32,2,4096]{2,1,0:T(2,128)(2,1)S(1)}, u32[]{:S(2)}, u32[]{:S(2)}) collective-permute-start(bf16[32,2,4096]{2,1,0:T(2,128)(2,1)} %get-tuple-element.52), channel_id=1, source_target_pairs={{0,2},{2,4},{4,6},{6,8},{8,10},{10,12},{12,14},{14,0},{1,3},{3,5},... | collective-permute-start | bytes 1572872 | tf_op jit(solution)/shard_map/ppermute | solution.py:38
  9.2 2.5 %shard_map.47 = bf16[32,2,4096]{2,1,0:T(2,128)(2,1)} custom-call(s32[3]{0:T(128)} %pad_add_fusion.place, s32[2,64]{1,0:T(2,128)} %ids.3, bf16[512,2,4096]{2,1,0:T(2,128)(2,1)} %x_ref.4), custom_call_target="tpu_custom_call" | custom-call | bytes 1048576 | tf_op jit(solution)/shard_map/pallas_call | solution.py:64
  11.7 7.5 %shard_map.48 = (bf16[2,16,256,512]{3,2,1,0:T(8,128)(2,1)}, f32[8,512]{1,0:T(8,128)}) custom-call(bf16[512,2,4096]{2,1,0:T(2,128)(2,1)} %x_ref.4, bf16[2,16,256,256]{3,2,1,0:T(8,128)(2,1)} %refs_4_.1), custom_call_target="tpu_custom_call" | custom-call | flops 536870912 | bytes 15728640 | tf_op jit(solution)/shard_map/pallas_call | solution.py:192
  19.2 5.0 %collective-permute-done.2 = bf16[32,2,4096]{2,1,0:T(2,128)(2,1)S(1)} collective-permute-done((bf16[32,2,4096]{2,1,0:T(2,128)(2,1)}, bf16[32,2,4096]{2,1,0:T(2,128)(2,1)S(1)}, u32[]{:S(2)}, u32[]{:S(2)}) %collective-permute-start.2) | collective-permute-done | bytes 524320 | tf_op jit(solution)/shard_map/ppermute | solution.py:38
  25.1 2.2 %collective-permute-start.4 = (bf16[2,4,2,4096]{3,2,1,0:T(2,128)(2,1)S(1)}, bf16[2,4,2,4096]{3,2,1,0:T(2,128)(2,1)S(1)}, u32[]{:S(2)}, u32[]{:S(2)}) collective-permute-start(bf16[2,4,2,4096]{3,2,1,0:T(2,128)(2,1)S(1)} %get-tuple-element.103), channel_id=1, source_target_pairs={{0,4},{2,6},{4,8},{6,10},{8,12},{10,14},{12,0},{14,2},{1,5},{3,7},... | collective-permute-start | bytes 393224 | tf_op jit(solution)/shard_map/ppermute | solution.py:38
  27.3 2.9 %collective-permute-start.5 = (bf16[2,4,2,4096]{3,2,1,0:T(2,128)(2,1)S(1)}, bf16[2,4,2,4096]{3,2,1,0:T(2,128)(2,1)S(1)}, u32[]{:S(2)}, u32[]{:S(2)}) collective-permute-start(bf16[2,4,2,4096]{3,2,1,0:T(2,128)(2,1)S(1)} %get-tuple-element.102), channel_id=1, source_target_pairs={{0,46},{2,32},{4,34},{6,36},{8,38},{10,40},{12,42},{14,44},{16,62}... | collective-permute-start | bytes 393224 | tf_op jit(solution)/shard_map/ppermute | solution.py:38
  30.2 7.4 %shard_map.49 = (bf16[2,16,256,512]{3,2,1,0:T(8,128)(2,1)}, f32[8,512]{1,0:T(8,128)}) custom-call(bf16[512,2,4096]{2,1,0:T(2,128)(2,1)} %x_ref.4, bf16[2,16,256,256]{3,2,1,0:T(8,128)(2,1)} %refs_4_.1, bf16[2,16,256,512]{3,2,1,0:T(8,128)(2,1)} %get-tuple-element.60.refs_0_), custom_call_target="tpu_custom_call", output_to_operand_aliasing={{0}: (2, {})} | custom-call | flops 536870912 | bytes 15728640 | tf_op jit(solution)/shard_map/pallas_call | solution.py:192
  38.1 4.0 %collective-permute-start.6 = (bf16[2,4,2,4096]{3,2,1,0:T(2,128)(2,1)S(1)}, bf16[2,4,2,4096]{3,2,1,0:T(2,128)(2,1)S(1)}, u32[]{:S(2)}, u32[]{:S(2)}) collective-permute-start(bf16[2,4,2,4096]{3,2,1,0:T(2,128)(2,1)S(1)} %broadcast_select_fusion.2), channel_id=1, source_target_pairs={{0,8},{2,10},{4,12},{6,14},{8,0},{10,2},{12,4},{14,6},{1,9},{3,11}... | collective-permute-start | bytes 393224 | tf_op jit(solution)/shard_map/ppermute | solution.py:38
  42.2 7.4 %shard_map.50 = (bf16[2,16,256,512]{3,2,1,0:T(8,128)(2,1)}, f32[8,512]{1,0:T(8,128)}) custom-call(bf16[512,2,4096]{2,1,0:T(2,128)(2,1)} %x_ref.4, bf16[2,16,256,256]{3,2,1,0:T(8,128)(2,1)} %refs_4_.1, bf16[2,16,256,512]{3,2,1,0:T(8,128)(2,1)} %get-tuple-element.66.refs_0_), custom_call_target="tpu_custom_call", output_to_operand_aliasing={{0}: (2, {})} | custom-call | flops 536870912 | bytes 15728640 | tf_op jit(solution)/shard_map/pallas_call | solution.py:192
  49.8 3.0 %collective-permute-start.7 = (bf16[2,4,2,4096]{3,2,1,0:T(2,128)(2,1)S(1)}, bf16[2,4,2,4096]{3,2,1,0:T(2,128)(2,1)S(1)}, u32[]{:S(2)}, u32[]{:S(2)}) collective-permute-start(bf16[2,4,2,4096]{3,2,1,0:T(2,128)(2,1)S(1)} %broadcast_select_fusion.3.rows_ref), channel_id=1, source_target_pairs={{0,1},{1,0},{2,3},{3,2},{4,5},{5,4},{6,7},{7,6},{8,9},{9,8},{10,11... | collective-permute-start | bytes 393224 | tf_op jit(solution)/shard_map/ppermute | solution.py:38
  52.8 4.9 %shard_map.51 = (bf16[2,16,256,512]{3,2,1,0:T(8,128)(2,1)}, f32[8,512]{1,0:T(8,128)}) custom-call(bf16[512,2,4096]{2,1,0:T(2,128)(2,1)} %x_ref.4, bf16[2,16,256,256]{3,2,1,0:T(8,128)(2,1)} %refs_4_.1, bf16[2,16,256,512]{3,2,1,0:T(8,128)(2,1)} %get-tuple-element.70.refs_0_), custom_call_target="tpu_custom_call", output_to_operand_aliasing={{0}: (2, {})} | custom-call | flops 268435456 | bytes 7864320 | tf_op jit(solution)/shard_map/pallas_call | solution.py:192
  58.6 1.0 collective-permute-start.8
  59.8 4.7 %collective-permute-start.10 = (bf16[2,8,4096]{2,1,0:T(8,128)(2,1)S(1)}, bf16[2,8,4096]{2,1,0:T(8,128)(2,1)S(1)}, u32[]{:S(2)}, u32[]{:S(2)}) collective-permute-start(bf16[2,8,4096]{2,1,0:T(8,128)(2,1)S(1)} %get-tuple-element.74), channel_id=1, source_target_pairs={{0,46},{2,32},{4,34},{6,36},{8,38},{10,40},{12,42},{14,44},{16,62}... | collective-permute-start | bytes 393224 | tf_op jit(solution)/shard_map/ppermute | solution.py:38
  64.5 5.1 %shard_map.53 = (bf16[2,16,256,512]{3,2,1,0:T(8,128)(2,1)}, f32[8,512]{1,0:T(8,128)}) custom-call(bf16[512,2,4096]{2,1,0:T(2,128)(2,1)} %x_ref.4, bf16[2,16,256,256]{3,2,1,0:T(8,128)(2,1)} %refs_4_.1, bf16[2,16,256,512]{3,2,1,0:T(8,128)(2,1)} %get-tuple-element.76.refs_0_), custom_call_target="tpu_custom_call", output_to_operand_aliasing={{0}: (2, {})} | custom-call | flops 268435456 | bytes 7864320 | tf_op jit(solution)/shard_map/pallas_call | solution.py:192
  69.7 1.6 %collective-permute-start.11 = (bf16[4,2,8,4096]{3,2,1,0:T(8,128)(2,1)S(1)}, bf16[4,2,8,4096]{3,2,1,0:T(8,128)(2,1)S(1)}, u32[]{:S(2)}, u32[]{:S(2)}) collective-permute-start(bf16[4,2,8,4096]{3,2,1,0:T(8,128)(2,1)S(1)} %bitcast_dynamic-update-slice_fusion.refs_0_), channel_id=1, source_target_pairs={{0,48},{16,0},{32,16},{48,32},{1,49},{17,1},{33,17},{49,33},{2,50}... | collective-permute-start | bytes 1572872 | tf_op jit(solution)/shard_map/ppermute | solution.py:38
  72.2 5.3 %collective-permute-start.14 = (f32[512]{0:T(512)S(1)}, f32[512]{0:T(512)S(1)}, u32[]{:S(2)}, u32[]{:S(2)}) collective-permute-start(f32[512]{0:T(512)S(1)} %add_reduce_fusion), channel_id=1, source_target_pairs={{0,64},{64,0},{1,65},{65,1},{2,66},{66,2},{3,67},{67,3},{4,68},{68... | collective-permute-start | bytes 6152 | tf_op jit(solution)/shard_map/ppermute | solution.py:42
  78.7 2.3 %collective-permute-done.15 = f32[512]{0:T(512)S(1)} collective-permute-done((f32[512]{0:T(512)S(1)}, f32[512]{0:T(512)S(1)}, u32[]{:S(2)}, u32[]{:S(2)}) %collective-permute-start.15) | collective-permute-done | bytes 2080 | tf_op jit(solution)/shard_map/ppermute | solution.py:42
  81.1 5.4 %shard_map.54 = (f32[2,2,4,4,512]{4,3,2,1,0:T(4,128)S(1)}, f32[2,2,4,4,512]{4,3,2,1,0:T(4,128)S(1)}) custom-call(s32[3]{0:T(128)S(1)} %copy-done.1, bf16[4,2,8,4096]{3,2,1,0:T(8,128)(2,1)S(1)} %bitcast_dynamic-update-slice_fusion.refs_0_, bf16[4,2,8,4096]{3,2,1,0:T(8,128)(2,1)S(1)} %collective-permute-done.11.refs_1_, ...), custom_call_target="tpu_custom_call" | custom-call | flops 1610612736 | bytes 14680064 | tf_op jit(solution)/shard_map/pallas_call | solution.py:268
  86.5 5.8 %collective-permute-start.16 = (f32[2,2,4,4,512]{4,3,2,1,0:T(4,128)S(1)}, f32[2,2,4,4,512]{4,3,2,1,0:T(4,128)S(1)}, u32[]{:S(2)}, u32[]{:S(2)}) collective-permute-start(f32[2,2,4,4,512]{4,3,2,1,0:T(4,128)S(1)} %get-tuple-element.93), channel_id=1, source_target_pairs={{0,64},{64,0},{1,65},{65,1},{2,66},{66,2},{3,67},{67,3},{4,68},{68... | collective-permute-start | bytes 393224 | tf_op jit(solution)/shard_map/ppermute | solution.py:42
  92.3 1.0 %collective-permute-done.16 = f32[2,2,4,4,512]{4,3,2,1,0:T(4,128)S(1)} collective-permute-done((f32[2,2,4,4,512]{4,3,2,1,0:T(4,128)S(1)}, f32[2,2,4,4,512]{4,3,2,1,0:T(4,128)S(1)}, u32[]{:S(2)}, u32[]{:S(2)}) %collective-permute-start.16) | collective-permute-done | bytes 131104 | tf_op jit(solution)/shard_map/ppermute | solution.py:42
  93.9 2.7 %collective-permute-done.17 = f32[2,4,4,512]{3,2,1,0:T(4,128)S(1)} collective-permute-done((f32[2,4,4,512]{3,2,1,0:T(4,128)S(1)}, f32[2,4,4,512]{3,2,1,0:T(4,128)S(1)}, u32[]{:S(2)}, u32[]{:S(2)}) %collective-permute-start.17) | collective-permute-done | bytes 65568 | tf_op jit(solution)/shard_map/ppermute | solution.py:42
  (57 shorter events, 6.9 us)
Async XLA Ops:
  0.0 9.1 %copy-start.7 = (s32[2]{0:T(128)S(1)}, s32[2]{0:T(128)}, u32[]{:S(2)}) copy-start(s32[2]{0:T(128)} %param.6) | copy-start | bytes 28
  3.9 15.4 %collective-permute-start = (bf16[32,2,4096]{2,1,0:T(2,128)(2,1)}, bf16[32,2,4096]{2,1,0:T(2,128)(2,1)S(1)}, u32[]{:S(2)}, u32[]{:S(2)}) collective-permute-start(bf16[32,2,4096]{2,1,0:T(2,128)(2,1)} %get-tuple-element.50), channel_id=1, source_target_pairs={{0,16},{16,32},{32,48},{48,0},{1,17},{17,33},{33,49},{49,1},{2,18}... | collective-permute-start | bytes 1572872 | tf_op jit(solution)/shard_map/ppermute | solution.py:38
  6.0 13.3 %collective-permute-start.1 = (bf16[32,2,4096]{2,1,0:T(2,128)(2,1)}, bf16[32,2,4096]{2,1,0:T(2,128)(2,1)S(1)}, u32[]{:S(2)}, u32[]{:S(2)}) collective-permute-start(bf16[32,2,4096]{2,1,0:T(2,128)(2,1)} %get-tuple-element.51), channel_id=1, source_target_pairs={{0,48},{16,0},{32,16},{48,32},{1,49},{17,1},{33,17},{49,33},{2,50}... | collective-permute-start | bytes 1572872 | tf_op jit(solution)/shard_map/ppermute | solution.py:38
  7.3 16.9 %collective-permute-start.2 = (bf16[32,2,4096]{2,1,0:T(2,128)(2,1)}, bf16[32,2,4096]{2,1,0:T(2,128)(2,1)S(1)}, u32[]{:S(2)}, u32[]{:S(2)}) collective-permute-start(bf16[32,2,4096]{2,1,0:T(2,128)(2,1)} %get-tuple-element.52), channel_id=1, source_target_pairs={{0,2},{2,4},{4,6},{6,8},{8,10},{10,12},{12,14},{14,0},{1,3},{3,5},... | collective-permute-start | bytes 1572872 | tf_op jit(solution)/shard_map/ppermute | solution.py:38
  11.7 12.6 %copy-start.2 = (bf16[32,2,4096]{2,1,0:T(2,128)(2,1)S(1)}, bf16[32,2,4096]{2,1,0:T(2,128)(2,1)}, u32[]{:S(2)}) copy-start(bf16[32,2,4096]{2,1,0:T(2,128)(2,1)} %shard_map.47) | copy-start | bytes 1572868
  25.0 12.6 %collective-permute-start.3 = (bf16[2,4,2,4096]{3,2,1,0:T(2,128)(2,1)S(1)}, bf16[2,4,2,4096]{3,2,1,0:T(2,128)(2,1)S(1)}, u32[]{:S(2)}, u32[]{:S(2)}) collective-permute-start(bf16[2,4,2,4096]{3,2,1,0:T(2,128)(2,1)S(1)} %get-tuple-element.104), channel_id=1, source_target_pairs={{0,34},{2,36},{4,38},{6,40},{8,42},{10,44},{12,46},{14,32},{16,50}... | collective-permute-start | bytes 393224 | tf_op jit(solution)/shard_map/ppermute | solution.py:38
  25.1 12.5 %collective-permute-start.4 = (bf16[2,4,2,4096]{3,2,1,0:T(2,128)(2,1)S(1)}, bf16[2,4,2,4096]{3,2,1,0:T(2,128)(2,1)S(1)}, u32[]{:S(2)}, u32[]{:S(2)}) collective-permute-start(bf16[2,4,2,4096]{3,2,1,0:T(2,128)(2,1)S(1)} %get-tuple-element.103), channel_id=1, source_target_pairs={{0,4},{2,6},{4,8},{6,10},{8,12},{10,14},{12,0},{14,2},{1,5},{3,7},... | collective-permute-start | bytes 393224 | tf_op jit(solution)/shard_map/ppermute | solution.py:38
  27.3 10.3 %collective-permute-start.5 = (bf16[2,4,2,4096]{3,2,1,0:T(2,128)(2,1)S(1)}, bf16[2,4,2,4096]{3,2,1,0:T(2,128)(2,1)S(1)}, u32[]{:S(2)}, u32[]{:S(2)}) collective-permute-start(bf16[2,4,2,4096]{3,2,1,0:T(2,128)(2,1)S(1)} %get-tuple-element.102), channel_id=1, source_target_pairs={{0,46},{2,32},{4,34},{6,36},{8,38},{10,40},{12,42},{14,44},{16,62}... | collective-permute-start | bytes 393224 | tf_op jit(solution)/shard_map/ppermute | solution.py:38
  38.1 11.4 %collective-permute-start.6 = (bf16[2,4,2,4096]{3,2,1,0:T(2,128)(2,1)S(1)}, bf16[2,4,2,4096]{3,2,1,0:T(2,128)(2,1)S(1)}, u32[]{:S(2)}, u32[]{:S(2)}) collective-permute-start(bf16[2,4,2,4096]{3,2,1,0:T(2,128)(2,1)S(1)} %broadcast_select_fusion.2), channel_id=1, source_target_pairs={{0,8},{2,10},{4,12},{6,14},{8,0},{10,2},{12,4},{14,6},{1,9},{3,11}... | collective-permute-start | bytes 393224 | tf_op jit(solution)/shard_map/ppermute | solution.py:38
  49.8 7.9 %collective-permute-start.7 = (bf16[2,4,2,4096]{3,2,1,0:T(2,128)(2,1)S(1)}, bf16[2,4,2,4096]{3,2,1,0:T(2,128)(2,1)S(1)}, u32[]{:S(2)}, u32[]{:S(2)}) collective-permute-start(bf16[2,4,2,4096]{3,2,1,0:T(2,128)(2,1)S(1)} %broadcast_select_fusion.3.rows_ref), channel_id=1, source_target_pairs={{0,1},{1,0},{2,3},{3,2},{4,5},{5,4},{6,7},{7,6},{8,9},{9,8},{10,11... | collective-permute-start | bytes 393224 | tf_op jit(solution)/shard_map/ppermute | solution.py:38
  58.6 11.0 %collective-permute-start.8 = (bf16[2,8,4096]{2,1,0:T(8,128)(2,1)S(1)}, bf16[2,8,4096]{2,1,0:T(8,128)(2,1)S(1)}, u32[]{:S(2)}, u32[]{:S(2)}) collective-permute-start(bf16[2,8,4096]{2,1,0:T(8,128)(2,1)S(1)} %get-tuple-element.74), channel_id=1, source_target_pairs={{0,34},{2,36},{4,38},{6,40},{8,42},{10,44},{12,46},{14,32},{16,50}... | collective-permute-start | bytes 393224 | tf_op jit(solution)/shard_map/ppermute | solution.py:38
  59.6 10.1 %collective-permute-start.9 = (bf16[2,8,4096]{2,1,0:T(8,128)(2,1)S(1)}, bf16[2,8,4096]{2,1,0:T(8,128)(2,1)S(1)}, u32[]{:S(2)}, u32[]{:S(2)}) collective-permute-start(bf16[2,8,4096]{2,1,0:T(8,128)(2,1)S(1)} %get-tuple-element.74), channel_id=1, source_target_pairs={{0,4},{2,6},{4,8},{6,10},{8,12},{10,14},{12,0},{14,2},{1,5},{3,7},... | collective-permute-start | bytes 393224 | tf_op jit(solution)/shard_map/ppermute | solution.py:38
  59.8 9.8 %collective-permute-start.10 = (bf16[2,8,4096]{2,1,0:T(8,128)(2,1)S(1)}, bf16[2,8,4096]{2,1,0:T(8,128)(2,1)S(1)}, u32[]{:S(2)}, u32[]{:S(2)}) collective-permute-start(bf16[2,8,4096]{2,1,0:T(8,128)(2,1)S(1)} %get-tuple-element.74), channel_id=1, source_target_pairs={{0,46},{2,32},{4,34},{6,36},{8,38},{10,40},{12,42},{14,44},{16,62}... | collective-permute-start | bytes 393224 | tf_op jit(solution)/shard_map/ppermute | solution.py:38
  64.5 7.0 %copy-start.5 = (f32[8,512]{1,0:T(8,128)S(1)}, f32[8,512]{1,0:T(8,128)}, u32[]{:S(2)}) copy-start(f32[8,512]{1,0:T(8,128)} %get-tuple-element.83) | copy-start | bytes 49156
  64.5 7.0 %copy-start.6 = (f32[8,512]{1,0:T(8,128)S(1)}, f32[8,512]{1,0:T(8,128)}, u32[]{:S(2)}) copy-start(f32[8,512]{1,0:T(8,128)} %get-tuple-element.84) | copy-start | bytes 49156
  64.5 16.6 %copy-start = (bf16[2,16,256,256]{3,2,1,0:T(8,128)(2,1)S(1)}, bf16[2,16,256,256]{3,2,1,0:T(8,128)(2,1)}, u32[]{:S(2)}) copy-start(bf16[2,16,256,256]{3,2,1,0:T(8,128)(2,1)} %refs_4_.1) | copy-start | bytes 12582916
  64.5 16.6 %copy-start.1 = (s32[3]{0:T(128)S(1)}, s32[3]{0:T(128)}, u32[]{:S(2)}) copy-start(s32[3]{0:T(128)} %pad_add_fusion.place) | copy-start | bytes 40
  69.7 11.4 %collective-permute-start.11 = (bf16[4,2,8,4096]{3,2,1,0:T(8,128)(2,1)S(1)}, bf16[4,2,8,4096]{3,2,1,0:T(8,128)(2,1)S(1)}, u32[]{:S(2)}, u32[]{:S(2)}) collective-permute-start(bf16[4,2,8,4096]{3,2,1,0:T(8,128)(2,1)S(1)} %bitcast_dynamic-update-slice_fusion.refs_0_), channel_id=1, source_target_pairs={{0,48},{16,0},{32,16},{48,32},{1,49},{17,1},{33,17},{49,33},{2,50}... | collective-permute-start | bytes 1572872 | tf_op jit(solution)/shard_map/ppermute | solution.py:38
  71.3 9.8 %collective-permute-start.12 = (bf16[4,2,8,4096]{3,2,1,0:T(8,128)(2,1)S(1)}, bf16[4,2,8,4096]{3,2,1,0:T(8,128)(2,1)S(1)}, u32[]{:S(2)}, u32[]{:S(2)}) collective-permute-start(bf16[4,2,8,4096]{3,2,1,0:T(8,128)(2,1)S(1)} %bitcast_dynamic-update-slice_fusion.refs_0_), channel_id=1, source_target_pairs={{0,2},{2,4},{4,6},{6,8},{8,10},{10,12},{12,14},{14,0},{1,3},{3,5},... | collective-permute-start | bytes 1572872 | tf_op jit(solution)/shard_map/ppermute | solution.py:38
  71.3 9.8 %collective-permute-start.13 = (bf16[4,2,8,4096]{3,2,1,0:T(8,128)(2,1)S(1)}, bf16[4,2,8,4096]{3,2,1,0:T(8,128)(2,1)S(1)}, u32[]{:S(2)}, u32[]{:S(2)}) collective-permute-start(bf16[4,2,8,4096]{3,2,1,0:T(8,128)(2,1)S(1)} %bitcast_dynamic-update-slice_fusion.refs_0_), channel_id=1, source_target_pairs={{0,16},{16,32},{32,48},{48,0},{1,17},{17,33},{33,49},{49,1},{2,18}... | collective-permute-start | bytes 1572872 | tf_op jit(solution)/shard_map/ppermute | solution.py:38
  72.2 6.1 %collective-permute-start.14 = (f32[512]{0:T(512)S(1)}, f32[512]{0:T(512)S(1)}, u32[]{:S(2)}, u32[]{:S(2)}) collective-permute-start(f32[512]{0:T(512)S(1)} %add_reduce_fusion), channel_id=1, source_target_pairs={{0,64},{64,0},{1,65},{65,1},{2,66},{66,2},{3,67},{67,3},{4,68},{68... | collective-permute-start | bytes 6152 | tf_op jit(solution)/shard_map/ppermute | solution.py:42
  78.4 2.7 %collective-permute-start.15 = (f32[512]{0:T(512)S(1)}, f32[512]{0:T(512)S(1)}, u32[]{:S(2)}, u32[]{:S(2)}) collective-permute-start(f32[512]{0:T(512)S(1)} %add.161), channel_id=1, source_target_pairs={{0,128},{128,0},{1,129},{129,1},{2,130},{130,2},{3,131},{131,3},{4... | collective-permute-start | bytes 6152 | tf_op jit(solution)/shard_map/ppermute | solution.py:42
  86.5 6.8 %collective-permute-start.16 = (f32[2,2,4,4,512]{4,3,2,1,0:T(4,128)S(1)}, f32[2,2,4,4,512]{4,3,2,1,0:T(4,128)S(1)}, u32[]{:S(2)}, u32[]{:S(2)}) collective-permute-start(f32[2,2,4,4,512]{4,3,2,1,0:T(4,128)S(1)} %get-tuple-element.93), channel_id=1, source_target_pairs={{0,64},{64,0},{1,65},{65,1},{2,66},{66,2},{3,67},{67,3},{4,68},{68... | collective-permute-start | bytes 393224 | tf_op jit(solution)/shard_map/ppermute | solution.py:42
  93.4 3.2 %collective-permute-start.17 = (f32[2,4,4,512]{3,2,1,0:T(4,128)S(1)}, f32[2,4,4,512]{3,2,1,0:T(4,128)S(1)}, u32[]{:S(2)}, u32[]{:S(2)}) collective-permute-start(f32[2,4,4,512]{3,2,1,0:T(4,128)S(1)} %dynamic-slice_bitcast_fusion), channel_id=1, source_target_pairs={{0,128},{128,0},{1,129},{129,1},{2,130},{130,2},{3,131},{131,3},{4... | collective-permute-start | bytes 196616 | tf_op jit(solution)/shard_map/ppermute | solution.py:42
  (2 other events, 14.0 us)

commit v2 on v1

--- a/solution.py
+++ b/solution.py
@@ -16,7 +16,8 @@
 SIZES = dict(x=NX, z=NZ, yhi=NY)
 NT = (((1,), (1,)), ((), ()))
 STEPS = (1, 2, -1)
-SMALL_LIMIT, SCORE_LIMIT, LARGE_LIMIT = 8 * 2**20, 40 * 2**20, 57 * 2**20
+SMALL_LIMIT, SCORE_LIMIT, LARGE_LIMIT = 8 * 2**20, 26 * 2**20, 57 * 2**20
+PICK_LIMIT, STAGE_LIMIT = 52 * 2**20, 24 * 2**20
 IN_VMEM = pl.BlockSpec(memory_space=pltpu.VMEM)
 IN_SMEM = pl.BlockSpec(memory_space=pltpu.SMEM)
 
@@ -42,34 +43,43 @@
     return lax.ppermute(value, axis, [(0, 1), (1, 0)])
 
 
-def pick_kernel(turns, place, ids, gradients, *rest):
+def colour_here():
+    return lax.rem(lax.axis_index("x") + 2 * lax.axis_index("z"), 4)
+
+
+def pick_kernel(wanted, ids, gradients, *rest):
     outs, sem = rest[:-1], rest[-1]
     rounds, queries = ids.shape
     quarter = queries // 4
-    for turn, out in zip(turns, outs):
-        first = lax.rem(place[0] + turn, 4) * quarter
+    colour = colour_here()
+    for (turn, skip), out in zip(wanted, outs):
+        count = out.shape[0] // rounds
+        first = lax.rem(colour + turn, 4) * quarter + skip * count
         for which in range(rounds):
-            for row in range(quarter):
+            for row in range(count):
                 pltpu.make_async_copy(
-                    gradients.at[ids[which, first + row]], out.at[which * quarter + row], sem
+                    gradients.at[ids[which, first + row]], out.at[which * count + row], sem
                 ).start()
     for out in outs:
         pltpu.make_async_copy(gradients.at[pl.ds(0, out.shape[0])], out, sem).wait()
 
 
-def pick_rows(gradients, query_ids, place, turns):
-    count = query_ids.size // 4
-    out = jax.ShapeDtypeStruct((count,) + gradients.shape[1:], gradients.dtype)
-    moved = 2 * len(turns) * out.size * 2
-    return pl.pallas_call(
-        functools.partial(pick_kernel, turns),
-        out_shape=[out for _ in turns],
-        in_specs=[IN_SMEM, IN_SMEM, pl.BlockSpec(memory_space=pl.ANY)],
-        out_specs=[IN_VMEM for _ in turns],
+def pick_rows(gradients, query_ids, wanted, limit=PICK_LIMIT):
+    outs = [
+        jax.ShapeDtypeStruct((query_ids.size // 4 // parts,) + gradients.shape[1:], gradients.dtype)
+        for _, _, parts in wanted
+    ]
+    return pl.pallas_call(
+        functools.partial(pick_kernel, tuple(entry[:2] for entry in wanted)),
+        out_shape=outs,
+        in_specs=[IN_SMEM, pl.BlockSpec(memory_space=pl.ANY)],
+        out_specs=[IN_VMEM for _ in wanted],
         scratch_shapes=[pltpu.SemaphoreType.DMA],
-        compiler_params=pltpu.CompilerParams(vmem_limit_bytes=LARGE_LIMIT),
-        cost_estimate=pl.CostEstimate(flops=0, bytes_accessed=moved, transcendentals=0),
-    )(place, query_ids, gradients)
+        compiler_params=pltpu.CompilerParams(vmem_limit_bytes=limit),
+        cost_estimate=pl.CostEstimate(
+            flops=0, bytes_accessed=4 * sum(out.size for out in outs), transcendentals=0
+        ),
+    )(query_ids, gradients)
 
 
 def split_kernel(same, rows_ref, other_ref, piece_ref, whole_ref):
@@ -106,7 +116,7 @@
     return lax.dynamic_index_in_dim(parts, at, 1, keepdims=False)
 
 
-def broadcast(gradients, owners, query_ids, place, beside):
+def broadcast(gradients, owners, query_ids, beside):
     rounds, queries = query_ids.shape
     tail = gradients.shape[1:]
     part = queries // 16
@@ -115,17 +125,21 @@
     own_x, own_z, own_y = owners // (NZ * NY), owners // NY % NZ, owners % NY
     far_x, far_z, same_y = (x - own_x) % NX, (z - own_z) % NZ, y == own_y
 
-    to_right, to_left, to_up = pick_rows(gradients, query_ids, place, (1, 3, 2))
-    given = shift(to_right, dx=1), shift(to_left, dx=-1), shift(to_up, dz=1)
-    rows, _ = lax.optimization_barrier((gradients, to_up))
-    (own,) = pick_rows(rows, query_ids, place, (0,))
+    to_right, to_left = pick_rows(gradients, query_ids, ((1, 0, 1), (3, 0, 1)))
+    given = shift(to_right, dx=1), shift(to_left, dx=-1)
+    rows, _ = lax.optimization_barrier((gradients, to_left))
+    to_up, to_down, own = pick_rows(rows, query_ids, ((2, 0, 2), (2, 1, 2), (0, 0, 1)), LARGE_LIMIT)
+    given += shift(to_up, dz=1), shift(to_down, dz=-1)
     given = beside(given, own, 2)
-    own, from_left, from_right, from_below = (
-        rows.reshape(rounds, 4, part, *tail) for rows in (own,) + tuple(given)
+    own, from_left, from_right, from_below, from_above = (
+        rows.reshape(rounds, -1, part, *tail) for rows in (own,) + tuple(given)
     )
 
     def held(at):
-        out = jnp.where(per_round((far_x == 0) & (far_z == 1)), piece(from_below, at), piece(own, at))
+        low = at < 2
+        out = piece(own, at)
+        out = jnp.where(per_round((far_x == 0) & (far_z == 1) & low), piece(from_below, at % 2), out)
+        out = jnp.where(per_round((far_x == 0) & (far_z == 7) & ~low), piece(from_above, at % 2), out)
         out = jnp.where(per_round((far_x == 1) & (far_z == 0)), piece(from_left, at), out)
         return jnp.where(per_round((far_x == 3) & (far_z == 0)), piece(from_right, at), out)
 
@@ -134,7 +148,7 @@
     got = [shift(rows, dx=(-2 * by) % 4, dz=by) for by, rows in zip(STEPS, pieces)]
     got = beside(tuple(got), pieces[0], 2)
     own_colour = (own_x + 2 * own_z) % 4
-    source_z = own_z + jnp.where((colour - own_colour) % 4 == 2, 1, 0)
+    source_z = own_z + jnp.where((colour - own_colour) % 4 == 2, jnp.where(mine < 2, 1, -1), 0)
     away = (z - source_z) % NZ
     part_rows = held(mine)
     for by, rows in zip(STEPS, got):
@@ -211,7 +225,25 @@
     )(*operands)
 
 
-def score_kernel(place, *refs):
+def stage_kernel(white, out, sem):
+    copy = pltpu.make_async_copy(white, out, sem)
+    copy.start()
+    copy.wait()
+
+
+def stage(white):
+    return pl.pallas_call(
+        stage_kernel,
+        out_shape=jax.ShapeDtypeStruct(white.shape, white.dtype),
+        in_specs=[pl.BlockSpec(memory_space=pl.ANY)],
+        out_specs=IN_VMEM,
+        scratch_shapes=[pltpu.SemaphoreType.DMA],
+        compiler_params=pltpu.CompilerParams(vmem_limit_bytes=STAGE_LIMIT),
+        cost_estimate=pl.CostEstimate(flops=0, bytes_accessed=4 * white.size, transcendentals=0),
+    )(white)
+
+
+def score_kernel(*refs):
     groups, (w_ref, white_ref, keep_ref, send_ref, total_ref) = refs[:4], refs[4:]
     layers, nb, block = w_ref.shape[:3]
     step = pl.program_id(0)
@@ -238,7 +270,8 @@
 
     @pl.when(step == pl.num_programs(0) - 1)
     def _():
-        colour, core, z = place[0], place[1], place[2]
+        colour, z = colour_here(), lax.axis_index("z")
+        core, ylo = lax.axis_index("core"), lax.axis_index("ylo")
         rounds, part = keep_ref.shape[0], keep_ref.shape[3]
         for turn in range(4):
             at = lax.rem(colour + turn, 4)
@@ -251,10 +284,10 @@
                         for which in range(rounds):
                             start = ((turn * 4 + slot) * rounds + which) * part
                             to = lax.rem(from_z - back, 4)
-                            ref[which, lax.rem(at, 2), to] = total_ref[start : start + part]
-
-
-def score(groups, whitener, white, place, rounds, nb=8):
+                            ref[lax.rem(which + ylo, 2), lax.rem(at, 2), to] = total_ref[start : start + part]
+
+
+def score(groups, whitener, white, rounds, nb=8):
     layers, nblock, block, examples = white.shape
     part = groups[0].shape[2] // rounds
     count = 16 * rounds * part
@@ -269,8 +302,7 @@
         score_kernel,
         grid=(nblock // nb,),
         out_shape=[out, out],
-        in_specs=[IN_SMEM]
-        + [pl.BlockSpec(g.shape[:3] + (nb * block,), lambda i: (0, 0, 0, i)) for g in groups]
+        in_specs=[pl.BlockSpec(g.shape[:3] + (nb * block,), lambda i: (0, 0, 0, i)) for g in groups]
         + [
             pl.BlockSpec((layers, nb, block, block), lambda i: (0, i, 0, 0)),
             pl.BlockSpec((layers, nb, block, examples), lambda i: (0, i, 0, 0)),
@@ -279,7 +311,7 @@
         scratch_shapes=[pltpu.VMEM((count, examples), jnp.float32)],
         compiler_params=pltpu.CompilerParams(vmem_limit_bytes=SCORE_LIMIT),
         cost_estimate=cost,
-    )(place, *groups, whitener, white)
+    )(*groups, whitener, white)
 
 
 UNITS = 8
@@ -289,9 +321,6 @@
     count = gradients.shape[0]
     rounds = owners.shape[0]
     unit = whitener.shape[1] // UNITS
-    x, z = lax.axis_index("x"), lax.axis_index("z")
-    core, ylo = lax.axis_index("core"), lax.axis_index("ylo")
-    place = jnp.stack([(x + 2 * z) % 4, core, z]).astype(jnp.int32)
     norms, done = [], dict(units=0, white=None)
 
     def beside(values, sent, units):
@@ -304,16 +333,16 @@
         done["units"] += units
         return values
 
-    groups = broadcast(gradients, owners, query_ids, place, beside)
+    groups = broadcast(gradients, owners, query_ids, beside)
     norm, _ = lax.optimization_barrier((jnp.sum(sum(norms), axis=0), groups[0]))
-    norm = norm + swap(norm, "core")
+    white, _ = lax.optimization_barrier((done["white"], norm))
+    norm, white = lax.optimization_barrier((norm + swap(norm, "core"), stage(white)))
     norm = norm + swap(norm, "ylo")
     groups, norm = lax.optimization_barrier((groups, norm))
 
-    keep, send = score(groups, whitener, done["white"], place, rounds)
-    half = keep + swap(send, "core")
-    mine = lax.dynamic_index_in_dim(half, ylo, 0, keepdims=False)
-    mine = mine + swap(lax.dynamic_index_in_dim(half, 1 - ylo, 0, keepdims=False), "ylo")
+    keep, send = score(groups, whitener, white, rounds)
+    got = swap(send, "core")
+    mine = keep[0] + got[0] + swap(keep[1] + got[1], "ylo")
     return mine.reshape(-1, count) / jnp.sqrt(norm + 1e-06)[None, :]
 
 

time: 97.7 us -> 94.1 us (0.963)
  waiting for transfers between devices: 11.9 us -> 6.07 us
  local copies, waits for them, and re-layouts: 0.11 us -> 4.14 us
  Pallas kernels: 44.4 us -> 42.3 us
    ppermute x14 -> x15, waiting for transfers between devices: 5.02 us -> 0.04 us  [shift(): return lax.ppermute(value, names if len(names) > 1 else names[0], pairs)]
    unnamed x16 -> x18, local copies, waits for them, and re-layouts: 0.03 us -> 4.09 us
    ppermute x14 -> x15, starting transfers between devices: 25 us -> 28.9 us  [shift(): return lax.ppermute(value, names if len(names) > 1 else names[0], pairs)]
    ppermute x4, starting transfers between devices: 12 us -> 8.6 us  [swap(): return lax.ppermute(value, axis, [(0, 1), (1, 0)])]
    pallas_call x1, Pallas kernels: 5.39 us -> 4.03 us  [score(): pl.pallas_call(score_kernel, grid=(nblock // nb,), out_shape=[out, out],...]
    pallas_call x2 -> x3, Pallas kernels: 5.75 us -> 5.21 us  [the longest x2 4.65 us: pick_rows(): pl.pallas_call(functools.partial(pick_kernel, tuple((entry[:2] for entry...]
  transfers between devices with their start and end apart: 18 -> 19, of which waited for: 5 -> 3; matrix products, arithmetic and copies ran while one was open for 1% -> 1% of each run, Pallas kernels for 36% -> 38%
where the time goes in v2:
time: 94.1 us; the launch traced here: 93.7 us
  Pallas kernels  42.3 us (45%)
  starting transfers between devices  37.5 us (40%)
  waiting for transfers between devices  6.07 us (6%)
  local copies, waits for them, and re-layouts  4.14 us (4%)
  other arithmetic  3.28 us (3%)
    pallas_call x5, Pallas kernels, whiten_blocks(): pl.pallas_call(whiten_kernel, grid=(count // nb,), out_shape=[jax.ShapeDt...  32.2 us
    ppermute x15, starting transfers between devices, shift(): return lax.ppermute(value, names if len(names) > 1 else names[0], pairs)  28.9 us
    ppermute x4, starting transfers between devices, swap(): return lax.ppermute(value, axis, [(0, 1), (1, 0)])  8.6 us
    ppermute x4, waiting for transfers between devices, swap(): return lax.ppermute(value, axis, [(0, 1), (1, 0)])  6.04 us
    pallas_call x2, Pallas kernels, pick_rows(): pl.pallas_call(functools.partial(pick_kernel, tuple((entry[:2] for entry...  4.65 us
    unnamed x18, local copies, waits for them, and re-layouts  4.09 us
    pallas_call x1, Pallas kernels, score(): pl.pallas_call(score_kernel, grid=(nblock // nb,), out_shape=[out, out],...  4.03 us
  transfers between devices with their start and end apart: 19, of which 3 were waited for; matrix products, arithmetic and copies ran while one was open for 1% of the time, Pallas kernels for 38%

profile of v2, /device:TPU:1, one launch (start us, length us, event | category | flops | bytes accessed | tf_op | source)
XLA Modules:
  0.0 93.7 jit_solution(6666944209212392393)
XLA Ops:
  0.7 1.7 %shard_map.46 = (bf16[32,2,4096]{2,1,0:T(2,128)(2,1)S(1)}, bf16[32,2,4096]{2,1,0:T(2,128)(2,1)S(1)}) custom-call(s32[2,64]{1,0:T(2,128)S(1)} %copy-done.2, bf16[512,2,4096]{2,1,0:T(2,128)(2,1)} %x_ref.4), custom_call_target="tpu_custom_call" | custom-call | bytes 2097152 | tf_op jit(solution)/shard_map/pallas_call | solution.py:72
  2.4 2.1 %collective-permute-start = (bf16[32,2,4096]{2,1,0:T(2,128)(2,1)S(1)}, bf16[32,2,4096]{2,1,0:T(2,128)(2,1)S(1)}, u32[]{:S(2)}, u32[]{:S(2)}) collective-permute-start(bf16[32,2,4096]{2,1,0:T(2,128)(2,1)S(1)} %get-tuple-element.56), channel_id=1, source_target_pairs={{0,16},{16,32},{32,48},{48,0},{1,17},{17,33},{33,49},{49,1},{2,18}... | collective-permute-start | bytes 1572872 | tf_op jit(solution)/shard_map/ppermute | solution.py:39
  4.6 1.4 %collective-permute-start.1 = (bf16[32,2,4096]{2,1,0:T(2,128)(2,1)S(1)}, bf16[32,2,4096]{2,1,0:T(2,128)(2,1)S(1)}, u32[]{:S(2)}, u32[]{:S(2)}) collective-permute-start(bf16[32,2,4096]{2,1,0:T(2,128)(2,1)S(1)} %get-tuple-element.57), channel_id=1, source_target_pairs={{0,48},{16,0},{32,16},{48,32},{1,49},{17,1},{33,17},{49,33},{2,50}... | collective-permute-start | bytes 1572872 | tf_op jit(solution)/shard_map/ppermute | solution.py:39
  5.9 2.9 %shard_map.47 = (bf16[16,2,4096]{2,1,0:T(2,128)(2,1)}, bf16[16,2,4096]{2,1,0:T(2,128)(2,1)}, bf16[32,2,4096]{2,1,0:T(2,128)(2,1)}) custom-call(s32[2,64]{1,0:T(2,128)} %ids.3, bf16[512,2,4096]{2,1,0:T(2,128)(2,1)} %x_ref.4), custom_call_target="tpu_custom_call" | custom-call | bytes 2097152 | tf_op jit(solution)/shard_map/pallas_call | solution.py:72
  8.8 1.8 %collective-permute-start.2 = (bf16[16,2,4096]{2,1,0:T(2,128)(2,1)}, bf16[16,2,4096]{2,1,0:T(2,128)(2,1)S(1)}, u32[]{:S(2)}, u32[]{:S(2)}) collective-permute-start(bf16[16,2,4096]{2,1,0:T(2,128)(2,1)} %get-tuple-element.59), channel_id=1, source_target_pairs={{0,2},{2,4},{4,6},{6,8},{8,10},{10,12},{12,14},{14,0},{1,3},{3,5},... | collective-permute-start | bytes 786440 | tf_op jit(solution)/shard_map/ppermute | solution.py:39
  10.7 4.0 %collective-permute-start.3 = (bf16[16,2,4096]{2,1,0:T(2,128)(2,1)}, bf16[16,2,4096]{2,1,0:T(2,128)(2,1)S(1)}, u32[]{:S(2)}, u32[]{:S(2)}) collective-permute-start(bf16[16,2,4096]{2,1,0:T(2,128)(2,1)} %get-tuple-element.60), channel_id=1, source_target_pairs={{0,14},{2,0},{4,2},{6,4},{8,6},{10,8},{12,10},{14,12},{1,15},{3,1}... | collective-permute-start | bytes 786440 | tf_op jit(solution)/shard_map/ppermute | solution.py:39
  14.9 7.4 %shard_map.48 = (bf16[2,16,256,512]{3,2,1,0:T(8,128)(2,1)}, f32[8,512]{1,0:T(8,128)}) custom-call(bf16[512,2,4096]{2,1,0:T(2,128)(2,1)} %x_ref.4, bf16[2,16,256,256]{3,2,1,0:T(8,128)(2,1)} %refs_4_.1), custom_call_target="tpu_custom_call" | custom-call | flops 536870912 | bytes 15728640 | tf_op jit(solution)/shard_map/pallas_call | solution.py:206
  23.4 3.1 %collective-permute-start.5 = (bf16[2,4,2,4096]{3,2,1,0:T(2,128)(2,1)S(1)}, bf16[2,4,2,4096]{3,2,1,0:T(2,128)(2,1)S(1)}, u32[]{:S(2)}, u32[]{:S(2)}) collective-permute-start(bf16[2,4,2,4096]{3,2,1,0:T(2,128)(2,1)S(1)} %get-tuple-element.118), channel_id=1, source_target_pairs={{0,4},{2,6},{4,8},{6,10},{8,12},{10,14},{12,0},{14,2},{1,5},{3,7},... | collective-permute-start | bytes 393224 | tf_op jit(solution)/shard_map/ppermute | solution.py:39
  26.5 2.0 %collective-permute-start.6 = (bf16[2,4,2,4096]{3,2,1,0:T(2,128)(2,1)S(1)}, bf16[2,4,2,4096]{3,2,1,0:T(2,128)(2,1)S(1)}, u32[]{:S(2)}, u32[]{:S(2)}) collective-permute-start(bf16[2,4,2,4096]{3,2,1,0:T(2,128)(2,1)S(1)} %get-tuple-element.117), channel_id=1, source_target_pairs={{0,46},{2,32},{4,34},{6,36},{8,38},{10,40},{12,42},{14,44},{16,62}... | collective-permute-start | bytes 393224 | tf_op jit(solution)/shard_map/ppermute | solution.py:39
  28.5 7.4 %shard_map.49 = (bf16[2,16,256,512]{3,2,1,0:T(8,128)(2,1)}, f32[8,512]{1,0:T(8,128)}) custom-call(bf16[512,2,4096]{2,1,0:T(2,128)(2,1)} %x_ref.4, bf16[2,16,256,256]{3,2,1,0:T(8,128)(2,1)} %refs_4_.1, bf16[2,16,256,512]{3,2,1,0:T(8,128)(2,1)} %get-tuple-element.69.refs_0_), custom_call_target="tpu_custom_call", output_to_operand_aliasing={{0}: (2, {})} | custom-call | flops 536870912 | bytes 15728640 | tf_op jit(solution)/shard_map/pallas_call | solution.py:206
  36.5 4.0 %collective-permute-start.7 = (bf16[2,4,2,4096]{3,2,1,0:T(2,128)(2,1)S(1)}, bf16[2,4,2,4096]{3,2,1,0:T(2,128)(2,1)S(1)}, u32[]{:S(2)}, u32[]{:S(2)}) collective-permute-start(bf16[2,4,2,4096]{3,2,1,0:T(2,128)(2,1)S(1)} %broadcast_select_fusion.10), channel_id=1, source_target_pairs={{0,8},{2,10},{4,12},{6,14},{8,0},{10,2},{12,4},{14,6},{1,9},{3,11}... | collective-permute-start | bytes 393224 | tf_op jit(solution)/shard_map/ppermute | solution.py:39
  40.5 7.4 %shard_map.50 = (bf16[2,16,256,512]{3,2,1,0:T(8,128)(2,1)}, f32[8,512]{1,0:T(8,128)}) custom-call(bf16[512,2,4096]{2,1,0:T(2,128)(2,1)} %x_ref.4, bf16[2,16,256,256]{3,2,1,0:T(8,128)(2,1)} %refs_4_.1, bf16[2,16,256,512]{3,2,1,0:T(8,128)(2,1)} %get-tuple-element.75.refs_0_), custom_call_target="tpu_custom_call", output_to_operand_aliasing={{0}: (2, {})} | custom-call | flops 536870912 | bytes 15728640 | tf_op jit(solution)/shard_map/pallas_call | solution.py:206
  48.2 3.0 %collective-permute-start.8 = (bf16[2,4,2,4096]{3,2,1,0:T(2,128)(2,1)S(1)}, bf16[2,4,2,4096]{3,2,1,0:T(2,128)(2,1)S(1)}, u32[]{:S(2)}, u32[]{:S(2)}) collective-permute-start(bf16[2,4,2,4096]{3,2,1,0:T(2,128)(2,1)S(1)} %broadcast_select_fusion.11.rows_ref), channel_id=1, source_target_pairs={{0,1},{1,0},{2,3},{3,2},{4,5},{5,4},{6,7},{7,6},{8,9},{9,8},{10,11... | collective-permute-start | bytes 393224 | tf_op jit(solution)/shard_map/ppermute | solution.py:39
  51.2 4.9 %shard_map.51 = (bf16[2,16,256,512]{3,2,1,0:T(8,128)(2,1)}, f32[8,512]{1,0:T(8,128)}) custom-call(bf16[512,2,4096]{2,1,0:T(2,128)(2,1)} %x_ref.4, bf16[2,16,256,256]{3,2,1,0:T(8,128)(2,1)} %refs_4_.1, bf16[2,16,256,512]{3,2,1,0:T(8,128)(2,1)} %get-tuple-element.79.refs_0_), custom_call_target="tpu_custom_call", output_to_operand_aliasing={{0}: (2, {})} | custom-call | flops 268435456 | bytes 7864320 | tf_op jit(solution)/shard_map/pallas_call | solution.py:206
  57.0 1.9 %collective-permute-start.9 = (bf16[2,8,4096]{2,1,0:T(8,128)(2,1)S(1)}, bf16[2,8,4096]{2,1,0:T(8,128)(2,1)S(1)}, u32[]{:S(2)}, u32[]{:S(2)}) collective-permute-start(bf16[2,8,4096]{2,1,0:T(8,128)(2,1)S(1)} %get-tuple-element.83), channel_id=1, source_target_pairs={{0,34},{2,36},{4,38},{6,40},{8,42},{10,44},{12,46},{14,32},{16,50}... | collective-permute-start | bytes 393224 | tf_op jit(solution)/shard_map/ppermute | solution.py:39
  59.0 3.7 %collective-permute-start.11 = (bf16[2,8,4096]{2,1,0:T(8,128)(2,1)S(1)}, bf16[2,8,4096]{2,1,0:T(8,128)(2,1)S(1)}, u32[]{:S(2)}, u32[]{:S(2)}) collective-permute-start(bf16[2,8,4096]{2,1,0:T(8,128)(2,1)S(1)} %get-tuple-element.83), channel_id=1, source_target_pairs={{0,46},{2,32},{4,34},{6,36},{8,38},{10,40},{12,42},{14,44},{16,62}... | collective-permute-start | bytes 393224 | tf_op jit(solution)/shard_map/ppermute | solution.py:39
  62.7 5.0 %shard_map.53 = (bf16[2,16,256,512]{3,2,1,0:T(8,128)(2,1)}, f32[8,512]{1,0:T(8,128)}) custom-call(bf16[512,2,4096]{2,1,0:T(2,128)(2,1)} %x_ref.4, bf16[2,16,256,256]{3,2,1,0:T(8,128)(2,1)} %refs_4_.1, bf16[2,16,256,512]{3,2,1,0:T(8,128)(2,1)} %get-tuple-element.85.refs_0_), custom_call_target="tpu_custom_call", output_to_operand_aliasing={{0}: (2, {})} | custom-call | flops 268435456 | bytes 7864320 | tf_op jit(solution)/shard_map/pallas_call | solution.py:206
  67.8 1.3 %collective-permute-start.12 = (bf16[4,2,8,4096]{3,2,1,0:T(8,128)(2,1)S(1)}, bf16[4,2,8,4096]{3,2,1,0:T(8,128)(2,1)S(1)}, u32[]{:S(2)}, u32[]{:S(2)}) collective-permute-start(bf16[4,2,8,4096]{3,2,1,0:T(8,128)(2,1)S(1)} %bitcast_dynamic-update-slice_fusion.refs_0_), channel_id=1, source_target_pairs={{0,48},{16,0},{32,16},{48,32},{1,49},{17,1},{33,17},{49,33},{2,50}... | collective-permute-start | bytes 1572872 | tf_op jit(solution)/shard_map/ppermute | solution.py:39
  70.3 5.2 %collective-permute-start.15 = (f32[512]{0:T(512)S(1)}, f32[512]{0:T(512)S(1)}, u32[]{:S(2)}, u32[]{:S(2)}) collective-permute-start(f32[512]{0:T(512)S(1)} %add_reduce_fusion), channel_id=1, source_target_pairs={{0,64},{64,0},{1,65},{65,1},{2,66},{66,2},{3,67},{67,3},{4,68},{68... | collective-permute-start | bytes 6152 | tf_op jit(solution)/shard_map/ppermute | solution.py:43
  75.5 3.4 %copy-done = bf16[2,16,256,512]{3,2,1,0:T(8,128)(2,1)S(1)} copy-done((bf16[2,16,256,512]{3,2,1,0:T(8,128)(2,1)S(1)}, bf16[2,16,256,512]{3,2,1,0:T(8,128)(2,1)}, u32[]{:S(2)}) %copy-start) | copy-done | bytes 8388632
  80.0 2.3 %collective-permute-done.16 = f32[512]{0:T(512)S(1)} collective-permute-done((f32[512]{0:T(512)S(1)}, f32[512]{0:T(512)S(1)}, u32[]{:S(2)}, u32[]{:S(2)}) %collective-permute-start.16) | collective-permute-done | bytes 2080 | tf_op jit(solution)/shard_map/ppermute | solution.py:43
  82.4 4.0 %shard_map.55 = (f32[2,2,4,4,512]{4,3,2,1,0:T(4,128)S(1)}, f32[2,2,4,4,512]{4,3,2,1,0:T(4,128)S(1)}) custom-call(bf16[4,2,8,4096]{3,2,1,0:T(8,128)(2,1)S(1)} %bitcast_dynamic-update-slice_fusion.refs_0_, bf16[4,2,8,4096]{3,2,1,0:T(8,128)(2,1)S(1)} %collective-permute-done.12.refs_1_, bf16[4,2,8,4096]{3,2,1,0:T(8,128)(2,1)S(1)} %collective-permute-done.13.refs_2_, ...), custom_call_target="tpu_custom_call" | custom-call | flops 1610612736 | bytes 14680064 | tf_op jit(solution)/shard_map/pallas_call | solution.py:301
  86.4 2.4 %collective-permute-start.17 = (f32[2,2,4,4,512]{4,3,2,1,0:T(4,128)S(1)}, f32[2,2,4,4,512]{4,3,2,1,0:T(4,128)S(1)}, u32[]{:S(2)}, u32[]{:S(2)}) collective-permute-start(f32[2,2,4,4,512]{4,3,2,1,0:T(4,128)S(1)} %get-tuple-element.105), channel_id=1, source_target_pairs={{0,64},{64,0},{1,65},{65,1},{2,66},{66,2},{3,67},{67,3},{4,68},{68... | collective-permute-start | bytes 393224 | tf_op jit(solution)/shard_map/ppermute | solution.py:43
  90.3 2.7 %collective-permute-done.18 = f32[2,4,4,512]{3,2,1,0:T(4,128)S(1)} collective-permute-done((f32[2,4,4,512]{3,2,1,0:T(4,128)S(1)}, f32[2,4,4,512]{3,2,1,0:T(4,128)S(1)}, u32[]{:S(2)}, u32[]{:S(2)}) %collective-permute-start.18) | collective-permute-done | bytes 65568 | tf_op jit(solution)/shard_map/ppermute | solution.py:43
  (61 shorter events, 8.0 us)
Async XLA Ops:
  0.7 14.0 %copy-start.8 = (s32[2]{0:T(128)S(1)}, s32[2]{0:T(128)}, u32[]{:S(2)}) copy-start(s32[2]{0:T(128)} %param.6) | copy-start | bytes 28
  2.4 19.9 %collective-permute-start = (bf16[32,2,4096]{2,1,0:T(2,128)(2,1)S(1)}, bf16[32,2,4096]{2,1,0:T(2,128)(2,1)S(1)}, u32[]{:S(2)}, u32[]{:S(2)}) collective-permute-start(bf16[32,2,4096]{2,1,0:T(2,128)(2,1)S(1)} %get-tuple-element.56), channel_id=1, source_target_pairs={{0,16},{16,32},{32,48},{48,0},{1,17},{17,33},{33,49},{49,1},{2,18}... | collective-permute-start | bytes 1572872 | tf_op jit(solution)/shard_map/ppermute | solution.py:39
  4.6 17.8 %collective-permute-start.1 = (bf16[32,2,4096]{2,1,0:T(2,128)(2,1)S(1)}, bf16[32,2,4096]{2,1,0:T(2,128)(2,1)S(1)}, u32[]{:S(2)}, u32[]{:S(2)}) collective-permute-start(bf16[32,2,4096]{2,1,0:T(2,128)(2,1)S(1)} %get-tuple-element.57), channel_id=1, source_target_pairs={{0,48},{16,0},{32,16},{48,32},{1,49},{17,1},{33,17},{49,33},{2,50}... | collective-permute-start | bytes 1572872 | tf_op jit(solution)/shard_map/ppermute | solution.py:39
  8.8 13.6 %copy-start.3 = (bf16[32,2,4096]{2,1,0:T(2,128)(2,1)S(1)}, bf16[32,2,4096]{2,1,0:T(2,128)(2,1)}, u32[]{:S(2)}) copy-start(bf16[32,2,4096]{2,1,0:T(2,128)(2,1)} %get-tuple-element.61) | copy-start | bytes 1572868
  8.8 13.5 %collective-permute-start.2 = (bf16[16,2,4096]{2,1,0:T(2,128)(2,1)}, bf16[16,2,4096]{2,1,0:T(2,128)(2,1)S(1)}, u32[]{:S(2)}, u32[]{:S(2)}) collective-permute-start(bf16[16,2,4096]{2,1,0:T(2,128)(2,1)} %get-tuple-element.59), channel_id=1, source_target_pairs={{0,2},{2,4},{4,6},{6,8},{8,10},{10,12},{12,14},{14,0},{1,3},{3,5},... | collective-permute-start | bytes 786440 | tf_op jit(solution)/shard_map/ppermute | solution.py:39
  10.7 11.7 %collective-permute-start.3 = (bf16[16,2,4096]{2,1,0:T(2,128)(2,1)}, bf16[16,2,4096]{2,1,0:T(2,128)(2,1)S(1)}, u32[]{:S(2)}, u32[]{:S(2)}) collective-permute-start(bf16[16,2,4096]{2,1,0:T(2,128)(2,1)} %get-tuple-element.60), channel_id=1, source_target_pairs={{0,14},{2,0},{4,2},{6,4},{8,6},{10,8},{12,10},{14,12},{1,15},{3,1}... | collective-permute-start | bytes 786440 | tf_op jit(solution)/shard_map/ppermute | solution.py:39
  23.3 12.6 %collective-permute-start.4 = (bf16[2,4,2,4096]{3,2,1,0:T(2,128)(2,1)S(1)}, bf16[2,4,2,4096]{3,2,1,0:T(2,128)(2,1)S(1)}, u32[]{:S(2)}, u32[]{:S(2)}) collective-permute-start(bf16[2,4,2,4096]{3,2,1,0:T(2,128)(2,1)S(1)} %get-tuple-element.119), channel_id=1, source_target_pairs={{0,34},{2,36},{4,38},{6,40},{8,42},{10,44},{12,46},{14,32},{16,50}... | collective-permute-start | bytes 393224 | tf_op jit(solution)/shard_map/ppermute | solution.py:39
  23.4 12.5 %collective-permute-start.5 = (bf16[2,4,2,4096]{3,2,1,0:T(2,128)(2,1)S(1)}, bf16[2,4,2,4096]{3,2,1,0:T(2,128)(2,1)S(1)}, u32[]{:S(2)}, u32[]{:S(2)}) collective-permute-start(bf16[2,4,2,4096]{3,2,1,0:T(2,128)(2,1)S(1)} %get-tuple-element.118), channel_id=1, source_target_pairs={{0,4},{2,6},{4,8},{6,10},{8,12},{10,14},{12,0},{14,2},{1,5},{3,7},... | collective-permute-start | bytes 393224 | tf_op jit(solution)/shard_map/ppermute | solution.py:39
  26.5 9.5 %collective-permute-start.6 = (bf16[2,4,2,4096]{3,2,1,0:T(2,128)(2,1)S(1)}, bf16[2,4,2,4096]{3,2,1,0:T(2,128)(2,1)S(1)}, u32[]{:S(2)}, u32[]{:S(2)}) collective-permute-start(bf16[2,4,2,4096]{3,2,1,0:T(2,128)(2,1)S(1)} %get-tuple-element.117), channel_id=1, source_target_pairs={{0,46},{2,32},{4,34},{6,36},{8,38},{10,40},{12,42},{14,44},{16,62}... | collective-permute-start | bytes 393224 | tf_op jit(solution)/shard_map/ppermute | solution.py:39
  36.5 11.4 %collective-permute-start.7 = (bf16[2,4,2,4096]{3,2,1,0:T(2,128)(2,1)S(1)}, bf16[2,4,2,4096]{3,2,1,0:T(2,128)(2,1)S(1)}, u32[]{:S(2)}, u32[]{:S(2)}) collective-permute-start(bf16[2,4,2,4096]{3,2,1,0:T(2,128)(2,1)S(1)} %broadcast_select_fusion.10), channel_id=1, source_target_pairs={{0,8},{2,10},{4,12},{6,14},{8,0},{10,2},{12,4},{14,6},{1,9},{3,11}... | collective-permute-start | bytes 393224 | tf_op jit(solution)/shard_map/ppermute | solution.py:39
  48.2 7.9 %collective-permute-start.8 = (bf16[2,4,2,4096]{3,2,1,0:T(2,128)(2,1)S(1)}, bf16[2,4,2,4096]{3,2,1,0:T(2,128)(2,1)S(1)}, u32[]{:S(2)}, u32[]{:S(2)}) collective-permute-start(bf16[2,4,2,4096]{3,2,1,0:T(2,128)(2,1)S(1)} %broadcast_select_fusion.11.rows_ref), channel_id=1, source_target_pairs={{0,1},{1,0},{2,3},{3,2},{4,5},{5,4},{6,7},{7,6},{8,9},{9,8},{10,11... | collective-permute-start | bytes 393224 | tf_op jit(solution)/shard_map/ppermute | solution.py:39
  57.0 10.7 %collective-permute-start.9 = (bf16[2,8,4096]{2,1,0:T(8,128)(2,1)S(1)}, bf16[2,8,4096]{2,1,0:T(8,128)(2,1)S(1)}, u32[]{:S(2)}, u32[]{:S(2)}) collective-permute-start(bf16[2,8,4096]{2,1,0:T(8,128)(2,1)S(1)} %get-tuple-element.83), channel_id=1, source_target_pairs={{0,34},{2,36},{4,38},{6,40},{8,42},{10,44},{12,46},{14,32},{16,50}... | collective-permute-start | bytes 393224 | tf_op jit(solution)/shard_map/ppermute | solution.py:39
  59.0 8.8 %collective-permute-start.10 = (bf16[2,8,4096]{2,1,0:T(8,128)(2,1)S(1)}, bf16[2,8,4096]{2,1,0:T(8,128)(2,1)S(1)}, u32[]{:S(2)}, u32[]{:S(2)}) collective-permute-start(bf16[2,8,4096]{2,1,0:T(8,128)(2,1)S(1)} %get-tuple-element.83), channel_id=1, source_target_pairs={{0,4},{2,6},{4,8},{6,10},{8,12},{10,14},{12,0},{14,2},{1,5},{3,7},... | collective-permute-start | bytes 393224 | tf_op jit(solution)/shard_map/ppermute | solution.py:39
  59.0 8.8 %collective-permute-start.11 = (bf16[2,8,4096]{2,1,0:T(8,128)(2,1)S(1)}, bf16[2,8,4096]{2,1,0:T(8,128)(2,1)S(1)}, u32[]{:S(2)}, u32[]{:S(2)}) collective-permute-start(bf16[2,8,4096]{2,1,0:T(8,128)(2,1)S(1)} %get-tuple-element.83), channel_id=1, source_target_pairs={{0,46},{2,32},{4,34},{6,36},{8,38},{10,40},{12,42},{14,44},{16,62}... | collective-permute-start | bytes 393224 | tf_op jit(solution)/shard_map/ppermute | solution.py:39
  62.7 6.9 %copy-start.5 = (f32[8,512]{1,0:T(8,128)S(1)}, f32[8,512]{1,0:T(8,128)}, u32[]{:S(2)}) copy-start(f32[8,512]{1,0:T(8,128)} %get-tuple-element.91) | copy-start | bytes 49156
  62.7 6.9 %copy-start.6 = (f32[8,512]{1,0:T(8,128)S(1)}, f32[8,512]{1,0:T(8,128)}, u32[]{:S(2)}) copy-start(f32[8,512]{1,0:T(8,128)} %get-tuple-element.92) | copy-start | bytes 49156
  62.7 6.9 %copy-start.7 = (f32[8,512]{1,0:T(8,128)S(1)}, f32[8,512]{1,0:T(8,128)}, u32[]{:S(2)}) copy-start(f32[8,512]{1,0:T(8,128)} %get-tuple-element.93) | copy-start | bytes 49156
  67.8 14.5 %collective-permute-start.12 = (bf16[4,2,8,4096]{3,2,1,0:T(8,128)(2,1)S(1)}, bf16[4,2,8,4096]{3,2,1,0:T(8,128)(2,1)S(1)}, u32[]{:S(2)}, u32[]{:S(2)}) collective-permute-start(bf16[4,2,8,4096]{3,2,1,0:T(8,128)(2,1)S(1)} %bitcast_dynamic-update-slice_fusion.refs_0_), channel_id=1, source_target_pairs={{0,48},{16,0},{32,16},{48,32},{1,49},{17,1},{33,17},{49,33},{2,50}... | collective-permute-start | bytes 1572872 | tf_op jit(solution)/shard_map/ppermute | solution.py:39
  69.1 13.2 %collective-permute-start.13 = (bf16[4,2,8,4096]{3,2,1,0:T(8,128)(2,1)S(1)}, bf16[4,2,8,4096]{3,2,1,0:T(8,128)(2,1)S(1)}, u32[]{:S(2)}, u32[]{:S(2)}) collective-permute-start(bf16[4,2,8,4096]{3,2,1,0:T(8,128)(2,1)S(1)} %bitcast_dynamic-update-slice_fusion.refs_0_), channel_id=1, source_target_pairs={{0,2},{2,4},{4,6},{6,8},{8,10},{10,12},{12,14},{14,0},{1,3},{3,5},... | collective-permute-start | bytes 1572872 | tf_op jit(solution)/shard_map/ppermute | solution.py:39
  69.2 13.2 %collective-permute-start.14 = (bf16[4,2,8,4096]{3,2,1,0:T(8,128)(2,1)S(1)}, bf16[4,2,8,4096]{3,2,1,0:T(8,128)(2,1)S(1)}, u32[]{:S(2)}, u32[]{:S(2)}) collective-permute-start(bf16[4,2,8,4096]{3,2,1,0:T(8,128)(2,1)S(1)} %bitcast_dynamic-update-slice_fusion.refs_0_), channel_id=1, source_target_pairs={{0,16},{16,32},{32,48},{48,0},{1,17},{17,33},{33,49},{49,1},{2,18}... | collective-permute-start | bytes 1572872 | tf_op jit(solution)/shard_map/ppermute | solution.py:39
  70.3 9.2 %collective-permute-start.15 = (f32[512]{0:T(512)S(1)}, f32[512]{0:T(512)S(1)}, u32[]{:S(2)}, u32[]{:S(2)}) collective-permute-start(f32[512]{0:T(512)S(1)} %add_reduce_fusion), channel_id=1, source_target_pairs={{0,64},{64,0},{1,65},{65,1},{2,66},{66,2},{3,67},{67,3},{4,68},{68... | collective-permute-start | bytes 6152 | tf_op jit(solution)/shard_map/ppermute | solution.py:43
  79.5 2.8 %collective-permute-start.16 = (f32[512]{0:T(512)S(1)}, f32[512]{0:T(512)S(1)}, u32[]{:S(2)}, u32[]{:S(2)}) collective-permute-start(f32[512]{0:T(512)S(1)} %add.197), channel_id=1, source_target_pairs={{0,128},{128,0},{1,129},{129,1},{2,130},{130,2},{3,131},{131,3},{4... | collective-permute-start | bytes 6152 | tf_op jit(solution)/shard_map/ppermute | solution.py:43
  86.4 3.4 %collective-permute-start.17 = (f32[2,2,4,4,512]{4,3,2,1,0:T(4,128)S(1)}, f32[2,2,4,4,512]{4,3,2,1,0:T(4,128)S(1)}, u32[]{:S(2)}, u32[]{:S(2)}) collective-permute-start(f32[2,2,4,4,512]{4,3,2,1,0:T(4,128)S(1)} %get-tuple-element.105), channel_id=1, source_target_pairs={{0,64},{64,0},{1,65},{65,1},{2,66},{66,2},{3,67},{67,3},{4,68},{68... | collective-permute-start | bytes 393224 | tf_op jit(solution)/shard_map/ppermute | solution.py:43
  89.8 3.2 %collective-permute-start.18 = (f32[2,4,4,512]{3,2,1,0:T(4,128)S(1)}, f32[2,4,4,512]{3,2,1,0:T(4,128)S(1)}, u32[]{:S(2)}, u32[]{:S(2)}) collective-permute-start(f32[2,4,4,512]{3,2,1,0:T(4,128)S(1)} %fusion), channel_id=1, source_target_pairs={{0,128},{128,0},{1,129},{129,1},{2,130},{130,2},{3,131},{131,3},{4... | collective-permute-start | bytes 196616 | tf_op jit(solution)/shard_map/ppermute | solution.py:43
  (4 other events, 14.4 us)

commit v3 on v2

--- a/solution.py
+++ b/solution.py
@@ -245,54 +245,53 @@
 
 def score_kernel(*refs):
     groups, (w_ref, white_ref, keep_ref, send_ref, total_ref) = refs[:4], refs[4:]
-    layers, nb, block = w_ref.shape[:3]
-    step = pl.program_id(0)
-
-    @pl.when(step == 0)
-    def _():
-        total_ref[...] = jnp.zeros_like(total_ref)
-
+    layers, nblock, block = w_ref.shape[:3]
+    nb = nblock // 2
     total = jnp.zeros(total_ref.shape, jnp.float32)
     for layer in range(layers):
-        rows = jnp.concatenate([g[:, layer].reshape(-1, g.shape[-1]) for g in groups], axis=0)
-        query = [
-            lax.dot_general(
-                rows[:, b * block : (b + 1) * block], w_ref[layer, b], NT, preferred_element_type=jnp.float32
-            ).astype(white_ref.dtype)
-            for b in range(nb)
-        ]
-        total = total + jnp.dot(
-            jnp.concatenate(query, axis=1),
-            white_ref[layer].reshape(nb * block, -1),
-            preferred_element_type=jnp.float32,
-        )
-    total_ref[...] += total
-
-    @pl.when(step == pl.num_programs(0) - 1)
-    def _():
-        colour, z = colour_here(), lax.axis_index("z")
-        core, ylo = lax.axis_index("core"), lax.axis_index("ylo")
-        rounds, part = keep_ref.shape[0], keep_ref.shape[3]
-        for turn in range(4):
-            at = lax.rem(colour + turn, 4)
-            from_z = z + 8 - (1 if turn == 2 else 0)
-            for ref, kept in ((keep_ref, True), (send_ref, False)):
-
-                @pl.when((at // 2 == core) == kept)
-                def _(ref=ref, turn=turn, at=at, from_z=from_z):
-                    for slot, back in enumerate((0,) + STEPS):
-                        for which in range(rounds):
-                            start = ((turn * 4 + slot) * rounds + which) * part
-                            to = lax.rem(from_z - back, 4)
-                            ref[lax.rem(which + ylo, 2), lax.rem(at, 2), to] = total_ref[start : start + part]
-
-
-def score(groups, whitener, white, rounds, nb=8):
+        for first in range(0, nblock, nb):
+            span = slice(first * block, (first + nb) * block)
+            rows = jnp.concatenate(
+                [g[:, layer, :, span].reshape(-1, nb * block) for g in groups], axis=0
+            )
+            query = [
+                lax.dot_general(
+                    rows[:, b * block : (b + 1) * block],
+                    w_ref[layer, first + b],
+                    NT,
+                    preferred_element_type=jnp.float32,
+                ).astype(white_ref.dtype)
+                for b in range(nb)
+            ]
+            total = total + jnp.dot(
+                jnp.concatenate(query, axis=1),
+                white_ref[layer, first : first + nb].reshape(nb * block, -1),
+                preferred_element_type=jnp.float32,
+            )
+    total_ref[...] = total
+
+    colour, z = colour_here(), lax.axis_index("z")
+    core, ylo = lax.axis_index("core"), lax.axis_index("ylo")
+    rounds, part = keep_ref.shape[0], keep_ref.shape[3]
+    for turn in range(4):
+        at = lax.rem(colour + turn, 4)
+        from_z = z + 8 - (1 if turn == 2 else 0)
+        for ref, kept in ((keep_ref, True), (send_ref, False)):
+
+            @pl.when((at // 2 == core) == kept)
+            def _(ref=ref, turn=turn, at=at, from_z=from_z):
+                for slot, back in enumerate((0,) + STEPS):
+                    for which in range(rounds):
+                        start = ((turn * 4 + slot) * rounds + which) * part
+                        to = lax.rem(from_z - back, 4)
+                        ref[lax.rem(which + ylo, 2), lax.rem(at, 2), to] = total_ref[start : start + part]
+
+
+def score(groups, whitener, white, rounds):
     layers, nblock, block, examples = white.shape
     part = groups[0].shape[2] // rounds
     count = 16 * rounds * part
     out = jax.ShapeDtypeStruct((rounds, 2, 4, part, examples), jnp.float32)
-    out_spec = pl.BlockSpec(out.shape, lambda i: (0, 0, 0, 0, 0))
     cost = pl.CostEstimate(
         flops=2 * layers * nblock * block * count * (block + examples),
         bytes_accessed=2 * layers * nblock * block * (examples + block + count),
@@ -300,14 +299,9 @@
     )
     return pl.pallas_call(
         score_kernel,
-        grid=(nblock // nb,),
         out_shape=[out, out],
-        in_specs=[pl.BlockSpec(g.shape[:3] + (nb * block,), lambda i: (0, 0, 0, i)) for g in groups]
-        + [
-            pl.BlockSpec((layers, nb, block, block), lambda i: (0, i, 0, 0)),
-            pl.BlockSpec((layers, nb, block, examples), lambda i: (0, i, 0, 0)),
-        ],
-        out_specs=[out_spec, out_spec],
+        in_specs=[IN_VMEM] * (len(groups) + 2),
+        out_specs=[IN_VMEM, IN_VMEM],
         scratch_shapes=[pltpu.VMEM((count, examples), jnp.float32)],
         compiler_params=pltpu.CompilerParams(vmem_limit_bytes=SCORE_LIMIT),
         cost_estimate=cost,
@@ -337,8 +331,8 @@
     norm, _ = lax.optimization_barrier((jnp.sum(sum(norms), axis=0), groups[0]))
     white, _ = lax.optimization_barrier((done["white"], norm))
     norm, white = lax.optimization_barrier((norm + swap(norm, "core"), stage(white)))
+    groups, white, norm = lax.optimization_barrier((groups, white, norm))
     norm = norm + swap(norm, "ylo")
-    groups, norm = lax.optimization_barrier((groups, norm))
 
     keep, send = score(groups, whitener, white, rounds)
     got = swap(send, "core")

time: 94.1 us -> 92.9 us (0.987)
  waiting for transfers between devices: 6.07 us -> 3.32 us
  local copies, waits for them, and re-layouts: 4.14 us -> 5.7 us
  starting transfers between devices: 37.5 us -> 38.7 us
  Pallas kernels: 42.3 us -> 41.1 us
    ppermute x4, waiting for transfers between devices: 6.04 us -> 3.18 us  [swap(): return lax.ppermute(value, axis, [(0, 1), (1, 0)])]
    unnamed x18, local copies, waits for them, and re-layouts: 4.09 us -> 5.64 us
    ppermute x4, starting transfers between devices: 8.6 us -> 10 us  [swap(): return lax.ppermute(value, axis, [(0, 1), (1, 0)])]
    pallas_call x1, Pallas kernels: 4.03 us -> 2.76 us  [score(): pl.pallas_call(score_kernel, out_shape=[out, out], in_specs=[IN_VMEM] * (...]
  transfers between devices with their start and end apart: 19 -> 19, of which waited for: 3 -> 4; matrix products, arithmetic and copies ran while one was open for 1% -> 1% of each run, Pallas kernels for 38% -> 39%
where the time goes in v3:
time: 92.9 us; the launch traced here: 92.5 us
  Pallas kernels  41.1 us (44%)
  starting transfers between devices  38.7 us (42%)
  local copies, waits for them, and re-layouts  5.7 us (6%)
  waiting for transfers between devices  3.32 us (4%)
  other arithmetic  3.28 us (4%)
    pallas_call x5, Pallas kernels, whiten_blocks(): pl.pallas_call(whiten_kernel, grid=(count // nb,), out_shape=[jax.ShapeDt...  32.2 us
    ppermute x15, starting transfers between devices, shift(): return lax.ppermute(value, names if len(names) > 1 else names[0], pairs)  28.7 us
    ppermute x4, starting transfers between devices, swap(): return lax.ppermute(value, axis, [(0, 1), (1, 0)])  10 us
    unnamed x18, local copies, waits for them, and re-layouts  5.64 us
    pallas_call x2, Pallas kernels, pick_rows(): pl.pallas_call(functools.partial(pick_kernel, tuple((entry[:2] for entry...  4.66 us
    ppermute x4, waiting for transfers between devices, swap(): return lax.ppermute(value, axis, [(0, 1), (1, 0)])  3.18 us
    pallas_call x1, Pallas kernels, score(): pl.pallas_call(score_kernel, out_shape=[out, out], in_specs=[IN_VMEM] * (...  2.76 us
  transfers between devices with their start and end apart: 19, of which 4 were waited for; matrix products, arithmetic and copies ran while one was open for 1% of the time, Pallas kernels for 39%

profile of v3, /device:TPU:1, one launch (start us, length us, event | category | flops | bytes accessed | tf_op | source)
XLA Modules:
  0.0 92.5 jit_solution(5469118370828420727)
XLA Ops:
  0.7 1.8 %shard_map.46 = (bf16[32,2,4096]{2,1,0:T(2,128)(2,1)S(1)}, bf16[32,2,4096]{2,1,0:T(2,128)(2,1)S(1)}) custom-call(s32[2,64]{1,0:T(2,128)S(1)} %copy-done.2, bf16[512,2,4096]{2,1,0:T(2,128)(2,1)} %x_ref.4), custom_call_target="tpu_custom_call" | custom-call | bytes 2097152 | tf_op jit(solution)/shard_map/pallas_call | solution.py:72
  2.4 2.1 %collective-permute-start = (bf16[32,2,4096]{2,1,0:T(2,128)(2,1)S(1)}, bf16[32,2,4096]{2,1,0:T(2,128)(2,1)S(1)}, u32[]{:S(2)}, u32[]{:S(2)}) collective-permute-start(bf16[32,2,4096]{2,1,0:T(2,128)(2,1)S(1)} %get-tuple-element.57), channel_id=1, source_target_pairs={{0,16},{16,32},{32,48},{48,0},{1,17},{17,33},{33,49},{49,1},{2,18}... | collective-permute-start | bytes 1572872 | tf_op jit(solution)/shard_map/ppermute | solution.py:39
  4.6 1.4 %collective-permute-start.1 = (bf16[32,2,4096]{2,1,0:T(2,128)(2,1)S(1)}, bf16[32,2,4096]{2,1,0:T(2,128)(2,1)S(1)}, u32[]{:S(2)}, u32[]{:S(2)}) collective-permute-start(bf16[32,2,4096]{2,1,0:T(2,128)(2,1)S(1)} %get-tuple-element.58), channel_id=1, source_target_pairs={{0,48},{16,0},{32,16},{48,32},{1,49},{17,1},{33,17},{49,33},{2,50}... | collective-permute-start | bytes 1572872 | tf_op jit(solution)/shard_map/ppermute | solution.py:39
  5.9 2.9 %shard_map.47 = (bf16[16,2,4096]{2,1,0:T(2,128)(2,1)}, bf16[16,2,4096]{2,1,0:T(2,128)(2,1)}, bf16[32,2,4096]{2,1,0:T(2,128)(2,1)}) custom-call(s32[2,64]{1,0:T(2,128)} %ids.3, bf16[512,2,4096]{2,1,0:T(2,128)(2,1)} %x_ref.4), custom_call_target="tpu_custom_call" | custom-call | bytes 2097152 | tf_op jit(solution)/shard_map/pallas_call | solution.py:72
  8.8 1.8 %collective-permute-start.2 = (bf16[16,2,4096]{2,1,0:T(2,128)(2,1)}, bf16[16,2,4096]{2,1,0:T(2,128)(2,1)S(1)}, u32[]{:S(2)}, u32[]{:S(2)}) collective-permute-start(bf16[16,2,4096]{2,1,0:T(2,128)(2,1)} %get-tuple-element.60), channel_id=1, source_target_pairs={{0,2},{2,4},{4,6},{6,8},{8,10},{10,12},{12,14},{14,0},{1,3},{3,5},... | collective-permute-start | bytes 786440 | tf_op jit(solution)/shard_map/ppermute | solution.py:39
  10.7 4.0 %collective-permute-start.3 = (bf16[16,2,4096]{2,1,0:T(2,128)(2,1)}, bf16[16,2,4096]{2,1,0:T(2,128)(2,1)S(1)}, u32[]{:S(2)}, u32[]{:S(2)}) collective-permute-start(bf16[16,2,4096]{2,1,0:T(2,128)(2,1)} %get-tuple-element.61), channel_id=1, source_target_pairs={{0,14},{2,0},{4,2},{6,4},{8,6},{10,8},{12,10},{14,12},{1,15},{3,1}... | collective-permute-start | bytes 786440 | tf_op jit(solution)/shard_map/ppermute | solution.py:39
  14.9 7.4 %shard_map.48 = (bf16[2,16,256,512]{3,2,1,0:T(8,128)(2,1)}, f32[8,512]{1,0:T(8,128)}) custom-call(bf16[512,2,4096]{2,1,0:T(2,128)(2,1)} %x_ref.4, bf16[2,16,256,256]{3,2,1,0:T(8,128)(2,1)} %refs_4_.1), custom_call_target="tpu_custom_call" | custom-call | flops 536870912 | bytes 15728640 | tf_op jit(solution)/shard_map/pallas_call | solution.py:206
  23.4 3.1 %collective-permute-start.5 = (bf16[2,4,2,4096]{3,2,1,0:T(2,128)(2,1)S(1)}, bf16[2,4,2,4096]{3,2,1,0:T(2,128)(2,1)S(1)}, u32[]{:S(2)}, u32[]{:S(2)}) collective-permute-start(bf16[2,4,2,4096]{3,2,1,0:T(2,128)(2,1)S(1)} %get-tuple-element.120), channel_id=1, source_target_pairs={{0,4},{2,6},{4,8},{6,10},{8,12},{10,14},{12,0},{14,2},{1,5},{3,7},... | collective-permute-start | bytes 393224 | tf_op jit(solution)/shard_map/ppermute | solution.py:39
  26.5 2.0 %collective-permute-start.6 = (bf16[2,4,2,4096]{3,2,1,0:T(2,128)(2,1)S(1)}, bf16[2,4,2,4096]{3,2,1,0:T(2,128)(2,1)S(1)}, u32[]{:S(2)}, u32[]{:S(2)}) collective-permute-start(bf16[2,4,2,4096]{3,2,1,0:T(2,128)(2,1)S(1)} %get-tuple-element.119), channel_id=1, source_target_pairs={{0,46},{2,32},{4,34},{6,36},{8,38},{10,40},{12,42},{14,44},{16,62}... | collective-permute-start | bytes 393224 | tf_op jit(solution)/shard_map/ppermute | solution.py:39
  28.5 7.4 %shard_map.49 = (bf16[2,16,256,512]{3,2,1,0:T(8,128)(2,1)}, f32[8,512]{1,0:T(8,128)}) custom-call(bf16[512,2,4096]{2,1,0:T(2,128)(2,1)} %x_ref.4, bf16[2,16,256,256]{3,2,1,0:T(8,128)(2,1)} %refs_4_.1, bf16[2,16,256,512]{3,2,1,0:T(8,128)(2,1)} %get-tuple-element.70.refs_0_), custom_call_target="tpu_custom_call", output_to_operand_aliasing={{0}: (2, {})} | custom-call | flops 536870912 | bytes 15728640 | tf_op jit(solution)/shard_map/pallas_call | solution.py:206
  36.5 4.0 %collective-permute-start.7 = (bf16[2,4,2,4096]{3,2,1,0:T(2,128)(2,1)S(1)}, bf16[2,4,2,4096]{3,2,1,0:T(2,128)(2,1)S(1)}, u32[]{:S(2)}, u32[]{:S(2)}) collective-permute-start(bf16[2,4,2,4096]{3,2,1,0:T(2,128)(2,1)S(1)} %broadcast_select_fusion.10), channel_id=1, source_target_pairs={{0,8},{2,10},{4,12},{6,14},{8,0},{10,2},{12,4},{14,6},{1,9},{3,11}... | collective-permute-start | bytes 393224 | tf_op jit(solution)/shard_map/ppermute | solution.py:39
  40.6 7.4 %shard_map.50 = (bf16[2,16,256,512]{3,2,1,0:T(8,128)(2,1)}, f32[8,512]{1,0:T(8,128)}) custom-call(bf16[512,2,4096]{2,1,0:T(2,128)(2,1)} %x_ref.4, bf16[2,16,256,256]{3,2,1,0:T(8,128)(2,1)} %refs_4_.1, bf16[2,16,256,512]{3,2,1,0:T(8,128)(2,1)} %get-tuple-element.76.refs_0_), custom_call_target="tpu_custom_call", output_to_operand_aliasing={{0}: (2, {})} | custom-call | flops 536870912 | bytes 15728640 | tf_op jit(solution)/shard_map/pallas_call | solution.py:206
  48.2 3.0 %collective-permute-start.8 = (bf16[2,4,2,4096]{3,2,1,0:T(2,128)(2,1)S(1)}, bf16[2,4,2,4096]{3,2,1,0:T(2,128)(2,1)S(1)}, u32[]{:S(2)}, u32[]{:S(2)}) collective-permute-start(bf16[2,4,2,4096]{3,2,1,0:T(2,128)(2,1)S(1)} %broadcast_select_fusion.11.rows_ref), channel_id=1, source_target_pairs={{0,1},{1,0},{2,3},{3,2},{4,5},{5,4},{6,7},{7,6},{8,9},{9,8},{10,11... | collective-permute-start | bytes 393224 | tf_op jit(solution)/shard_map/ppermute | solution.py:39
  51.2 4.9 %shard_map.51 = (bf16[2,16,256,512]{3,2,1,0:T(8,128)(2,1)}, f32[8,512]{1,0:T(8,128)}) custom-call(bf16[512,2,4096]{2,1,0:T(2,128)(2,1)} %x_ref.4, bf16[2,16,256,256]{3,2,1,0:T(8,128)(2,1)} %refs_4_.1, bf16[2,16,256,512]{3,2,1,0:T(8,128)(2,1)} %get-tuple-element.80.refs_0_), custom_call_target="tpu_custom_call", output_to_operand_aliasing={{0}: (2, {})} | custom-call | flops 268435456 | bytes 7864320 | tf_op jit(solution)/shard_map/pallas_call | solution.py:206
  57.0 2.5 %collective-permute-start.9 = (bf16[2,8,4096]{2,1,0:T(8,128)(2,1)S(1)}, bf16[2,8,4096]{2,1,0:T(8,128)(2,1)S(1)}, u32[]{:S(2)}, u32[]{:S(2)}) collective-permute-start(bf16[2,8,4096]{2,1,0:T(8,128)(2,1)S(1)} %get-tuple-element.84), channel_id=1, source_target_pairs={{0,34},{2,36},{4,38},{6,40},{8,42},{10,44},{12,46},{14,32},{16,50}... | collective-permute-start | bytes 393224 | tf_op jit(solution)/shard_map/ppermute | solution.py:39
  59.5 3.1 %collective-permute-start.11 = (bf16[2,8,4096]{2,1,0:T(8,128)(2,1)S(1)}, bf16[2,8,4096]{2,1,0:T(8,128)(2,1)S(1)}, u32[]{:S(2)}, u32[]{:S(2)}) collective-permute-start(bf16[2,8,4096]{2,1,0:T(8,128)(2,1)S(1)} %get-tuple-element.84), channel_id=1, source_target_pairs={{0,46},{2,32},{4,34},{6,36},{8,38},{10,40},{12,42},{14,44},{16,62}... | collective-permute-start | bytes 393224 | tf_op jit(solution)/shard_map/ppermute | solution.py:39
  62.7 5.0 %shard_map.53 = (bf16[2,16,256,512]{3,2,1,0:T(8,128)(2,1)}, f32[8,512]{1,0:T(8,128)}) custom-call(bf16[512,2,4096]{2,1,0:T(2,128)(2,1)} %x_ref.4, bf16[2,16,256,256]{3,2,1,0:T(8,128)(2,1)} %refs_4_.1, bf16[2,16,256,512]{3,2,1,0:T(8,128)(2,1)} %get-tuple-element.86.refs_0_), custom_call_target="tpu_custom_call", output_to_operand_aliasing={{0}: (2, {})} | custom-call | flops 268435456 | bytes 7864320 | tf_op jit(solution)/shard_map/pallas_call | solution.py:206
  67.9 1.3 %collective-permute-start.12 = (bf16[4,2,8,4096]{3,2,1,0:T(8,128)(2,1)S(1)}, bf16[4,2,8,4096]{3,2,1,0:T(8,128)(2,1)S(1)}, u32[]{:S(2)}, u32[]{:S(2)}) collective-permute-start(bf16[4,2,8,4096]{3,2,1,0:T(8,128)(2,1)S(1)} %bitcast_dynamic-update-slice_fusion.refs_0_), channel_id=1, source_target_pairs={{0,48},{16,0},{32,16},{48,32},{1,49},{17,1},{33,17},{49,33},{2,50}... | collective-permute-start | bytes 1572872 | tf_op jit(solution)/shard_map/ppermute | solution.py:39
  70.2 5.3 %collective-permute-start.15 = (f32[512]{0:T(512)S(1)}, f32[512]{0:T(512)S(1)}, u32[]{:S(2)}, u32[]{:S(2)}) collective-permute-start(f32[512]{0:T(512)S(1)} %add_reduce_fusion), channel_id=1, source_target_pairs={{0,64},{64,0},{1,65},{65,1},{2,66},{66,2},{3,67},{67,3},{4,68},{68... | collective-permute-start | bytes 6152 | tf_op jit(solution)/shard_map/ppermute | solution.py:43
  75.5 3.4 %copy-done = bf16[2,16,256,512]{3,2,1,0:T(8,128)(2,1)S(1)} copy-done((bf16[2,16,256,512]{3,2,1,0:T(8,128)(2,1)S(1)}, bf16[2,16,256,512]{3,2,1,0:T(8,128)(2,1)}, u32[]{:S(2)}) %copy-start) | copy-done | bytes 8388632
  79.5 1.6 %copy-done.1 = bf16[2,16,256,256]{3,2,1,0:T(8,128)(2,1)S(1)} copy-done((bf16[2,16,256,256]{3,2,1,0:T(8,128)(2,1)S(1)}, bf16[2,16,256,256]{3,2,1,0:T(8,128)(2,1)}, u32[]{:S(2)}) %copy-start.1) | copy-done | bytes 4194328
  81.1 2.8 %shard_map.55 = (f32[2,2,4,4,512]{4,3,2,1,0:T(4,128)S(1)}, f32[2,2,4,4,512]{4,3,2,1,0:T(4,128)S(1)}) custom-call(bf16[4,2,8,4096]{3,2,1,0:T(8,128)(2,1)S(1)} %bitcast_dynamic-update-slice_fusion.refs_0_, bf16[4,2,8,4096]{3,2,1,0:T(8,128)(2,1)S(1)} %collective-permute-done.12.refs_1_, bf16[4,2,8,4096]{3,2,1,0:T(8,128)(2,1)S(1)} %collective-permute-done.13.refs_2_, ...), custom_call_target="tpu_custom_call" | custom-call | flops 1610612736 | bytes 14680064 | tf_op jit(solution)/shard_map/pallas_call | solution.py:300
  83.9 3.7 %collective-permute-start.16 = (f32[2,2,4,4,512]{4,3,2,1,0:T(4,128)S(1)}, f32[2,2,4,4,512]{4,3,2,1,0:T(4,128)S(1)}, u32[]{:S(2)}, u32[]{:S(2)}) collective-permute-start(f32[2,2,4,4,512]{4,3,2,1,0:T(4,128)S(1)} %get-tuple-element.107), channel_id=1, source_target_pairs={{0,64},{64,0},{1,65},{65,1},{2,66},{66,2},{3,67},{67,3},{4,68},{68... | collective-permute-start | bytes 393224 | tf_op jit(solution)/shard_map/ppermute | solution.py:43
  90.0 1.7 %collective-permute-done.17 = f32[2,4,4,512]{3,2,1,0:T(4,128)S(1)} collective-permute-done((f32[2,4,4,512]{3,2,1,0:T(4,128)S(1)}, f32[2,4,4,512]{3,2,1,0:T(4,128)S(1)}, u32[]{:S(2)}, u32[]{:S(2)}) %collective-permute-start.17) | collective-permute-done | bytes 65568 | tf_op jit(solution)/shard_map/ppermute | solution.py:43
  (60 shorter events, 8.4 us)
Async XLA Ops:
  0.7 14.0 %copy-start.8 = (s32[2]{0:T(128)S(1)}, s32[2]{0:T(128)}, u32[]{:S(2)}) copy-start(s32[2]{0:T(128)} %param.6) | copy-start | bytes 28
  2.4 19.9 %collective-permute-start = (bf16[32,2,4096]{2,1,0:T(2,128)(2,1)S(1)}, bf16[32,2,4096]{2,1,0:T(2,128)(2,1)S(1)}, u32[]{:S(2)}, u32[]{:S(2)}) collective-permute-start(bf16[32,2,4096]{2,1,0:T(2,128)(2,1)S(1)} %get-tuple-element.57), channel_id=1, source_target_pairs={{0,16},{16,32},{32,48},{48,0},{1,17},{17,33},{33,49},{49,1},{2,18}... | collective-permute-start | bytes 1572872 | tf_op jit(solution)/shard_map/ppermute | solution.py:39
  4.6 17.8 %collective-permute-start.1 = (bf16[32,2,4096]{2,1,0:T(2,128)(2,1)S(1)}, bf16[32,2,4096]{2,1,0:T(2,128)(2,1)S(1)}, u32[]{:S(2)}, u32[]{:S(2)}) collective-permute-start(bf16[32,2,4096]{2,1,0:T(2,128)(2,1)S(1)} %get-tuple-element.58), channel_id=1, source_target_pairs={{0,48},{16,0},{32,16},{48,32},{1,49},{17,1},{33,17},{49,33},{2,50}... | collective-permute-start | bytes 1572872 | tf_op jit(solution)/shard_map/ppermute | solution.py:39
  8.8 13.6 %copy-start.3 = (bf16[32,2,4096]{2,1,0:T(2,128)(2,1)S(1)}, bf16[32,2,4096]{2,1,0:T(2,128)(2,1)}, u32[]{:S(2)}) copy-start(bf16[32,2,4096]{2,1,0:T(2,128)(2,1)} %get-tuple-element.62) | copy-start | bytes 1572868
  8.8 13.5 %collective-permute-start.2 = (bf16[16,2,4096]{2,1,0:T(2,128)(2,1)}, bf16[16,2,4096]{2,1,0:T(2,128)(2,1)S(1)}, u32[]{:S(2)}, u32[]{:S(2)}) collective-permute-start(bf16[16,2,4096]{2,1,0:T(2,128)(2,1)} %get-tuple-element.60), channel_id=1, source_target_pairs={{0,2},{2,4},{4,6},{6,8},{8,10},{10,12},{12,14},{14,0},{1,3},{3,5},... | collective-permute-start | bytes 786440 | tf_op jit(solution)/shard_map/ppermute | solution.py:39
  10.7 11.7 %collective-permute-start.3 = (bf16[16,2,4096]{2,1,0:T(2,128)(2,1)}, bf16[16,2,4096]{2,1,0:T(2,128)(2,1)S(1)}, u32[]{:S(2)}, u32[]{:S(2)}) collective-permute-start(bf16[16,2,4096]{2,1,0:T(2,128)(2,1)} %get-tuple-element.61), channel_id=1, source_target_pairs={{0,14},{2,0},{4,2},{6,4},{8,6},{10,8},{12,10},{14,12},{1,15},{3,1}... | collective-permute-start | bytes 786440 | tf_op jit(solution)/shard_map/ppermute | solution.py:39
  23.3 12.6 %collective-permute-start.4 = (bf16[2,4,2,4096]{3,2,1,0:T(2,128)(2,1)S(1)}, bf16[2,4,2,4096]{3,2,1,0:T(2,128)(2,1)S(1)}, u32[]{:S(2)}, u32[]{:S(2)}) collective-permute-start(bf16[2,4,2,4096]{3,2,1,0:T(2,128)(2,1)S(1)} %get-tuple-element.121), channel_id=1, source_target_pairs={{0,34},{2,36},{4,38},{6,40},{8,42},{10,44},{12,46},{14,32},{16,50}... | collective-permute-start | bytes 393224 | tf_op jit(solution)/shard_map/ppermute | solution.py:39
  23.4 12.5 %collective-permute-start.5 = (bf16[2,4,2,4096]{3,2,1,0:T(2,128)(2,1)S(1)}, bf16[2,4,2,4096]{3,2,1,0:T(2,128)(2,1)S(1)}, u32[]{:S(2)}, u32[]{:S(2)}) collective-permute-start(bf16[2,4,2,4096]{3,2,1,0:T(2,128)(2,1)S(1)} %get-tuple-element.120), channel_id=1, source_target_pairs={{0,4},{2,6},{4,8},{6,10},{8,12},{10,14},{12,0},{14,2},{1,5},{3,7},... | collective-permute-start | bytes 393224 | tf_op jit(solution)/shard_map/ppermute | solution.py:39
  26.5 9.5 %collective-permute-start.6 = (bf16[2,4,2,4096]{3,2,1,0:T(2,128)(2,1)S(1)}, bf16[2,4,2,4096]{3,2,1,0:T(2,128)(2,1)S(1)}, u32[]{:S(2)}, u32[]{:S(2)}) collective-permute-start(bf16[2,4,2,4096]{3,2,1,0:T(2,128)(2,1)S(1)} %get-tuple-element.119), channel_id=1, source_target_pairs={{0,46},{2,32},{4,34},{6,36},{8,38},{10,40},{12,42},{14,44},{16,62}... | collective-permute-start | bytes 393224 | tf_op jit(solution)/shard_map/ppermute | solution.py:39
  36.5 11.4 %collective-permute-start.7 = (bf16[2,4,2,4096]{3,2,1,0:T(2,128)(2,1)S(1)}, bf16[2,4,2,4096]{3,2,1,0:T(2,128)(2,1)S(1)}, u32[]{:S(2)}, u32[]{:S(2)}) collective-permute-start(bf16[2,4,2,4096]{3,2,1,0:T(2,128)(2,1)S(1)} %broadcast_select_fusion.10), channel_id=1, source_target_pairs={{0,8},{2,10},{4,12},{6,14},{8,0},{10,2},{12,4},{14,6},{1,9},{3,11}... | collective-permute-start | bytes 393224 | tf_op jit(solution)/shard_map/ppermute | solution.py:39
  48.2 7.9 %collective-permute-start.8 = (bf16[2,4,2,4096]{3,2,1,0:T(2,128)(2,1)S(1)}, bf16[2,4,2,4096]{3,2,1,0:T(2,128)(2,1)S(1)}, u32[]{:S(2)}, u32[]{:S(2)}) collective-permute-start(bf16[2,4,2,4096]{3,2,1,0:T(2,128)(2,1)S(1)} %broadcast_select_fusion.11.rows_ref), channel_id=1, source_target_pairs={{0,1},{1,0},{2,3},{3,2},{4,5},{5,4},{6,7},{7,6},{8,9},{9,8},{10,11... | collective-permute-start | bytes 393224 | tf_op jit(solution)/shard_map/ppermute | solution.py:39
  57.0 10.7 %collective-permute-start.9 = (bf16[2,8,4096]{2,1,0:T(8,128)(2,1)S(1)}, bf16[2,8,4096]{2,1,0:T(8,128)(2,1)S(1)}, u32[]{:S(2)}, u32[]{:S(2)}) collective-permute-start(bf16[2,8,4096]{2,1,0:T(8,128)(2,1)S(1)} %get-tuple-element.84), channel_id=1, source_target_pairs={{0,34},{2,36},{4,38},{6,40},{8,42},{10,44},{12,46},{14,32},{16,50}... | collective-permute-start | bytes 393224 | tf_op jit(solution)/shard_map/ppermute | solution.py:39
  59.5 8.3 %collective-permute-start.10 = (bf16[2,8,4096]{2,1,0:T(8,128)(2,1)S(1)}, bf16[2,8,4096]{2,1,0:T(8,128)(2,1)S(1)}, u32[]{:S(2)}, u32[]{:S(2)}) collective-permute-start(bf16[2,8,4096]{2,1,0:T(8,128)(2,1)S(1)} %get-tuple-element.84), channel_id=1, source_target_pairs={{0,4},{2,6},{4,8},{6,10},{8,12},{10,14},{12,0},{14,2},{1,5},{3,7},... | collective-permute-start | bytes 393224 | tf_op jit(solution)/shard_map/ppermute | solution.py:39
  59.5 8.3 %collective-permute-start.11 = (bf16[2,8,4096]{2,1,0:T(8,128)(2,1)S(1)}, bf16[2,8,4096]{2,1,0:T(8,128)(2,1)S(1)}, u32[]{:S(2)}, u32[]{:S(2)}) collective-permute-start(bf16[2,8,4096]{2,1,0:T(8,128)(2,1)S(1)} %get-tuple-element.84), channel_id=1, source_target_pairs={{0,46},{2,32},{4,34},{6,36},{8,38},{10,40},{12,42},{14,44},{16,62}... | collective-permute-start | bytes 393224 | tf_op jit(solution)/shard_map/ppermute | solution.py:39
  62.7 6.8 %copy-start.5 = (f32[8,512]{1,0:T(8,128)S(1)}, f32[8,512]{1,0:T(8,128)}, u32[]{:S(2)}) copy-start(f32[8,512]{1,0:T(8,128)} %get-tuple-element.92) | copy-start | bytes 49156
  62.7 6.8 %copy-start.6 = (f32[8,512]{1,0:T(8,128)S(1)}, f32[8,512]{1,0:T(8,128)}, u32[]{:S(2)}) copy-start(f32[8,512]{1,0:T(8,128)} %get-tuple-element.93) | copy-start | bytes 49156
  62.7 6.8 %copy-start.7 = (f32[8,512]{1,0:T(8,128)S(1)}, f32[8,512]{1,0:T(8,128)}, u32[]{:S(2)}) copy-start(f32[8,512]{1,0:T(8,128)} %get-tuple-element.94) | copy-start | bytes 49156
  67.9 11.6 %collective-permute-start.12 = (bf16[4,2,8,4096]{3,2,1,0:T(8,128)(2,1)S(1)}, bf16[4,2,8,4096]{3,2,1,0:T(8,128)(2,1)S(1)}, u32[]{:S(2)}, u32[]{:S(2)}) collective-permute-start(bf16[4,2,8,4096]{3,2,1,0:T(8,128)(2,1)S(1)} %bitcast_dynamic-update-slice_fusion.refs_0_), channel_id=1, source_target_pairs={{0,48},{16,0},{32,16},{48,32},{1,49},{17,1},{33,17},{49,33},{2,50}... | collective-permute-start | bytes 1572872 | tf_op jit(solution)/shard_map/ppermute | solution.py:39
  69.1 10.4 %collective-permute-start.13 = (bf16[4,2,8,4096]{3,2,1,0:T(8,128)(2,1)S(1)}, bf16[4,2,8,4096]{3,2,1,0:T(8,128)(2,1)S(1)}, u32[]{:S(2)}, u32[]{:S(2)}) collective-permute-start(bf16[4,2,8,4096]{3,2,1,0:T(8,128)(2,1)S(1)} %bitcast_dynamic-update-slice_fusion.refs_0_), channel_id=1, source_target_pairs={{0,2},{2,4},{4,6},{6,8},{8,10},{10,12},{12,14},{14,0},{1,3},{3,5},... | collective-permute-start | bytes 1572872 | tf_op jit(solution)/shard_map/ppermute | solution.py:39
  69.2 10.4 %collective-permute-start.14 = (bf16[4,2,8,4096]{3,2,1,0:T(8,128)(2,1)S(1)}, bf16[4,2,8,4096]{3,2,1,0:T(8,128)(2,1)S(1)}, u32[]{:S(2)}, u32[]{:S(2)}) collective-permute-start(bf16[4,2,8,4096]{3,2,1,0:T(8,128)(2,1)S(1)} %bitcast_dynamic-update-slice_fusion.refs_0_), channel_id=1, source_target_pairs={{0,16},{16,32},{32,48},{48,0},{1,17},{17,33},{33,49},{49,1},{2,18}... | collective-permute-start | bytes 1572872 | tf_op jit(solution)/shard_map/ppermute | solution.py:39
  70.2 9.3 %collective-permute-start.15 = (f32[512]{0:T(512)S(1)}, f32[512]{0:T(512)S(1)}, u32[]{:S(2)}, u32[]{:S(2)}) collective-permute-start(f32[512]{0:T(512)S(1)} %add_reduce_fusion), channel_id=1, source_target_pairs={{0,64},{64,0},{1,65},{65,1},{2,66},{66,2},{3,67},{67,3},{4,68},{68... | collective-permute-start | bytes 6152 | tf_op jit(solution)/shard_map/ppermute | solution.py:43
  83.9 4.7 %collective-permute-start.16 = (f32[2,2,4,4,512]{4,3,2,1,0:T(4,128)S(1)}, f32[2,2,4,4,512]{4,3,2,1,0:T(4,128)S(1)}, u32[]{:S(2)}, u32[]{:S(2)}) collective-permute-start(f32[2,2,4,4,512]{4,3,2,1,0:T(4,128)S(1)} %get-tuple-element.107), channel_id=1, source_target_pairs={{0,64},{64,0},{1,65},{65,1},{2,66},{66,2},{3,67},{67,3},{4,68},{68... | collective-permute-start | bytes 393224 | tf_op jit(solution)/shard_map/ppermute | solution.py:43
  87.6 2.5 %collective-permute-start.18 = (f32[512]{0:T(512)S(1)}, f32[512]{0:T(512)S(1)}, u32[]{:S(2)}, u32[]{:S(2)}) collective-permute-start(f32[512]{0:T(512)S(1)} %add.197), channel_id=1, source_target_pairs={{0,128},{128,0},{1,129},{129,1},{2,130},{130,2},{3,131},{131,3},{4... | collective-permute-start | bytes 6152 | tf_op jit(solution)/shard_map/ppermute | solution.py:43
  88.6 3.2 %collective-permute-start.17 = (f32[2,4,4,512]{3,2,1,0:T(4,128)S(1)}, f32[2,4,4,512]{3,2,1,0:T(4,128)S(1)}, u32[]{:S(2)}, u32[]{:S(2)}) collective-permute-start(f32[2,4,4,512]{3,2,1,0:T(4,128)S(1)} %fusion), channel_id=1, source_target_pairs={{0,128},{128,0},{1,129},{129,1},{2,130},{130,2},{3,131},{131,3},{4... | collective-permute-start | bytes 196616 | tf_op jit(solution)/shard_map/ppermute | solution.py:43
  (4 other events, 13.0 us)

commit v4 on v3

--- a/solution.py
+++ b/solution.py
@@ -165,7 +165,8 @@
     for at, rows in enumerate(got):
         whole = lax.dynamic_update_index_in_dim(whole, rows, at + 1, 0)
 
-    return whole, shift(whole, dx=-1), shift(whole, dz=1), shift(whole, dx=1)
+    after, before = shift(whole, dx=-1), shift(whole, dx=1)
+    return whole, after, shift(whole[:2], dz=1), shift(whole[:2], dz=-1), before
 
 
 def whiten_kernel(x_ref, w_ref, *refs):
@@ -225,26 +226,26 @@
     )(*operands)
 
 
-def stage_kernel(white, out, sem):
+def stage_kernel(white, _, out, sem):
     copy = pltpu.make_async_copy(white, out, sem)
     copy.start()
     copy.wait()
 
 
-def stage(white):
+def stage(white, whitener):
     return pl.pallas_call(
         stage_kernel,
         out_shape=jax.ShapeDtypeStruct(white.shape, white.dtype),
-        in_specs=[pl.BlockSpec(memory_space=pl.ANY)],
+        in_specs=[pl.BlockSpec(memory_space=pl.ANY), IN_VMEM],
         out_specs=IN_VMEM,
         scratch_shapes=[pltpu.SemaphoreType.DMA],
         compiler_params=pltpu.CompilerParams(vmem_limit_bytes=STAGE_LIMIT),
         cost_estimate=pl.CostEstimate(flops=0, bytes_accessed=4 * white.size, transcendentals=0),
-    )(white)
+    )(white, whitener)
 
 
 def score_kernel(*refs):
-    groups, (w_ref, white_ref, keep_ref, send_ref, total_ref) = refs[:4], refs[4:]
+    groups, (w_ref, white_ref, keep_ref, send_ref, total_ref) = refs[:5], refs[5:]
     layers, nblock, block = w_ref.shape[:3]
     nb = nblock // 2
     total = jnp.zeros(total_ref.shape, jnp.float32)
@@ -275,15 +276,14 @@
     rounds, part = keep_ref.shape[0], keep_ref.shape[3]
     for turn in range(4):
         at = lax.rem(colour + turn, 4)
-        from_z = z + 8 - (1 if turn == 2 else 0)
         for ref, kept in ((keep_ref, True), (send_ref, False)):
 
             @pl.when((at // 2 == core) == kept)
-            def _(ref=ref, turn=turn, at=at, from_z=from_z):
-                for slot, back in enumerate((0,) + STEPS):
+            def _(ref=ref, turn=turn, at=at):
+                for slot, back in enumerate((1, 2, -1, 0) if turn == 2 else (0,) + STEPS):
                     for which in range(rounds):
                         start = ((turn * 4 + slot) * rounds + which) * part
-                        to = lax.rem(from_z - back, 4)
+                        to = lax.rem(z + 8 - back, 4)
                         ref[lax.rem(which + ylo, 2), lax.rem(at, 2), to] = total_ref[start : start + part]
 
 
@@ -330,7 +330,7 @@
     groups = broadcast(gradients, owners, query_ids, beside)
     norm, _ = lax.optimization_barrier((jnp.sum(sum(norms), axis=0), groups[0]))
     white, _ = lax.optimization_barrier((done["white"], norm))
-    norm, white = lax.optimization_barrier((norm + swap(norm, "core"), stage(white)))
+    norm, white = lax.optimization_barrier((norm + swap(norm, "core"), stage(white, whitener)))
     groups, white, norm = lax.optimization_barrier((groups, white, norm))
     norm = norm + swap(norm, "ylo")
 

time: 92.9 us -> 93 us (level)
  starting transfers between devices: 38.7 us -> 40.3 us
  local copies, waits for them, and re-layouts: 5.7 us -> 4.16 us
    ppermute x15 -> x16, starting transfers between devices: 28.7 us -> 31.5 us  [shift(): return lax.ppermute(value, names if len(names) > 1 else names[0], pairs)]
    unnamed x18, local copies, waits for them, and re-layouts: 5.64 us -> 4.09 us
    ppermute x4, starting transfers between devices: 10 us -> 8.84 us  [swap(): return lax.ppermute(value, axis, [(0, 1), (1, 0)])]
  transfers between devices with their start and end apart: 19 -> 20, of which waited for: 4 -> 3; matrix products, arithmetic and copies ran while one was open for 1% -> 1% of each run, Pallas kernels for 39% -> 39%
where the time goes in v4:
time: 93 us; the launch traced here: 92.6 us
  Pallas kernels  41.2 us (44%)
  starting transfers between devices  40.3 us (43%)
  local copies, waits for them, and re-layouts  4.16 us (4%)
  other arithmetic  3.28 us (4%)
  waiting for transfers between devices  3.22 us (3%)
    pallas_call x5, Pallas kernels, whiten_blocks(): pl.pallas_call(whiten_kernel, grid=(count // nb,), out_shape=[jax.ShapeDt...  32.3 us
    ppermute x16, starting transfers between devices, shift(): return lax.ppermute(value, names if len(names) > 1 else names[0], pairs)  31.5 us
    ppermute x4, starting transfers between devices, swap(): return lax.ppermute(value, axis, [(0, 1), (1, 0)])  8.84 us
    pallas_call x2, Pallas kernels, pick_rows(): pl.pallas_call(functools.partial(pick_kernel, tuple((entry[:2] for entry...  4.7 us
    unnamed x18, local copies, waits for them, and re-layouts  4.09 us
    ppermute x4, waiting for transfers between devices, swap(): return lax.ppermute(value, axis, [(0, 1), (1, 0)])  3.18 us
    pallas_call x1, Pallas kernels, score(): pl.pallas_call(score_kernel, out_shape=[out, out], in_specs=[IN_VMEM] * (...  2.76 us
  transfers between devices with their start and end apart: 20, of which 3 were waited for; matrix products, arithmetic and copies ran while one was open for 1% of the time, Pallas kernels for 39%

profile of v4, /device:TPU:1, one launch (start us, length us, event | category | flops | bytes accessed | tf_op | source)
XLA Modules:
  0.0 92.6 jit_solution(12480130003458972602)
XLA Ops:
  0.7 1.8 %shard_map.46 = (bf16[32,2,4096]{2,1,0:T(2,128)(2,1)S(1)}, bf16[32,2,4096]{2,1,0:T(2,128)(2,1)S(1)}) custom-call(s32[2,64]{1,0:T(2,128)S(1)} %copy-done.2, bf16[512,2,4096]{2,1,0:T(2,128)(2,1)} %x_ref.4), custom_call_target="tpu_custom_call" | custom-call | bytes 2097152 | tf_op jit(solution)/shard_map/pallas_call | solution.py:72
  2.5 2.1 %collective-permute-start = (bf16[32,2,4096]{2,1,0:T(2,128)(2,1)S(1)}, bf16[32,2,4096]{2,1,0:T(2,128)(2,1)S(1)}, u32[]{:S(2)}, u32[]{:S(2)}) collective-permute-start(bf16[32,2,4096]{2,1,0:T(2,128)(2,1)S(1)} %get-tuple-element.58), channel_id=1, source_target_pairs={{0,16},{16,32},{32,48},{48,0},{1,17},{17,33},{33,49},{49,1},{2,18}... | collective-permute-start | bytes 1572872 | tf_op jit(solution)/shard_map/ppermute | solution.py:39
  4.6 1.4 %collective-permute-start.1 = (bf16[32,2,4096]{2,1,0:T(2,128)(2,1)S(1)}, bf16[32,2,4096]{2,1,0:T(2,128)(2,1)S(1)}, u32[]{:S(2)}, u32[]{:S(2)}) collective-permute-start(bf16[32,2,4096]{2,1,0:T(2,128)(2,1)S(1)} %get-tuple-element.59), channel_id=1, source_target_pairs={{0,48},{16,0},{32,16},{48,32},{1,49},{17,1},{33,17},{49,33},{2,50}... | collective-permute-start | bytes 1572872 | tf_op jit(solution)/shard_map/ppermute | solution.py:39
  5.9 2.9 %shard_map.47 = (bf16[16,2,4096]{2,1,0:T(2,128)(2,1)}, bf16[16,2,4096]{2,1,0:T(2,128)(2,1)}, bf16[32,2,4096]{2,1,0:T(2,128)(2,1)}) custom-call(s32[2,64]{1,0:T(2,128)} %ids.3, bf16[512,2,4096]{2,1,0:T(2,128)(2,1)} %x_ref.4), custom_call_target="tpu_custom_call" | custom-call | bytes 2097152 | tf_op jit(solution)/shard_map/pallas_call | solution.py:72
  8.9 1.8 %collective-permute-start.2 = (bf16[16,2,4096]{2,1,0:T(2,128)(2,1)}, bf16[16,2,4096]{2,1,0:T(2,128)(2,1)S(1)}, u32[]{:S(2)}, u32[]{:S(2)}) collective-permute-start(bf16[16,2,4096]{2,1,0:T(2,128)(2,1)} %get-tuple-element.61), channel_id=1, source_target_pairs={{0,2},{2,4},{4,6},{6,8},{8,10},{10,12},{12,14},{14,0},{1,3},{3,5},... | collective-permute-start | bytes 786440 | tf_op jit(solution)/shard_map/ppermute | solution.py:39
  10.7 4.0 %collective-permute-start.3 = (bf16[16,2,4096]{2,1,0:T(2,128)(2,1)}, bf16[16,2,4096]{2,1,0:T(2,128)(2,1)S(1)}, u32[]{:S(2)}, u32[]{:S(2)}) collective-permute-start(bf16[16,2,4096]{2,1,0:T(2,128)(2,1)} %get-tuple-element.62), channel_id=1, source_target_pairs={{0,14},{2,0},{4,2},{6,4},{8,6},{10,8},{12,10},{14,12},{1,15},{3,1}... | collective-permute-start | bytes 786440 | tf_op jit(solution)/shard_map/ppermute | solution.py:39
  15.0 7.4 %shard_map.48 = (bf16[2,16,256,512]{3,2,1,0:T(8,128)(2,1)}, f32[8,512]{1,0:T(8,128)}) custom-call(bf16[512,2,4096]{2,1,0:T(2,128)(2,1)} %x_ref.4, bf16[2,16,256,256]{3,2,1,0:T(8,128)(2,1)} %refs_5_.1), custom_call_target="tpu_custom_call" | custom-call | flops 536870912 | bytes 15728640 | tf_op jit(solution)/shard_map/pallas_call | solution.py:207
  23.5 3.1 %collective-permute-start.5 = (bf16[2,4,2,4096]{3,2,1,0:T(2,128)(2,1)S(1)}, bf16[2,4,2,4096]{3,2,1,0:T(2,128)(2,1)S(1)}, u32[]{:S(2)}, u32[]{:S(2)}) collective-permute-start(bf16[2,4,2,4096]{3,2,1,0:T(2,128)(2,1)S(1)} %get-tuple-element.122), channel_id=1, source_target_pairs={{0,4},{2,6},{4,8},{6,10},{8,12},{10,14},{12,0},{14,2},{1,5},{3,7},... | collective-permute-start | bytes 393224 | tf_op jit(solution)/shard_map/ppermute | solution.py:39
  26.5 2.0 %collective-permute-start.6 = (bf16[2,4,2,4096]{3,2,1,0:T(2,128)(2,1)S(1)}, bf16[2,4,2,4096]{3,2,1,0:T(2,128)(2,1)S(1)}, u32[]{:S(2)}, u32[]{:S(2)}) collective-permute-start(bf16[2,4,2,4096]{3,2,1,0:T(2,128)(2,1)S(1)} %get-tuple-element.121), channel_id=1, source_target_pairs={{0,46},{2,32},{4,34},{6,36},{8,38},{10,40},{12,42},{14,44},{16,62}... | collective-permute-start | bytes 393224 | tf_op jit(solution)/shard_map/ppermute | solution.py:39
  28.6 7.4 %shard_map.49 = (bf16[2,16,256,512]{3,2,1,0:T(8,128)(2,1)}, f32[8,512]{1,0:T(8,128)}) custom-call(bf16[512,2,4096]{2,1,0:T(2,128)(2,1)} %x_ref.4, bf16[2,16,256,256]{3,2,1,0:T(8,128)(2,1)} %refs_5_.1, bf16[2,16,256,512]{3,2,1,0:T(8,128)(2,1)} %get-tuple-element.71.refs_0_), custom_call_target="tpu_custom_call", output_to_operand_aliasing={{0}: (2, {})} | custom-call | flops 536870912 | bytes 15728640 | tf_op jit(solution)/shard_map/pallas_call | solution.py:207
  36.6 4.0 %collective-permute-start.7 = (bf16[2,4,2,4096]{3,2,1,0:T(2,128)(2,1)S(1)}, bf16[2,4,2,4096]{3,2,1,0:T(2,128)(2,1)S(1)}, u32[]{:S(2)}, u32[]{:S(2)}) collective-permute-start(bf16[2,4,2,4096]{3,2,1,0:T(2,128)(2,1)S(1)} %broadcast_select_fusion.10), channel_id=1, source_target_pairs={{0,8},{2,10},{4,12},{6,14},{8,0},{10,2},{12,4},{14,6},{1,9},{3,11}... | collective-permute-start | bytes 393224 | tf_op jit(solution)/shard_map/ppermute | solution.py:39
  40.6 7.4 %shard_map.50 = (bf16[2,16,256,512]{3,2,1,0:T(8,128)(2,1)}, f32[8,512]{1,0:T(8,128)}) custom-call(bf16[512,2,4096]{2,1,0:T(2,128)(2,1)} %x_ref.4, bf16[2,16,256,256]{3,2,1,0:T(8,128)(2,1)} %refs_5_.1, bf16[2,16,256,512]{3,2,1,0:T(8,128)(2,1)} %get-tuple-element.77.refs_0_), custom_call_target="tpu_custom_call", output_to_operand_aliasing={{0}: (2, {})} | custom-call | flops 536870912 | bytes 15728640 | tf_op jit(solution)/shard_map/pallas_call | solution.py:207
  48.3 3.0 %collective-permute-start.8 = (bf16[2,4,2,4096]{3,2,1,0:T(2,128)(2,1)S(1)}, bf16[2,4,2,4096]{3,2,1,0:T(2,128)(2,1)S(1)}, u32[]{:S(2)}, u32[]{:S(2)}) collective-permute-start(bf16[2,4,2,4096]{3,2,1,0:T(2,128)(2,1)S(1)} %broadcast_select_fusion.11.rows_ref), channel_id=1, source_target_pairs={{0,1},{1,0},{2,3},{3,2},{4,5},{5,4},{6,7},{7,6},{8,9},{9,8},{10,11... | collective-permute-start | bytes 393224 | tf_op jit(solution)/shard_map/ppermute | solution.py:39
  51.2 4.9 %shard_map.51 = (bf16[2,16,256,512]{3,2,1,0:T(8,128)(2,1)}, f32[8,512]{1,0:T(8,128)}) custom-call(bf16[512,2,4096]{2,1,0:T(2,128)(2,1)} %x_ref.4, bf16[2,16,256,256]{3,2,1,0:T(8,128)(2,1)} %refs_5_.1, bf16[2,16,256,512]{3,2,1,0:T(8,128)(2,1)} %get-tuple-element.81.refs_0_), custom_call_target="tpu_custom_call", output_to_operand_aliasing={{0}: (2, {})} | custom-call | flops 268435456 | bytes 7864320 | tf_op jit(solution)/shard_map/pallas_call | solution.py:207
  57.1 2.0 %collective-permute-start.9 = (bf16[2,8,4096]{2,1,0:T(8,128)(2,1)S(1)}, bf16[2,8,4096]{2,1,0:T(8,128)(2,1)S(1)}, u32[]{:S(2)}, u32[]{:S(2)}) collective-permute-start(bf16[2,8,4096]{2,1,0:T(8,128)(2,1)S(1)} %get-tuple-element.85), channel_id=1, source_target_pairs={{0,34},{2,36},{4,38},{6,40},{8,42},{10,44},{12,46},{14,32},{16,50}... | collective-permute-start | bytes 393224 | tf_op jit(solution)/shard_map/ppermute | solution.py:39
  59.0 3.7 %collective-permute-start.11 = (bf16[2,8,4096]{2,1,0:T(8,128)(2,1)S(1)}, bf16[2,8,4096]{2,1,0:T(8,128)(2,1)S(1)}, u32[]{:S(2)}, u32[]{:S(2)}) collective-permute-start(bf16[2,8,4096]{2,1,0:T(8,128)(2,1)S(1)} %get-tuple-element.85), channel_id=1, source_target_pairs={{0,46},{2,32},{4,34},{6,36},{8,38},{10,40},{12,42},{14,44},{16,62}... | collective-permute-start | bytes 393224 | tf_op jit(solution)/shard_map/ppermute | solution.py:39
  62.8 5.1 %shard_map.53 = (bf16[2,16,256,512]{3,2,1,0:T(8,128)(2,1)}, f32[8,512]{1,0:T(8,128)}) custom-call(bf16[512,2,4096]{2,1,0:T(2,128)(2,1)} %x_ref.4, bf16[2,16,256,256]{3,2,1,0:T(8,128)(2,1)} %refs_5_.1, bf16[2,16,256,512]{3,2,1,0:T(8,128)(2,1)} %get-tuple-element.87.refs_0_), custom_call_target="tpu_custom_call", output_to_operand_aliasing={{0}: (2, {})} | custom-call | flops 268435456 | bytes 7864320 | tf_op jit(solution)/shard_map/pallas_call | solution.py:207
  68.0 1.3 %collective-permute-start.12 = (bf16[4,2,8,4096]{3,2,1,0:T(8,128)(2,1)S(1)}, bf16[4,2,8,4096]{3,2,1,0:T(8,128)(2,1)S(1)}, u32[]{:S(2)}, u32[]{:S(2)}) collective-permute-start(bf16[4,2,8,4096]{3,2,1,0:T(8,128)(2,1)S(1)} %bitcast_dynamic-update-slice_fusion.refs_0_), channel_id=1, source_target_pairs={{0,48},{16,0},{32,16},{48,32},{1,49},{17,1},{33,17},{49,33},{2,50}... | collective-permute-start | bytes 1572872 | tf_op jit(solution)/shard_map/ppermute | solution.py:39
  69.7 2.6 %collective-permute-start.14 = (bf16[2,2,8,4096]{3,2,1,0:T(8,128)(2,1)S(1)}, bf16[2,2,8,4096]{3,2,1,0:T(8,128)(2,1)S(1)}, u32[]{:S(2)}, u32[]{:S(2)}) collective-permute-start(bf16[2,2,8,4096]{3,2,1,0:T(8,128)(2,1)S(1)} %slice.21), channel_id=1, source_target_pairs={{0,14},{2,0},{4,2},{6,4},{8,6},{10,8},{12,10},{14,12},{1,15},{3,1}... | collective-permute-start | bytes 786440 | tf_op jit(solution)/shard_map/ppermute | solution.py:39
  73.1 5.9 %collective-permute-start.16 = (f32[512]{0:T(512)S(1)}, f32[512]{0:T(512)S(1)}, u32[]{:S(2)}, u32[]{:S(2)}) collective-permute-start(f32[512]{0:T(512)S(1)} %add_reduce_fusion), channel_id=1, source_target_pairs={{0,64},{64,0},{1,65},{65,1},{2,66},{66,2},{3,67},{67,3},{4,68},{68... | collective-permute-start | bytes 6152 | tf_op jit(solution)/shard_map/ppermute | solution.py:43
  78.9 3.4 %copy-done = bf16[2,16,256,512]{3,2,1,0:T(8,128)(2,1)S(1)} copy-done((bf16[2,16,256,512]{3,2,1,0:T(8,128)(2,1)S(1)}, bf16[2,16,256,512]{3,2,1,0:T(8,128)(2,1)}, u32[]{:S(2)}) %copy-start) | copy-done | bytes 8388632
  82.9 2.8 %shard_map.55 = (f32[2,2,4,4,512]{4,3,2,1,0:T(4,128)S(1)}, f32[2,2,4,4,512]{4,3,2,1,0:T(4,128)S(1)}) custom-call(bf16[4,2,8,4096]{3,2,1,0:T(8,128)(2,1)S(1)} %bitcast_dynamic-update-slice_fusion.refs_0_, bf16[4,2,8,4096]{3,2,1,0:T(8,128)(2,1)S(1)} %collective-permute-done.12.refs_1_, bf16[2,2,8,4096]{3,2,1,0:T(8,128)(2,1)S(1)} %collective-permute-done.13.refs_2_, ...), custom_call_target="tpu_custom_call" | custom-call | flops 1610612736 | bytes 14680064 | tf_op jit(solution)/shard_map/pallas_call | solution.py:300
  85.7 2.0 %collective-permute-start.17 = (f32[2,2,4,4,512]{4,3,2,1,0:T(4,128)S(1)}, f32[2,2,4,4,512]{4,3,2,1,0:T(4,128)S(1)}, u32[]{:S(2)}, u32[]{:S(2)}) collective-permute-start(f32[2,2,4,4,512]{4,3,2,1,0:T(4,128)S(1)} %get-tuple-element.109), channel_id=1, source_target_pairs={{0,64},{64,0},{1,65},{65,1},{2,66},{66,2},{3,67},{67,3},{4,68},{68... | collective-permute-start | bytes 393224 | tf_op jit(solution)/shard_map/ppermute | solution.py:43
  90.1 1.7 %collective-permute-done.18 = f32[2,4,4,512]{3,2,1,0:T(4,128)S(1)} collective-permute-done((f32[2,4,4,512]{3,2,1,0:T(4,128)S(1)}, f32[2,4,4,512]{3,2,1,0:T(4,128)S(1)}, u32[]{:S(2)}, u32[]{:S(2)}) %collective-permute-start.18) | collective-permute-done | bytes 65568 | tf_op jit(solution)/shard_map/ppermute | solution.py:43
  (63 shorter events, 8.5 us)
Async XLA Ops:
  0.7 14.1 %copy-start.8 = (s32[2]{0:T(128)S(1)}, s32[2]{0:T(128)}, u32[]{:S(2)}) copy-start(s32[2]{0:T(128)} %param.6) | copy-start | bytes 28
  2.5 20.0 %collective-permute-start = (bf16[32,2,4096]{2,1,0:T(2,128)(2,1)S(1)}, bf16[32,2,4096]{2,1,0:T(2,128)(2,1)S(1)}, u32[]{:S(2)}, u32[]{:S(2)}) collective-permute-start(bf16[32,2,4096]{2,1,0:T(2,128)(2,1)S(1)} %get-tuple-element.58), channel_id=1, source_target_pairs={{0,16},{16,32},{32,48},{48,0},{1,17},{17,33},{33,49},{49,1},{2,18}... | collective-permute-start | bytes 1572872 | tf_op jit(solution)/shard_map/ppermute | solution.py:39
  4.6 17.9 %collective-permute-start.1 = (bf16[32,2,4096]{2,1,0:T(2,128)(2,1)S(1)}, bf16[32,2,4096]{2,1,0:T(2,128)(2,1)S(1)}, u32[]{:S(2)}, u32[]{:S(2)}) collective-permute-start(bf16[32,2,4096]{2,1,0:T(2,128)(2,1)S(1)} %get-tuple-element.59), channel_id=1, source_target_pairs={{0,48},{16,0},{32,16},{48,32},{1,49},{17,1},{33,17},{49,33},{2,50}... | collective-permute-start | bytes 1572872 | tf_op jit(solution)/shard_map/ppermute | solution.py:39
  8.9 13.6 %copy-start.3 = (bf16[32,2,4096]{2,1,0:T(2,128)(2,1)S(1)}, bf16[32,2,4096]{2,1,0:T(2,128)(2,1)}, u32[]{:S(2)}) copy-start(bf16[32,2,4096]{2,1,0:T(2,128)(2,1)} %get-tuple-element.63) | copy-start | bytes 1572868
  8.9 13.5 %collective-permute-start.2 = (bf16[16,2,4096]{2,1,0:T(2,128)(2,1)}, bf16[16,2,4096]{2,1,0:T(2,128)(2,1)S(1)}, u32[]{:S(2)}, u32[]{:S(2)}) collective-permute-start(bf16[16,2,4096]{2,1,0:T(2,128)(2,1)} %get-tuple-element.61), channel_id=1, source_target_pairs={{0,2},{2,4},{4,6},{6,8},{8,10},{10,12},{12,14},{14,0},{1,3},{3,5},... | collective-permute-start | bytes 786440 | tf_op jit(solution)/shard_map/ppermute | solution.py:39
  10.7 11.7 %collective-permute-start.3 = (bf16[16,2,4096]{2,1,0:T(2,128)(2,1)}, bf16[16,2,4096]{2,1,0:T(2,128)(2,1)S(1)}, u32[]{:S(2)}, u32[]{:S(2)}) collective-permute-start(bf16[16,2,4096]{2,1,0:T(2,128)(2,1)} %get-tuple-element.62), channel_id=1, source_target_pairs={{0,14},{2,0},{4,2},{6,4},{8,6},{10,8},{12,10},{14,12},{1,15},{3,1}... | collective-permute-start | bytes 786440 | tf_op jit(solution)/shard_map/ppermute | solution.py:39
  23.4 12.6 %collective-permute-start.4 = (bf16[2,4,2,4096]{3,2,1,0:T(2,128)(2,1)S(1)}, bf16[2,4,2,4096]{3,2,1,0:T(2,128)(2,1)S(1)}, u32[]{:S(2)}, u32[]{:S(2)}) collective-permute-start(bf16[2,4,2,4096]{3,2,1,0:T(2,128)(2,1)S(1)} %get-tuple-element.123), channel_id=1, source_target_pairs={{0,34},{2,36},{4,38},{6,40},{8,42},{10,44},{12,46},{14,32},{16,50}... | collective-permute-start | bytes 393224 | tf_op jit(solution)/shard_map/ppermute | solution.py:39
  23.5 12.5 %collective-permute-start.5 = (bf16[2,4,2,4096]{3,2,1,0:T(2,128)(2,1)S(1)}, bf16[2,4,2,4096]{3,2,1,0:T(2,128)(2,1)S(1)}, u32[]{:S(2)}, u32[]{:S(2)}) collective-permute-start(bf16[2,4,2,4096]{3,2,1,0:T(2,128)(2,1)S(1)} %get-tuple-element.122), channel_id=1, source_target_pairs={{0,4},{2,6},{4,8},{6,10},{8,12},{10,14},{12,0},{14,2},{1,5},{3,7},... | collective-permute-start | bytes 393224 | tf_op jit(solution)/shard_map/ppermute | solution.py:39
  26.5 9.5 %collective-permute-start.6 = (bf16[2,4,2,4096]{3,2,1,0:T(2,128)(2,1)S(1)}, bf16[2,4,2,4096]{3,2,1,0:T(2,128)(2,1)S(1)}, u32[]{:S(2)}, u32[]{:S(2)}) collective-permute-start(bf16[2,4,2,4096]{3,2,1,0:T(2,128)(2,1)S(1)} %get-tuple-element.121), channel_id=1, source_target_pairs={{0,46},{2,32},{4,34},{6,36},{8,38},{10,40},{12,42},{14,44},{16,62}... | collective-permute-start | bytes 393224 | tf_op jit(solution)/shard_map/ppermute | solution.py:39
  36.6 11.4 %collective-permute-start.7 = (bf16[2,4,2,4096]{3,2,1,0:T(2,128)(2,1)S(1)}, bf16[2,4,2,4096]{3,2,1,0:T(2,128)(2,1)S(1)}, u32[]{:S(2)}, u32[]{:S(2)}) collective-permute-start(bf16[2,4,2,4096]{3,2,1,0:T(2,128)(2,1)S(1)} %broadcast_select_fusion.10), channel_id=1, source_target_pairs={{0,8},{2,10},{4,12},{6,14},{8,0},{10,2},{12,4},{14,6},{1,9},{3,11}... | collective-permute-start | bytes 393224 | tf_op jit(solution)/shard_map/ppermute | solution.py:39
  48.3 7.9 %collective-permute-start.8 = (bf16[2,4,2,4096]{3,2,1,0:T(2,128)(2,1)S(1)}, bf16[2,4,2,4096]{3,2,1,0:T(2,128)(2,1)S(1)}, u32[]{:S(2)}, u32[]{:S(2)}) collective-permute-start(bf16[2,4,2,4096]{3,2,1,0:T(2,128)(2,1)S(1)} %broadcast_select_fusion.11.rows_ref), channel_id=1, source_target_pairs={{0,1},{1,0},{2,3},{3,2},{4,5},{5,4},{6,7},{7,6},{8,9},{9,8},{10,11... | collective-permute-start | bytes 393224 | tf_op jit(solution)/shard_map/ppermute | solution.py:39
  57.1 10.8 %collective-permute-start.9 = (bf16[2,8,4096]{2,1,0:T(8,128)(2,1)S(1)}, bf16[2,8,4096]{2,1,0:T(8,128)(2,1)S(1)}, u32[]{:S(2)}, u32[]{:S(2)}) collective-permute-start(bf16[2,8,4096]{2,1,0:T(8,128)(2,1)S(1)} %get-tuple-element.85), channel_id=1, source_target_pairs={{0,34},{2,36},{4,38},{6,40},{8,42},{10,44},{12,46},{14,32},{16,50}... | collective-permute-start | bytes 393224 | tf_op jit(solution)/shard_map/ppermute | solution.py:39
  59.0 8.9 %collective-permute-start.10 = (bf16[2,8,4096]{2,1,0:T(8,128)(2,1)S(1)}, bf16[2,8,4096]{2,1,0:T(8,128)(2,1)S(1)}, u32[]{:S(2)}, u32[]{:S(2)}) collective-permute-start(bf16[2,8,4096]{2,1,0:T(8,128)(2,1)S(1)} %get-tuple-element.85), channel_id=1, source_target_pairs={{0,4},{2,6},{4,8},{6,10},{8,12},{10,14},{12,0},{14,2},{1,5},{3,7},... | collective-permute-start | bytes 393224 | tf_op jit(solution)/shard_map/ppermute | solution.py:39
  59.0 8.9 %collective-permute-start.11 = (bf16[2,8,4096]{2,1,0:T(8,128)(2,1)S(1)}, bf16[2,8,4096]{2,1,0:T(8,128)(2,1)S(1)}, u32[]{:S(2)}, u32[]{:S(2)}) collective-permute-start(bf16[2,8,4096]{2,1,0:T(8,128)(2,1)S(1)} %get-tuple-element.85), channel_id=1, source_target_pairs={{0,46},{2,32},{4,34},{6,36},{8,38},{10,40},{12,42},{14,44},{16,62}... | collective-permute-start | bytes 393224 | tf_op jit(solution)/shard_map/ppermute | solution.py:39
  62.8 9.6 %copy-start.7 = (f32[8,512]{1,0:T(8,128)S(1)}, f32[8,512]{1,0:T(8,128)}, u32[]{:S(2)}) copy-start(f32[8,512]{1,0:T(8,128)} %get-tuple-element.95) | copy-start | bytes 49156
  62.8 16.2 %copy-start.1 = (bf16[2,16,256,256]{3,2,1,0:T(8,128)(2,1)S(1)}, bf16[2,16,256,256]{3,2,1,0:T(8,128)(2,1)}, u32[]{:S(2)}) copy-start(bf16[2,16,256,256]{3,2,1,0:T(8,128)(2,1)} %refs_5_.1) | copy-start | bytes 12582916
  68.0 14.9 %collective-permute-start.12 = (bf16[4,2,8,4096]{3,2,1,0:T(8,128)(2,1)S(1)}, bf16[4,2,8,4096]{3,2,1,0:T(8,128)(2,1)S(1)}, u32[]{:S(2)}, u32[]{:S(2)}) collective-permute-start(bf16[4,2,8,4096]{3,2,1,0:T(8,128)(2,1)S(1)} %bitcast_dynamic-update-slice_fusion.refs_0_), channel_id=1, source_target_pairs={{0,48},{16,0},{32,16},{48,32},{1,49},{17,1},{33,17},{49,33},{2,50}... | collective-permute-start | bytes 1572872 | tf_op jit(solution)/shard_map/ppermute | solution.py:39
  69.3 13.7 %collective-permute-start.15 = (bf16[4,2,8,4096]{3,2,1,0:T(8,128)(2,1)S(1)}, bf16[4,2,8,4096]{3,2,1,0:T(8,128)(2,1)S(1)}, u32[]{:S(2)}, u32[]{:S(2)}) collective-permute-start(bf16[4,2,8,4096]{3,2,1,0:T(8,128)(2,1)S(1)} %bitcast_dynamic-update-slice_fusion.refs_0_), channel_id=1, source_target_pairs={{0,16},{16,32},{32,48},{48,0},{1,17},{17,33},{33,49},{49,1},{2,18}... | collective-permute-start | bytes 1572872 | tf_op jit(solution)/shard_map/ppermute | solution.py:39
  69.5 13.4 %collective-permute-start.13 = (bf16[2,2,8,4096]{3,2,1,0:T(8,128)(2,1)S(1)}, bf16[2,2,8,4096]{3,2,1,0:T(8,128)(2,1)S(1)}, u32[]{:S(2)}, u32[]{:S(2)}) collective-permute-start(bf16[2,2,8,4096]{3,2,1,0:T(8,128)(2,1)S(1)} %slice.21), channel_id=1, source_target_pairs={{0,2},{2,4},{4,6},{6,8},{8,10},{10,12},{12,14},{14,0},{1,3},{3,5},... | collective-permute-start | bytes 786440 | tf_op jit(solution)/shard_map/ppermute | solution.py:39
  69.7 13.2 %collective-permute-start.14 = (bf16[2,2,8,4096]{3,2,1,0:T(8,128)(2,1)S(1)}, bf16[2,2,8,4096]{3,2,1,0:T(8,128)(2,1)S(1)}, u32[]{:S(2)}, u32[]{:S(2)}) collective-permute-start(bf16[2,2,8,4096]{3,2,1,0:T(8,128)(2,1)S(1)} %slice.21), channel_id=1, source_target_pairs={{0,14},{2,0},{4,2},{6,4},{8,6},{10,8},{12,10},{14,12},{1,15},{3,1}... | collective-permute-start | bytes 786440 | tf_op jit(solution)/shard_map/ppermute | solution.py:39
  73.1 9.8 %collective-permute-start.16 = (f32[512]{0:T(512)S(1)}, f32[512]{0:T(512)S(1)}, u32[]{:S(2)}, u32[]{:S(2)}) collective-permute-start(f32[512]{0:T(512)S(1)} %add_reduce_fusion), channel_id=1, source_target_pairs={{0,64},{64,0},{1,65},{65,1},{2,66},{66,2},{3,67},{67,3},{4,68},{68... | collective-permute-start | bytes 6152 | tf_op jit(solution)/shard_map/ppermute | solution.py:43
  85.7 3.0 %collective-permute-start.17 = (f32[2,2,4,4,512]{4,3,2,1,0:T(4,128)S(1)}, f32[2,2,4,4,512]{4,3,2,1,0:T(4,128)S(1)}, u32[]{:S(2)}, u32[]{:S(2)}) collective-permute-start(f32[2,2,4,4,512]{4,3,2,1,0:T(4,128)S(1)} %get-tuple-element.109), channel_id=1, source_target_pairs={{0,64},{64,0},{1,65},{65,1},{2,66},{66,2},{3,67},{67,3},{4,68},{68... | collective-permute-start | bytes 393224 | tf_op jit(solution)/shard_map/ppermute | solution.py:43
  87.7 2.5 %collective-permute-start.19 = (f32[512]{0:T(512)S(1)}, f32[512]{0:T(512)S(1)}, u32[]{:S(2)}, u32[]{:S(2)}) collective-permute-start(f32[512]{0:T(512)S(1)} %add.197), channel_id=1, source_target_pairs={{0,128},{128,0},{1,129},{129,1},{2,130},{130,2},{3,131},{131,3},{4... | collective-permute-start | bytes 6152 | tf_op jit(solution)/shard_map/ppermute | solution.py:43
  88.7 3.2 %collective-permute-start.18 = (f32[2,4,4,512]{3,2,1,0:T(4,128)S(1)}, f32[2,4,4,512]{3,2,1,0:T(4,128)S(1)}, u32[]{:S(2)}, u32[]{:S(2)}) collective-permute-start(f32[2,4,4,512]{3,2,1,0:T(4,128)S(1)} %fusion), channel_id=1, source_target_pairs={{0,128},{128,0},{1,129},{129,1},{2,130},{130,2},{3,131},{131,3},{4... | collective-permute-start | bytes 196616 | tf_op jit(solution)/shard_map/ppermute | solution.py:43
  (5 other events, 32.7 us)
